TPU v7x, 32 devices: a whole 2x2x4 slice. The times are simulated.
32 devices in a mesh: dp: 8 (over z, y), mp: 4 (over x, core).
Axes of the slice: x: 2, y: 2, z: 4, core: 2. Of those that a mesh axis runs over, the one named last changes fastest.
Arguments:
- layer_input: bfloat16 [4096, 2048], P(('dp', 'mp')), may hold values from -6 to 6
- output_grad: bfloat16 [4096, 2048], P(('dp', 'mp')), may hold values from -6 to 6
- attention_gain: bfloat16 [2048], P('dp'), may hold values from 0.25 to 1.75
- query_weight: bfloat16 [2048, 2048], P('dp', 'mp'), may hold values from -0.125 to 0.125
- key_weight: bfloat16 [2048, 256], P('dp'), may hold values from -0.125 to 0.125
- value_weight: bfloat16 [2048, 256], P('dp'), may hold values from -0.125 to 0.125
- output_weight: bfloat16 [2048, 2048], P('mp', 'dp'), may hold values from -0.5 to 0.5
- query_shrink: bfloat16 [2048, 256], P('dp'), may hold values from -0.125 to 0.125
- query_expand: bfloat16 [256, 2048], P('dp', 'mp'), may hold values from -0.375 to 0.375
- key_shrink: bfloat16 [2048, 256], P('dp'), may hold values from -0.125 to 0.125
- key_expand: bfloat16 [256, 256], P('dp'), may hold values from -0.375 to 0.375
- value_shrink: bfloat16 [2048, 256], P('dp'), may hold values from -0.125 to 0.125
- value_expand: bfloat16 [256, 256], P('dp'), may hold values from -0.375 to 0.375
- output_shrink: bfloat16 [2048, 256], P(('mp', 'dp')), may hold values from -0.5 to 0.5
- output_expand: bfloat16 [256, 2048], P('dp'), may hold values from -0.375 to 0.375
- feedforward_gain: bfloat16 [2048], P('dp'), may hold values from 0.25 to 1.75
- gate_weight: bfloat16 [2048, 16384], P('dp', 'mp'), may hold values from -0.125 to 0.125
- up_weight: bfloat16 [2048, 16384], P('dp', 'mp'), may hold values from -0.125 to 0.125
- down_weight: bfloat16 [16384, 2048], P('mp', 'dp'), may hold values from -0.046875 to 0.046875
- gate_shrink: bfloat16 [2048, 256], P('dp'), may hold values from -0.125 to 0.125
- gate_expand: bfloat16 [256, 16384], P('dp', 'mp'), may hold values from -0.375 to 0.375
- up_shrink: bfloat16 [2048, 256], P('dp'), may hold values from -0.125 to 0.125
- up_expand: bfloat16 [256, 16384], P('dp', 'mp'), may hold values from -0.375 to 0.375
- down_shrink: bfloat16 [16384, 256], P(('mp', 'dp')), may hold values from -0.046875 to 0.046875
- down_expand: bfloat16 [256, 2048], P('dp'), may hold values from -0.375 to 0.375
- group_ids: int32 [4096], P('dp'), may hold values from 0 to 15, as said below
- positions: int32 [4096], P('dp'), may hold values from 0 to 191, as said below
- segments: int32 [4096], P('dp'), may hold values from 0 to 2, as said below
Outputs:
- layer_output: bfloat16 [4096, 2048], P(('dp', 'mp'))
- input_grad: float32 [4096, 2048], P(('dp', 'mp'))
- attention_gain_grad: float32 [2048], P(('dp', 'mp'))
- query_weight_grad: float32 [2048, 2048], P('dp', 'mp')
- key_weight_grad: float32 [2048, 256], P(('dp', 'mp'))
- value_weight_grad: float32 [2048, 256], P(('dp', 'mp'))
- output_weight_grad: float32 [2048, 2048], P('mp', 'dp')
- query_shrink_grad: float32 [2048, 256], P(('dp', 'mp'))
- query_expand_grad: float32 [256, 2048], P('dp', 'mp')
- key_shrink_grad: float32 [2048, 256], P(('dp', 'mp'))
- key_expand_grad: float32 [256, 256], P(('dp', 'mp'))
- value_shrink_grad: float32 [2048, 256], P(('dp', 'mp'))
- value_expand_grad: float32 [256, 256], P(('dp', 'mp'))
- output_shrink_grad: float32 [2048, 256], P(('mp', 'dp'))
- output_expand_grad: float32 [256, 2048], P('dp')
- feedforward_gain_grad: float32 [2048], P(('dp', 'mp'))
- gate_weight_grad: float32 [2048, 16384], P('dp', 'mp')
- up_weight_grad: float32 [2048, 16384], P('dp', 'mp')
- down_weight_grad: float32 [16384, 2048], P('mp', 'dp')
- gate_shrink_grad: float32 [2048, 256], P(('dp', 'mp'))
- gate_expand_grad: float32 [256, 16384], P('dp', 'mp')
- up_shrink_grad: float32 [2048, 256], P(('dp', 'mp'))
- up_expand_grad: float32 [256, 16384], P('dp', 'mp')
- down_shrink_grad: float32 [16384, 256], P(('mp', 'dp'))
- down_expand_grad: float32 [256, 2048], P('dp')
Inputs may be any that keep to these rules, and one draw needn't show every extreme that they name: `group_ids`: the rows of each index of dp hold 2 whole groups, with ids that index times 2 up to 2 more, the groups' tokens mixed in an order drawn from the seed; a group has 128 prompt tokens and 2 continuations of 64 tokens. A group's prompt tokens have positions 0 to 127 once each; each continuation's tokens have 128 to 191 once each. `segments`: 0 on prompt tokens; the continuations of a group are numbered 1 to 2.
All inputs are finite; a program needn't handle non-finite values.
Results may differ from a plain program's by a relative error of at most 0.024.
Values may be sent and summed in bfloat16 or wider, within the bound.
A program may use at most 320 MiB of HBM per device.

v0:
```python
import jax
import jax.numpy as jnp
from jax import lax
from jax.sharding import PartitionSpec as P

EPS = 1e-06


def matmul(left, right):
    return jnp.dot(left, right, preferred_element_type=jnp.float32)


def against(left, right):
    return lax.dot_general(
        left, right, (((1,), (1,)), ((), ())), preferred_element_type=jnp.float32
    )


def outer_sum(left, right):
    return lax.dot_general(
        left, right, (((0,), (0,)), ((), ())), preferred_element_type=jnp.float32
    )


def against_exact(left, right):
    return lax.dot_general(
        left,
        right,
        (((1,), (1,)), ((), ())),
        precision=lax.Precision.HIGHEST,
        preferred_element_type=jnp.float32,
    )


def outer_exact(left, right):
    return lax.dot_general(
        left,
        right,
        (((0,), (0,)), ((), ())),
        precision=lax.Precision.HIGHEST,
        preferred_element_type=jnp.float32,
    )


def norm_rows(rows, gain):
    return rows * lax.rsqrt(jnp.mean(rows * rows, axis=-1, keepdims=True) + EPS) * gain


def rotary(entries, places, sign):
    half = entries.shape[-1] // 2
    freq = 10000.0 ** (-jnp.arange(half).astype(jnp.float32) * 2.0 / entries.shape[-1])
    angle = places.astype(jnp.float32)[:, None] * freq[None, :]
    cosine = jnp.cos(angle)[:, None, :]
    sine = sign * jnp.sin(angle)[:, None, :]
    first = entries[..., :half]
    second = entries[..., half:]
    return jnp.concatenate(
        [first * cosine - second * sine, second * cosine + first * sine], axis=-1
    )


def body(
    layer_input,
    output_grad,
    attention_gain,
    query_weight,
    key_weight,
    value_weight,
    output_weight,
    query_shrink,
    query_expand,
    key_shrink,
    key_expand,
    value_shrink,
    value_expand,
    output_shrink,
    output_expand,
    feedforward_gain,
    gate_weight,
    up_weight,
    down_weight,
    gate_shrink,
    gate_expand,
    up_shrink,
    up_expand,
    down_shrink,
    down_expand,
    group_ids,
    positions,
    segments,
):
    rows_local = layer_input.shape[0]
    own_start = lax.axis_index("mp") * rows_local
    allowed = (
        (group_ids[:, None] == group_ids[None, :])
        & (positions[None, :] <= positions[:, None])
        & ((segments[None, :] == 0) | (segments[None, :] == segments[:, None]))
    )

    def gather_attention():
        return (
            lax.all_gather(attention_gain, "dp", axis=0, tiled=True),
            lax.all_gather(query_weight, "dp", axis=0, tiled=True),
            lax.all_gather(key_weight, "dp", axis=0, tiled=True),
            lax.all_gather(value_weight, "dp", axis=0, tiled=True),
            lax.all_gather(output_weight, "dp", axis=1, tiled=True),
            lax.all_gather(query_shrink, "dp", axis=0, tiled=True),
            lax.all_gather(query_expand, "dp", axis=0, tiled=True),
            lax.all_gather(key_shrink, "dp", axis=0, tiled=True),
            lax.all_gather(key_expand, "dp", axis=0, tiled=True),
            lax.all_gather(value_shrink, "dp", axis=0, tiled=True),
            lax.all_gather(value_expand, "dp", axis=0, tiled=True),
            lax.all_gather(output_shrink, "dp", axis=0, tiled=True),
            lax.all_gather(output_expand, "dp", axis=0, tiled=True),
        )

    def gather_feed():
        return (
            lax.all_gather(feedforward_gain, "dp", axis=0, tiled=True),
            lax.all_gather(gate_weight, "dp", axis=0, tiled=True),
            lax.all_gather(up_weight, "dp", axis=0, tiled=True),
            lax.all_gather(down_weight, "dp", axis=1, tiled=True),
            lax.all_gather(gate_shrink, "dp", axis=0, tiled=True),
            lax.all_gather(gate_expand, "dp", axis=0, tiled=True),
            lax.all_gather(up_shrink, "dp", axis=0, tiled=True),
            lax.all_gather(up_expand, "dp", axis=0, tiled=True),
            lax.all_gather(down_shrink, "dp", axis=0, tiled=True),
            lax.all_gather(down_expand, "dp", axis=0, tiled=True),
        )

    def gather_rows(rows):
        return lax.all_gather(rows, "mp", axis=0, tiled=True)

    def gather_grads(rows):
        return lax.all_gather(rows, "mp", axis=0, tiled=True)

    def scatter_grads(term):
        return lax.psum_scatter(
            term(jnp.int32(0), lax.axis_size("mp") * rows_local),
            "mp",
            scatter_dimension=0,
            tiled=True,
        )

    def project_out(mixed, weight, shrink, expand):
        reduced = lax.psum(matmul(mixed, shrink), "mp").astype(jnp.bfloat16)

        def term(start, count):
            return matmul(mixed, weight)

        branch = lax.psum_scatter(
            term(jnp.int32(0), lax.axis_size("mp") * rows_local),
            "mp",
            scatter_dimension=0,
            tiled=True,
        )
        own = lax.dynamic_slice_in_dim(reduced, own_start, rows_local, 0)
        return (branch + matmul(own, expand), reduced)

    def masked_scores(queries, keys_rot):
        scores = jnp.einsum("thd,sd->hts", queries, keys_rot, preferred_element_type=jnp.float32)
        return jnp.where(allowed[None], scores, -1e30)

    def attention_forward(rows_in, params):
        (
            gain_one,
            w_query,
            w_key,
            w_value,
            w_output,
            query_a,
            query_b,
            key_a,
            key_b,
            value_a,
            value_b,
            output_a,
            output_b,
        ) = params
        normed = gather_rows(norm_rows(rows_in, gain_one.astype(jnp.float32)).astype(jnp.bfloat16))
        tokens = normed.shape[0]
        head_size = w_key.shape[1]
        heads = w_query.shape[1] // head_size
        query_low = matmul(normed, query_a).astype(jnp.bfloat16)
        key_low = matmul(normed, key_a).astype(jnp.bfloat16)
        value_low = matmul(normed, value_a).astype(jnp.bfloat16)
        query_lin = matmul(normed, w_query) + matmul(query_low, query_b)
        key_lin = matmul(normed, w_key) + matmul(key_low, key_b)
        value_lin = matmul(normed, w_value) + matmul(value_low, value_b)
        queries = (
            rotary(query_lin.reshape(tokens, heads, head_size), positions, 1.0)
            * head_size ** (-0.5)
        ).astype(jnp.bfloat16)
        keys_rot = rotary(key_lin[:, None, :], positions, 1.0)[:, 0, :].astype(jnp.bfloat16)
        values = value_lin.astype(jnp.bfloat16)
        scores = masked_scores(queries, keys_rot)
        highest = jnp.max(scores, axis=-1, keepdims=True)
        expo = jnp.exp(scores - highest)
        totals = jnp.sum(expo, axis=-1, keepdims=True)
        probability = expo / totals
        logsum = highest + jnp.log(totals)
        mixed = jnp.einsum(
            "hts,sd->thd",
            probability.astype(jnp.bfloat16),
            values,
            preferred_element_type=jnp.float32,
        )
        mixed = mixed.reshape(tokens, heads * head_size).astype(jnp.bfloat16)
        branch, reduced = project_out(mixed, w_output, output_a, output_b)
        saved = (
            normed,
            query_low,
            key_low,
            value_low,
            queries,
            keys_rot,
            values,
            logsum,
            mixed,
            reduced,
        )
        return (rows_in + branch, saved)

    def feed_forward(middle, params):
        gain_two, w_gate, w_up, w_down, gate_a, gate_b, up_a, up_b, down_a, down_b = params
        normed = gather_rows(norm_rows(middle, gain_two.astype(jnp.float32)).astype(jnp.bfloat16))
        gate_low = matmul(normed, gate_a).astype(jnp.bfloat16)
        up_low = matmul(normed, up_a).astype(jnp.bfloat16)
        gate_pre = matmul(normed, w_gate) + matmul(gate_low, gate_b)
        up_pre = matmul(normed, w_up) + matmul(up_low, up_b)
        hidden = (jax.nn.gelu(gate_pre, approximate=True) * up_pre).astype(jnp.bfloat16)
        branch, reduced = project_out(hidden, w_down, down_a, down_b)
        return (middle + branch, (normed, gate_low, up_low, gate_pre, up_pre, hidden, reduced))

    rows_in = layer_input.astype(jnp.float32)
    attention_params = gather_attention()
    middle, attention_saved = attention_forward(rows_in, attention_params)
    feed_params = gather_feed()
    result, feed_saved = feed_forward(middle, feed_params)
    feed_params = gather_feed()
    feed_saved = feed_forward(middle, feed_params)[1]
    gain_two, w_gate, w_up, w_down, gate_a, gate_b, up_a, up_b, down_a, down_b = feed_params
    normed_feed, gate_low, up_low, gate_pre, up_pre, hidden, reduced_feed = feed_saved
    grad_branch_feed = gather_grads(output_grad)
    down_weight_grad = outer_sum(hidden, grad_branch_feed)
    down_expand_grad = outer_sum(reduced_feed, grad_branch_feed)
    grad_reduced_feed = against(grad_branch_feed, down_b).astype(jnp.bfloat16)
    down_shrink_grad = outer_sum(hidden, grad_reduced_feed)
    grad_hidden = against(grad_branch_feed, w_down) + against(grad_reduced_feed, down_a)
    unused, gelu_pull = jax.vjp(
        lambda gated, upper: jax.nn.gelu(gated, approximate=True) * upper, gate_pre, up_pre
    )
    grad_gate, grad_up = gelu_pull(grad_hidden)
    grad_gate = grad_gate.astype(jnp.bfloat16)
    grad_up = grad_up.astype(jnp.bfloat16)
    gate_expand_grad = outer_sum(gate_low, grad_gate)
    up_expand_grad = outer_sum(up_low, grad_up)
    grad_gate_low = against(grad_gate, gate_b)
    grad_up_low = against(grad_up, up_b)
    feed_wide = normed_feed.astype(jnp.float32)
    gate_shrink_grad = outer_exact(feed_wide, grad_gate_low)
    up_shrink_grad = outer_exact(feed_wide, grad_up_low)
    gate_a_wide = gate_a.astype(jnp.float32)
    up_a_wide = up_a.astype(jnp.float32)

    def feed_term(start, count):

        def pick(rows):
            return rows

        total = against(pick(grad_gate), w_gate) + against(pick(grad_up), w_up)
        return (
            total
            + against_exact(pick(grad_gate_low), gate_a_wide)
            + against_exact(pick(grad_up_low), up_a_wide)
        )

    grad_normed_feed = scatter_grads(feed_term)
    unused, norm_pull = jax.vjp(norm_rows, middle, gain_two.astype(jnp.float32))
    grad_middle_part, feed_gain_grad = norm_pull(grad_normed_feed)
    grad_middle = output_grad.astype(jnp.float32) + grad_middle_part
    gate_weight_grad = outer_sum(normed_feed, grad_gate)
    up_weight_grad = outer_sum(normed_feed, grad_up)
    feed_split = (
        lax.psum_scatter(
            gate_weight_grad.astype(jnp.bfloat16), "dp", scatter_dimension=0, tiled=True
        ).astype(jnp.float32),
        lax.psum_scatter(
            up_weight_grad.astype(jnp.bfloat16), "dp", scatter_dimension=0, tiled=True
        ).astype(jnp.float32),
        lax.psum_scatter(
            down_weight_grad.astype(jnp.bfloat16), "dp", scatter_dimension=1, tiled=True
        ).astype(jnp.float32),
        lax.psum_scatter(
            gate_expand_grad.astype(jnp.bfloat16), "dp", scatter_dimension=0, tiled=True
        ).astype(jnp.float32),
        lax.psum_scatter(
            up_expand_grad.astype(jnp.bfloat16), "dp", scatter_dimension=0, tiled=True
        ).astype(jnp.float32),
        lax.psum_scatter(
            down_shrink_grad.astype(jnp.bfloat16), "dp", scatter_dimension=0, tiled=True
        ).astype(jnp.float32),
        lax.psum_scatter(
            down_expand_grad.astype(jnp.bfloat16), "dp", scatter_dimension=0, tiled=True
        ).astype(jnp.float32),
    )
    gate_weight_own, up_weight_own = (feed_split[0], feed_split[1])
    down_weight_own, gate_expand_own, up_expand_own, down_shrink_own, down_expand_own = (
        feed_split[2],
        feed_split[3],
        feed_split[4],
        feed_split[5],
        feed_split[6],
    )
    feed_shared = (
        lax.psum_scatter(feed_gain_grad, ("dp", "mp"), scatter_dimension=0, tiled=True),
        lax.psum_scatter(gate_shrink_grad, ("dp", "mp"), scatter_dimension=0, tiled=True),
        lax.psum_scatter(up_shrink_grad, ("dp", "mp"), scatter_dimension=0, tiled=True),
    )
    attention_params = gather_attention()
    attention_saved = attention_forward(rows_in, attention_params)[1]
    (
        gain_one,
        w_query,
        w_key,
        w_value,
        w_output,
        query_a,
        query_b,
        key_a,
        key_b,
        value_a,
        value_b,
        output_a,
        output_b,
    ) = attention_params
    normed, query_low, key_low, value_low, queries, keys_rot, values, logsum, mixed, reduced = (
        attention_saved
    )
    tokens = normed.shape[0]
    head_size = w_key.shape[1]
    heads = w_query.shape[1] // head_size
    grad_branch = gather_grads(grad_middle.astype(jnp.bfloat16))
    output_weight_grad = outer_sum(mixed, grad_branch)
    output_expand_grad = outer_sum(reduced, grad_branch)
    grad_reduced = against(grad_branch, output_b).astype(jnp.bfloat16)
    output_shrink_grad = outer_sum(mixed, grad_reduced)
    grad_mixed = (against(grad_branch, w_output) + against(grad_reduced, output_a)).astype(
        jnp.bfloat16
    )
    grad_mixed = grad_mixed.reshape(tokens, heads, head_size)
    probability = jnp.exp(masked_scores(queries, keys_rot) - logsum)
    grad_values = jnp.einsum(
        "hts,thd->sd",
        probability.astype(jnp.bfloat16),
        grad_mixed,
        preferred_element_type=jnp.float32,
    )
    grad_probability = jnp.einsum(
        "thd,sd->hts", grad_mixed, values, preferred_element_type=jnp.float32
    )
    grad_scores = probability * (
        grad_probability - jnp.sum(probability * grad_probability, axis=-1, keepdims=True)
    )
    grad_scores = grad_scores.astype(jnp.bfloat16)
    grad_queries_rot = jnp.einsum(
        "hts,sd->thd", grad_scores, keys_rot, preferred_element_type=jnp.float32
    )
    grad_keys_rot = jnp.einsum(
        "hts,thd->sd", grad_scores, queries, preferred_element_type=jnp.float32
    )
    grad_query = (
        rotary(grad_queries_rot * head_size ** (-0.5), positions, -1.0)
        .reshape(tokens, heads * head_size)
        .astype(jnp.bfloat16)
    )
    grad_key = rotary(grad_keys_rot[:, None, :], positions, -1.0)[:, 0, :]
    normed_wide = normed.astype(jnp.float32)
    query_weight_grad = outer_sum(normed, grad_query)
    query_expand_grad = outer_sum(query_low, grad_query)
    grad_query_low = against(grad_query, query_b)
    query_shrink_grad = outer_exact(normed_wide, grad_query_low)
    key_weight_grad = outer_exact(normed_wide, grad_key)
    key_expand_grad = outer_exact(key_low.astype(jnp.float32), grad_key)
    grad_key_low = against_exact(grad_key, key_b.astype(jnp.float32))
    key_shrink_grad = outer_exact(normed_wide, grad_key_low)
    value_weight_grad = outer_exact(normed_wide, grad_values)
    value_expand_grad = outer_exact(value_low.astype(jnp.float32), grad_values)
    grad_value_low = against_exact(grad_values, value_b.astype(jnp.float32))
    value_shrink_grad = outer_exact(normed_wide, grad_value_low)
    query_a_wide = query_a.astype(jnp.float32)
    key_wide = w_key.astype(jnp.float32)
    key_a_wide = key_a.astype(jnp.float32)
    value_wide = w_value.astype(jnp.float32)
    value_a_wide = value_a.astype(jnp.float32)

    def attention_term(start, count):

        def pick(rows):
            return rows

        total = against(pick(grad_query), w_query) + against_exact(
            pick(grad_query_low), query_a_wide
        )
        total = (
            total
            + against_exact(pick(grad_key), key_wide)
            + against_exact(pick(grad_key_low), key_a_wide)
        )
        return (
            total
            + against_exact(pick(grad_values), value_wide)
            + against_exact(pick(grad_value_low), value_a_wide)
        )

    grad_normed = scatter_grads(attention_term)
    unused, norm_pull_one = jax.vjp(norm_rows, rows_in, gain_one.astype(jnp.float32))
    grad_input_part, attention_gain_grad = norm_pull_one(grad_normed)
    input_grad = grad_middle + grad_input_part
    attention_split = (
        lax.psum_scatter(
            query_weight_grad.astype(jnp.bfloat16), "dp", scatter_dimension=0, tiled=True
        ).astype(jnp.float32),
        lax.psum_scatter(
            output_weight_grad.astype(jnp.bfloat16), "dp", scatter_dimension=1, tiled=True
        ).astype(jnp.float32),
        lax.psum_scatter(
            query_expand_grad.astype(jnp.bfloat16), "dp", scatter_dimension=0, tiled=True
        ).astype(jnp.float32),
        lax.psum_scatter(
            output_shrink_grad.astype(jnp.bfloat16), "dp", scatter_dimension=0, tiled=True
        ).astype(jnp.float32),
        lax.psum_scatter(
            output_expand_grad.astype(jnp.bfloat16), "dp", scatter_dimension=0, tiled=True
        ).astype(jnp.float32),
    )
    attention_shared = (
        lax.psum_scatter(attention_gain_grad, ("dp", "mp"), scatter_dimension=0, tiled=True),
        lax.psum_scatter(key_weight_grad, ("dp", "mp"), scatter_dimension=0, tiled=True),
        lax.psum_scatter(value_weight_grad, ("dp", "mp"), scatter_dimension=0, tiled=True),
        lax.psum_scatter(query_shrink_grad, ("dp", "mp"), scatter_dimension=0, tiled=True),
        lax.psum_scatter(key_shrink_grad, ("dp", "mp"), scatter_dimension=0, tiled=True),
        lax.psum_scatter(key_expand_grad, ("dp", "mp"), scatter_dimension=0, tiled=True),
        lax.psum_scatter(value_shrink_grad, ("dp", "mp"), scatter_dimension=0, tiled=True),
        lax.psum_scatter(value_expand_grad, ("dp", "mp"), scatter_dimension=0, tiled=True),
    )
    return (
        result.astype(jnp.bfloat16),
        input_grad,
        attention_shared[0],
        attention_split[0],
        attention_shared[1],
        attention_shared[2],
        attention_split[1],
        attention_shared[3],
        attention_split[2],
        attention_shared[4],
        attention_shared[5],
        attention_shared[6],
        attention_shared[7],
        attention_split[3],
        attention_split[4],
        feed_shared[0],
        gate_weight_own,
        up_weight_own,
        down_weight_own,
        feed_shared[1],
        gate_expand_own,
        feed_shared[2],
        up_expand_own,
        down_shrink_own,
        down_expand_own,
    )


def solution(mesh):
    placed = (
        P(("dp", "mp"), None),
        P(("dp", "mp"), None),
        P("dp"),
        P("dp", "mp"),
        P("dp", None),
        P("dp", None),
        P("mp", "dp"),
        P("dp", None),
        P("dp", "mp"),
        P("dp", None),
        P("dp", None),
        P("dp", None),
        P("dp", None),
        P(("mp", "dp"), None),
        P("dp", None),
        P("dp"),
        P("dp", "mp"),
        P("dp", "mp"),
        P("mp", "dp"),
        P("dp", None),
        P("dp", "mp"),
        P("dp", None),
        P("dp", "mp"),
        P(("mp", "dp"), None),
        P("dp", None),
        P("dp"),
        P("dp"),
        P("dp"),
    )
    return jax.shard_map(
        body,
        mesh=mesh,
        in_specs=placed,
        out_specs=(
            P(("dp", "mp"), None),
            P(("dp", "mp"), None),
            P(("dp", "mp")),
            P("dp", "mp"),
            P(("dp", "mp"), None),
            P(("dp", "mp"), None),
            P("mp", "dp"),
            P(("dp", "mp"), None),
            P("dp", "mp"),
            P(("dp", "mp"), None),
            P(("dp", "mp"), None),
            P(("dp", "mp"), None),
            P(("dp", "mp"), None),
            P(("mp", "dp"), None),
            P("dp", None),
            P(("dp", "mp")),
            P("dp", "mp"),
            P("dp", "mp"),
            P("mp", "dp"),
            P(("dp", "mp"), None),
            P("dp", "mp"),
            P(("dp", "mp"), None),
            P("dp", "mp"),
            P(("mp", "dp"), None),
            P("dp", None),
        ),
        check_vma=False,
    )
```

profile of v0, /device:TPU:0, one launch (start us, length us, event | category | flops | bytes accessed | tf_op | source)
XLA Modules:
  0.0 4381.5 jit_solution(14167552040372830595)
XLA Ops:
  163.2 38.7 all-gather.36.cloned.1.call-done
  245.5 47.6 %all-gather.34.cloned.1.call-done = bf16[2048,512]{1,0:T(8,128)(2,1)} async-done(((bf16[256,512]{1,0:T(8,128)(2,1)}), bf16[2048,512]{1,0:T(8,128)(2,1)}) %all-gather.34.cloned.1.call-update) | async-done | bytes 2097168 | tf_op jit(solution)/shard_map/all_gather | solution.py:103
  302.1 42.6 all-gather.38.cloned.1.call-done
  504.9 49.1 %all-gather.58.cloned.1.call-done = bf16[4096,256]{1,0:T(8,128)(2,1)} async-done(((bf16[512,256]{1,0:T(8,128)(2,1)}), bf16[4096,256]{1,0:T(8,128)(2,1)}) %all-gather.58.cloned.1.call-update) | async-done | bytes 2097168 | tf_op jit(solution)/shard_map/all_gather | solution.py:127
  621.0 39.7 all-gather.46.cloned.1.call-done
  663.3 47.6 %all-gather.48.cloned.1.call-done = bf16[256,4096]{1,0:T(8,128)(2,1)} async-done(((bf16[32,4096]{1,0:T(8,128)(2,1)}), bf16[256,4096]{1,0:T(8,128)(2,1)}) %all-gather.48.cloned.1.call-update) | async-done | bytes 2097168 | tf_op jit(solution)/shard_map/all_gather | solution.py:124
  717.3 43.7 all-gather.54.cloned.1.call-done
  767.1 222.3 %all-gather.56.cloned.1.call-done = bf16[4096,2048]{1,0:T(8,128)(2,1)} async-done(((bf16[4096,256]{1,0:T(8,128)(2,1)}), bf16[4096,2048]{1,0:T(8,128)(2,1)}) %all-gather.56.cloned.1.call-update) | async-done | bytes 16777232 | tf_op jit(solution)/shard_map/all_gather | solution.py:122
  1006.4 211.1 %all-gather.50.cloned.1.call-done = bf16[2048,4096]{1,0:T(8,128)(2,1)} async-done(((bf16[256,4096]{1,0:T(8,128)(2,1)}), bf16[2048,4096]{1,0:T(8,128)(2,1)}) %all-gather.50.cloned.1.call-update) | async-done | bytes 16777232 | tf_op jit(solution)/shard_map/all_gather | solution.py:121
  1233.1 212.6 %all-gather.44.cloned.1.call-done = bf16[2048,4096]{1,0:T(8,128)(2,1)} async-done(((bf16[256,4096]{1,0:T(8,128)(2,1)}), bf16[2048,4096]{1,0:T(8,128)(2,1)}) %all-gather.44.cloned.1.call-update) | async-done | bytes 16777232 | tf_op jit(solution)/shard_map/all_gather | solution.py:120
  1515.5 42.8 reduce-scatter.30.cloned.1.call-done
  1802.3 68.9 %reduce-scatter.72.cloned.1.call-done = bf16[512,256]{1,0:T(8,128)(2,1)} async-done(((bf16[4096,256]{1,0:T(8,128)(2,1)}), bf16[512,256]{1,0:T(8,128)(2,1)}) %reduce-scatter.72.cloned.1.call-update) | async-done | bytes 262160 | tf_op jit(solution)/shard_map/reduce_scatter | solution.py:300
  1873.0 45.0 %reduce-scatter.28.cloned.1.call-done = f32[128,2048]{1,0:T(8,128)} async-done(((f32[512,2048]{1,0:T(8,128)}), f32[128,2048]{1,0:T(8,128)}) %reduce-scatter.28.cloned.1.call-update) | async-done | bytes 1048592 | tf_op jit(solution)/shard_map/reduce_scatter | solution.py:151
  1920.3 62.8 %reduce-scatter.54.cloned.1.call-done = bf16[64,256]{1,0:T(8,128)(2,1)} async-done(((bf16[512,256]{1,0:T(8,128)(2,1)}), bf16[64,256]{1,0:T(8,128)(2,1)}) %reduce-scatter.54.cloned.1.call-update) | async-done | bytes 32784 | tf_op jit(solution)/shard_map/reduce_scatter | solution.py:430
  1984.5 62.6 %reduce-scatter.44.cloned.1.call-done = bf16[32,512]{1,0:T(8,128)(2,1)} async-done(((bf16[256,512]{1,0:T(8,128)(2,1)}), bf16[32,512]{1,0:T(8,128)(2,1)}) %reduce-scatter.44.cloned.1.call-update) | async-done | bytes 32784 | tf_op jit(solution)/shard_map/reduce_scatter | solution.py:427
  2048.6 64.6 %reduce-scatter.56.cloned.1.call-done = bf16[32,2048]{1,0:T(8,128)(2,1)} async-done(((bf16[256,2048]{1,0:T(8,128)(2,1)}), bf16[32,2048]{1,0:T(8,128)(2,1)}) %reduce-scatter.56.cloned.1.call-update) | async-done | bytes 131088 | tf_op jit(solution)/shard_map/reduce_scatter | solution.py:433
  2114.8 69.5 %reduce-scatter.40.cloned.1.call-done = bf16[512,256]{1,0:T(8,128)(2,1)} async-done(((bf16[512,2048]{1,0:T(8,128)(2,1)}), bf16[512,256]{1,0:T(8,128)(2,1)}) %reduce-scatter.40.cloned.1.call-update) | async-done | bytes 262160 | tf_op jit(solution)/shard_map/reduce_scatter | solution.py:424
  2186.0 68.9 %reduce-scatter.34.cloned.1.call-done = bf16[256,512]{1,0:T(8,128)(2,1)} async-done(((bf16[2048,512]{1,0:T(8,128)(2,1)}), bf16[256,512]{1,0:T(8,128)(2,1)}) %reduce-scatter.34.cloned.1.call-update) | async-done | bytes 262160 | tf_op jit(solution)/shard_map/reduce_scatter | solution.py:421
  2256.7 45.0 %reduce-scatter.32.cloned.1.call-done = f32[128,2048]{1,0:T(8,128)} async-done(((f32[512,2048]{1,0:T(8,128)}), f32[128,2048]{1,0:T(8,128)}) %reduce-scatter.32.cloned.1.call-update) | async-done | bytes 1048592 | tf_op jit(solution)/shard_map/reduce_scatter | solution.py:138
  2303.3 42.0 all-reduce.2
  2349.4 239.9 %reduce-scatter.62.cloned.1.call-done = bf16[4096,256]{1,0:T(8,128)(2,1)} async-done(((bf16[4096,2048]{1,0:T(8,128)(2,1)}), bf16[4096,256]{1,0:T(8,128)(2,1)}) %reduce-scatter.62.cloned.1.call-update) | async-done | bytes 2097168 | tf_op jit(solution)/shard_map/reduce_scatter | solution.py:291
  2593.2 282.0 %reduce-scatter.60.cloned.1.call-done = bf16[256,4096]{1,0:T(8,128)(2,1)} async-done(((bf16[2048,4096]{1,0:T(8,128)(2,1)}), bf16[256,4096]{1,0:T(8,128)(2,1)}) %reduce-scatter.60.cloned.1.call-update) | async-done | bytes 2097168 | tf_op jit(solution)/shard_map/reduce_scatter | solution.py:288
  2879.3 281.4 %reduce-scatter.58.cloned.1.call-done = bf16[256,4096]{1,0:T(8,128)(2,1)} async-done(((bf16[2048,4096]{1,0:T(8,128)(2,1)}), bf16[256,4096]{1,0:T(8,128)(2,1)}) %reduce-scatter.58.cloned.1.call-update) | async-done | bytes 2097168 | tf_op jit(solution)/shard_map/reduce_scatter | solution.py:285
  3164.8 134.3 %reduce-scatter.64.cloned.1.call-done = f32[64,256]{1,0:T(8,128)} async-done(((f32[2048,256]{1,0:T(8,128)}), f32[64,256]{1,0:T(8,128)}) %reduce-scatter.64.cloned.1.call-update) | async-done | bytes 65552 | tf_op jit(solution)/shard_map/reduce_scatter | solution.py:317
  3299.0 135.0 %reduce-scatter.68.cloned.1.call-done = f32[64,256]{1,0:T(8,128)} async-done(((f32[2048,256]{1,0:T(8,128)}), f32[64,256]{1,0:T(8,128)}) %reduce-scatter.68.cloned.1.call-update) | async-done | bytes 65552 | tf_op jit(solution)/shard_map/reduce_scatter | solution.py:318
  3434.0 132.7 %reduce-scatter.52.cloned.1.call-done = f32[8,256]{1,0:T(8,128)} async-done(((f32[256,256]{1,0:T(8,128)}), f32[8,256]{1,0:T(8,128)}) %reduce-scatter.52.cloned.1.call-update) | async-done | bytes 8208 | tf_op jit(solution)/shard_map/reduce_scatter | solution.py:445
  3566.7 132.6 %reduce-scatter.48.cloned.1.call-done = f32[8,256]{1,0:T(8,128)} async-done(((f32[256,256]{1,0:T(8,128)}), f32[8,256]{1,0:T(8,128)}) %reduce-scatter.48.cloned.1.call-update) | async-done | bytes 8208 | tf_op jit(solution)/shard_map/reduce_scatter | solution.py:443
  3699.2 135.2 %reduce-scatter.46.cloned.1.call-done = f32[64,256]{1,0:T(8,128)} async-done(((f32[2048,256]{1,0:T(8,128)}), f32[64,256]{1,0:T(8,128)}) %reduce-scatter.46.cloned.1.call-update) | async-done | bytes 65552 | tf_op jit(solution)/shard_map/reduce_scatter | solution.py:442
  3834.4 135.0 %reduce-scatter.42.cloned.1.call-done = f32[64,256]{1,0:T(8,128)} async-done(((f32[2048,256]{1,0:T(8,128)}), f32[64,256]{1,0:T(8,128)}) %reduce-scatter.42.cloned.1.call-update) | async-done | bytes 65552 | tf_op jit(solution)/shard_map/reduce_scatter | solution.py:441
  3969.4 135.3 %reduce-scatter.36.cloned.1.call-done = f32[64,256]{1,0:T(8,128)} async-done(((f32[2048,256]{1,0:T(8,128)}), f32[64,256]{1,0:T(8,128)}) %reduce-scatter.36.cloned.1.call-update) | async-done | bytes 65552 | tf_op jit(solution)/shard_map/reduce_scatter | solution.py:439
  4104.7 135.0 %reduce-scatter.38.cloned.1.call-done = f32[64,256]{1,0:T(8,128)} async-done(((f32[2048,256]{1,0:T(8,128)}), f32[64,256]{1,0:T(8,128)}) %reduce-scatter.38.cloned.1.call-update) | async-done | bytes 65552 | tf_op jit(solution)/shard_map/reduce_scatter | solution.py:440
  4239.7 135.0 %reduce-scatter.50.cloned.1.call-done = f32[64,256]{1,0:T(8,128)} async-done(((f32[2048,256]{1,0:T(8,128)}), f32[64,256]{1,0:T(8,128)}) %reduce-scatter.50.cloned.1.call-update) | async-done | bytes 65552 | tf_op jit(solution)/shard_map/reduce_scatter | solution.py:444
  (428 shorter events, 825.3 us)
Async XLA Ops:
  36.8 256.3 %all-gather.34.cloned.1.call-start = ((), (), s32[]{:S(2)}) async-start(), calls=%async_computation.30 | async-start | bytes 2359296 | tf_op jit(solution)/shard_map/all_gather | solution.py:103
  37.5 307.2 %all-gather.38.cloned.1.call-start = ((), (), s32[]{:S(2)}) async-start(), calls=%async_computation.32 | async-start | bytes 2359296 | tf_op jit(solution)/shard_map/all_gather | solution.py:106
  38.3 387.5 %all-gather.40.cloned.1.call-start = ((), (), s32[]{:S(2)}) async-start(), calls=%async_computation.34 | async-start | bytes 1179648 | tf_op jit(solution)/shard_map/all_gather | solution.py:114
  39.0 399.8 %reduce-scatter.26.cloned.1.call-start = ((), (), s32[]{:S(2)}) async-start(), calls=%async_computation.33 | async-start | bytes 5242880 | tf_op jit(solution)/shard_map/reduce_scatter | solution.py:151
  351.7 243.2 %all-gather.52.cloned.1.call-start = ((), (), s32[]{:S(2)}) async-start(), calls=%async_computation.40 | async-start | bytes 1179648 | tf_op jit(solution)/shard_map/all_gather | solution.py:125
  352.3 266.0 %all-gather.42.cloned.1.call-start = ((), (), s32[]{:S(2)}) async-start(), calls=%async_computation.35 | async-start | bytes 2621440 | tf_op jit(solution)/shard_map/all_gather | solution.py:132
  442.4 268.6 %all-gather.48.cloned.1.call-start = ((), (), s32[]{:S(2)}) async-start(), calls=%async_computation.38 | async-start | bytes 2359296 | tf_op jit(solution)/shard_map/all_gather | solution.py:124
  443.0 318.0 %all-gather.54.cloned.1.call-start = ((), (), s32[]{:S(2)}) async-start(), calls=%async_computation.41 | async-start | bytes 2359296 | tf_op jit(solution)/shard_map/all_gather | solution.py:126
  443.5 545.9 %all-gather.56.cloned.1.call-start = ((), (), s32[]{:S(2)}) async-start(), calls=%async_computation.42 | async-start | bytes 18874368 | tf_op jit(solution)/shard_map/all_gather | solution.py:122
  444.3 773.2 %all-gather.50.cloned.1.call-start = ((), (), s32[]{:S(2)}) async-start(), calls=%async_computation.39 | async-start | bytes 18874368 | tf_op jit(solution)/shard_map/all_gather | solution.py:121
  444.9 1000.8 %all-gather.44.cloned.1.call-start = ((), (), s32[]{:S(2)}) async-start(), calls=%async_computation.36 | async-start | bytes 18874368 | tf_op jit(solution)/shard_map/all_gather | solution.py:120
  445.6 1112.7 %reduce-scatter.30.cloned.1.call-start = ((), (), s32[]{:S(2)}) async-start(), calls=%async_computation.47 | async-start | bytes 5242880 | tf_op jit(solution)/shard_map/reduce_scatter | solution.py:138
  1604.6 266.6 %reduce-scatter.72.cloned.1.call-start = ((), (), s32[]{:S(2)}) async-start(), calls=%async_computation.69 | async-start | bytes 2359296 | tf_op jit(solution)/shard_map/reduce_scatter | solution.py:300
  1610.3 307.6 %reduce-scatter.28.cloned.1.call-start = ((), (), s32[]{:S(2)}) async-start(), calls=%async_computation.43 | async-start | bytes 5242880 | tf_op jit(solution)/shard_map/reduce_scatter | solution.py:151
  1625.8 357.3 %reduce-scatter.54.cloned.1.call-start = ((), (), s32[]{:S(2)}) async-start(), calls=%async_computation.60 | async-start | bytes 294912 | tf_op jit(solution)/shard_map/reduce_scatter | solution.py:430
  1638.8 408.4 %reduce-scatter.44.cloned.1.call-start = ((), (), s32[]{:S(2)}) async-start(), calls=%async_computation.55 | async-start | bytes 294912 | tf_op jit(solution)/shard_map/reduce_scatter | solution.py:427
  1641.3 471.9 %reduce-scatter.56.cloned.1.call-start = ((), (), s32[]{:S(2)}) async-start(), calls=%async_computation.61 | async-start | bytes 1179648 | tf_op jit(solution)/shard_map/reduce_scatter | solution.py:433
  1644.7 539.6 %reduce-scatter.40.cloned.1.call-start = ((), (), s32[]{:S(2)}) async-start(), calls=%async_computation.53 | async-start | bytes 2359296 | tf_op jit(solution)/shard_map/reduce_scatter | solution.py:424
  1648.9 606.0 %reduce-scatter.34.cloned.1.call-start = ((), (), s32[]{:S(2)}) async-start(), calls=%async_computation.50 | async-start | bytes 2359296 | tf_op jit(solution)/shard_map/reduce_scatter | solution.py:421
  1654.3 647.4 %reduce-scatter.32.cloned.1.call-start = ((), (), s32[]{:S(2)}) async-start(), calls=%async_computation.49 | async-start | bytes 5242880 | tf_op jit(solution)/shard_map/reduce_scatter | solution.py:138
  1678.4 910.8 %reduce-scatter.62.cloned.1.call-start = ((), (), s32[]{:S(2)}) async-start(), calls=%async_computation.64 | async-start | bytes 18874368 | tf_op jit(solution)/shard_map/reduce_scatter | solution.py:291
  1693.5 1181.7 %reduce-scatter.60.cloned.1.call-start = ((), (), s32[]{:S(2)}) async-start(), calls=%async_computation.63 | async-start | bytes 18874368 | tf_op jit(solution)/shard_map/reduce_scatter | solution.py:288
  1708.6 1452.1 %reduce-scatter.58.cloned.1.call-start = ((), (), s32[]{:S(2)}) async-start(), calls=%async_computation.62 | async-start | bytes 18874368 | tf_op jit(solution)/shard_map/reduce_scatter | solution.py:285
  1724.1 1575.0 %reduce-scatter.64.cloned.1.call-start = ((), (), s32[]{:S(2)}) async-start(), calls=%async_computation.65 | async-start | bytes 2162688 | tf_op jit(solution)/shard_map/reduce_scatter | solution.py:317
  1729.6 1704.4 %reduce-scatter.68.cloned.1.call-start = ((), (), s32[]{:S(2)}) async-start(), calls=%async_computation.67 | async-start | bytes 2162688 | tf_op jit(solution)/shard_map/reduce_scatter | solution.py:318
  1735.0 1831.7 %reduce-scatter.52.cloned.1.call-start = ((), (), s32[]{:S(2)}) async-start(), calls=%async_computation.59 | async-start | bytes 270336 | tf_op jit(solution)/shard_map/reduce_scatter | solution.py:445
  1737.4 1961.9 %reduce-scatter.48.cloned.1.call-start = ((), (), s32[]{:S(2)}) async-start(), calls=%async_computation.57 | async-start | bytes 270336 | tf_op jit(solution)/shard_map/reduce_scatter | solution.py:443
  1739.6 2094.8 %reduce-scatter.46.cloned.1.call-start = ((), (), s32[]{:S(2)}) async-start(), calls=%async_computation.56 | async-start | bytes 2162688 | tf_op jit(solution)/shard_map/reduce_scatter | solution.py:442
  1744.7 2224.8 %reduce-scatter.42.cloned.1.call-start = ((), (), s32[]{:S(2)}) async-start(), calls=%async_computation.54 | async-start | bytes 2162688 | tf_op jit(solution)/shard_map/reduce_scatter | solution.py:441
  1749.5 2355.2 %reduce-scatter.36.cloned.1.call-start = ((), (), s32[]{:S(2)}) async-start(), calls=%async_computation.51 | async-start | bytes 2162688 | tf_op jit(solution)/shard_map/reduce_scatter | solution.py:439
  1754.1 2485.6 %reduce-scatter.38.cloned.1.call-start = ((), (), s32[]{:S(2)}) async-start(), calls=%async_computation.52 | async-start | bytes 2162688 | tf_op jit(solution)/shard_map/reduce_scatter | solution.py:440
  1758.9 2615.8 %reduce-scatter.50.cloned.1.call-start = ((), (), s32[]{:S(2)}) async-start(), calls=%async_computation.58 | async-start | bytes 2162688 | tf_op jit(solution)/shard_map/reduce_scatter | solution.py:444
  (113 other events, 9270.8 us)
Sparse Core Ops, SparseCore 0:
  10.2 43.5 all-gather.31
  245.0 48.0 all-gather.33
  295.1 49.5 all-gather.37
  389.1 49.6 reduce-scatter.25
  504.7 49.2 all-gather.57
  662.9 48.0 all-gather.47
  713.2 47.7 all-gather.53
  763.2 226.2 all-gather.55
  991.7 225.7 all-gather.49
  1219.8 225.7 all-gather.43
  1595.5 63.4 reduce-scatter.73
  1663.0 66.8 reduce-scatter.65
  1733.7 66.8 reduce-scatter.69
  1804.3 66.8 reduce-scatter.71
  1921.8 61.2 reduce-scatter.53
  1986.9 60.2 reduce-scatter.43
  2050.6 62.5 reduce-scatter.55
  2117.1 67.1 reduce-scatter.39
  2188.0 66.8 reduce-scatter.33
  2258.2 43.4 reduce-scatter.31
  2305.5 283.7 reduce-scatter.61
  2593.4 281.7 reduce-scatter.59
  2878.8 281.7 reduce-scatter.57
  3163.6 135.3 reduce-scatter.63
  3301.7 132.2 reduce-scatter.67
  3436.9 129.7 reduce-scatter.51
  3569.5 129.7 reduce-scatter.47
  3702.2 132.1 reduce-scatter.45
  3837.1 132.3 reduce-scatter.41
  3972.3 132.2 reduce-scatter.35
  4107.4 132.3 reduce-scatter.37
  4242.5 132.1 reduce-scatter.49
  (14 shorter events, 493.5 us)
where the time goes:
time: 4390 us; the launch traced here: 4380 us
  waiting for transfers between devices  3730 us (85%)
  matrix products  318 us (7%)
  blocking collectives  257 us (6%)
  other arithmetic  46.9 us (1%)
    reduce_scatter x1, waiting for transfers between devices, body(): lax.psum_scatter(up_weight_grad.astype(jnp.bfloat16), 'dp', scatter_dimen...  282 us
    reduce_scatter x1, waiting for transfers between devices, body(): lax.psum_scatter(gate_weight_grad.astype(jnp.bfloat16), 'dp', scatter_dim...  281 us
    reduce_scatter x1, waiting for transfers between devices, body(): lax.psum_scatter(down_weight_grad.astype(jnp.bfloat16), 'dp', scatter_dim...  240 us
    all_gather x1, waiting for transfers between devices, gather_feed(): lax.all_gather(down_weight, 'dp', axis=1, tiled=True)  222 us
    all_gather x1, waiting for transfers between devices, gather_feed(): lax.all_gather(gate_weight, 'dp', axis=0, tiled=True)  213 us
    all_gather x1, waiting for transfers between devices, gather_feed(): lax.all_gather(up_weight, 'dp', axis=0, tiled=True)  211 us
    reduce_scatter x1, waiting for transfers between devices, body(): lax.psum_scatter(key_weight_grad, ('dp', 'mp'), scatter_dimension=0, tile...  135 us
    reduce_scatter x1, waiting for transfers between devices, body(): lax.psum_scatter(key_shrink_grad, ('dp', 'mp'), scatter_dimension=0, tile...  135 us
  transfers between devices with their start and end apart: 46, of which 39 were waited for; matrix products, arithmetic and copies ran while one was open for 7% of the time, Pallas kernels for 0%

commit v1 on v0

--- a/solution.py
+++ b/solution.py
@@ -1,7 +1,15 @@
+import functools
+from types import SimpleNamespace
+
 import jax
 import jax.numpy as jnp
 from jax import lax
+from jax.experimental import pallas as pl
+from jax.experimental.pallas import tpu as pltpu
 from jax.sharding import PartitionSpec as P
+
+MESH = pl.DeviceIdType.MESH
+MIB = 1 << 20
 
 EPS = 1e-06
 
@@ -56,6 +64,967 @@
     second = entries[..., half:]
     return jnp.concatenate(
         [first * cosine - second * sine, second * cosine + first * sine], axis=-1
+    )
+
+
+class Wires:
+    def __init__(self, levels, sends, lands, locals_=None):
+        self.sends, self.lands, self.locals = sends, lands, locals_
+        self.levels = levels
+        self.count = self.local_count = 0
+        self.open = []
+        dp, mp = lax.axis_index("dp"), lax.axis_index("mp")
+        self.dp, self.mp = dp, mp
+        self.z, self.y, self.x, self.c = dp // 2, dp % 2, mp // 2, mp % 2
+
+    def take(self, number=1):
+        first = self.count
+        self.count += number
+        assert self.count <= self.sends.shape[0], self.count
+        return first
+
+    def at(self, z, y, x, c):
+        return (z * 2 + y, x * 2 + c)
+
+    def up(self):
+        return self.at(self.z + 1, self.y, self.x, self.c)
+
+    def down(self):
+        return self.at(self.z - 1, self.y, self.x, self.c)
+
+    def over_x(self):
+        return self.at(self.z, self.y, 1 - self.x, self.c)
+
+    def over_y(self):
+        return self.at(self.z, 1 - self.y, self.x, self.c)
+
+    def over_core(self):
+        return self.at(self.z, self.y, self.x, 1 - self.c)
+
+    def copy(self, source, target, out, land, device):
+        return pltpu.make_async_remote_copy(
+            src_ref=source,
+            dst_ref=target,
+            send_sem=self.sends.at[out],
+            recv_sem=self.lands.at[land],
+            device_id=device,
+            device_id_type=MESH,
+        )
+
+    def send(self, source, target, out, land, device, when=True):
+        made = self.copy(source, target, out, land, device)
+        under(when, made.start)
+        self.open.append((when, made.wait_send))
+
+    def landed(self, target, land):
+        self.copy(target, target, land, land, self.over_x()).wait_recv()
+
+    def local(self, source, target):
+        made = pltpu.make_async_copy(source, target, self.locals.at[self.local_count])
+        self.local_count += 1
+        assert self.local_count <= self.locals.shape[0], self.local_count
+        made.start()
+        return made
+
+    def finish(self):
+        for when, wait in self.open:
+            under(when, wait)
+
+    def greet(self, far=False, flat=False):
+        barrier = pltpu.get_barrier_semaphore()
+
+        def call(device):
+            pl.semaphore_signal(barrier, inc=1, device_id=device, device_id_type=MESH)
+
+        call(self.over_x())
+        call(self.over_core())
+        if far:
+            call(self.at(self.z, self.y, 1 - self.x, 1 - self.c))
+            for step in range(1, 2 * self.levels):
+                call((lax.rem(self.dp + step, 2 * self.levels), self.mp))
+            pl.semaphore_wait(barrier, 2 + 2 * self.levels)
+            return
+        if flat:
+            pl.semaphore_wait(barrier, 2)
+            return
+        call(self.over_y())
+        pl.when(self.z > 0)(lambda: call(self.down()))
+        pl.when(self.z < self.levels - 1)(lambda: call(self.up()))
+        ends = jnp.where(self.z > 0, 1, 0) + jnp.where(self.z < self.levels - 1, 1, 0)
+        pl.semaphore_wait(barrier, 3 + ends)
+
+
+def under(when, act):
+    if when is True:
+        act()
+    else:
+        pl.when(when)(act)
+
+
+def sides(w, step):
+    yield (True, w.z - step, w.z >= step)
+    yield (False, w.z + step, w.z < w.levels - step)
+
+
+def gather_all(w, own, at, parts):
+    z, y, x, c = w.z, w.y, w.x, w.c
+    n = w.levels
+    rise, fall, by_x, by_y, last_x, last_y = (w.take(n) for _ in range(6))
+    by_core = w.take(4 * n)
+
+    def core(block, zs, ys, xs):
+        place = by_core + zs * 4 + ys * 2 + xs
+        return (block, block, place, place, w.over_core())
+
+    here = at(z, y, x, c)
+    kept = w.local(own, here)
+    w.send(own, here, rise + z, rise + z, w.up(), z < n - 1)
+    w.send(own, here, fall + z, fall + z, w.down(), z > 0)
+    w.send(own, here, by_x + z, by_x + z, w.over_x())
+    w.send(own, here, by_y + z, by_y + z, w.over_y())
+    place = by_core + z * 4 + y * 2 + x
+    w.send(own, here, place, place, w.over_core())
+    yield
+
+    def plane(zs, ok):
+        block = at(zs, y, 1 - x, c)
+        under(ok, lambda: w.landed(block, by_x + zs))
+        for piece in parts(block)[:1]:
+            if piece is not None:
+                w.send(piece, piece, last_y + zs, last_y + zs, w.over_y(), ok)
+        w.send(*core(block, zs, y, 1 - x), ok)
+        block = at(zs, 1 - y, x, c)
+        under(ok, lambda: w.landed(block, by_y + zs))
+        for piece in parts(block)[1:]:
+            if piece is not None:
+                w.send(piece, piece, last_x + zs, last_x + zs, w.over_x(), ok)
+        w.send(*core(block, zs, 1 - y, x), ok)
+
+    plane(z, True)
+    yield
+    for step in range(1, n):
+        for rising, zs, ok in sides(w, step):
+            block = at(zs, y, x, c)
+            lane = rise if rising else fall
+            under(ok, lambda: w.landed(block, lane + zs))
+            if rising:
+                w.send(block, block, rise + zs, rise + zs, w.up(), jnp.logical_and(ok, z < n - 1))
+            else:
+                w.send(block, block, fall + zs, fall + zs, w.down(), jnp.logical_and(ok, z > 0))
+            w.send(block, block, by_x + zs, by_x + zs, w.over_x(), ok)
+            w.send(block, block, by_y + zs, by_y + zs, w.over_y(), ok)
+            w.send(*core(block, zs, y, x), ok)
+        yield
+        for _, zs, ok in sides(w, step):
+            plane(zs, ok)
+        yield
+    for step in range(n):
+        for _, zs, ok in sides(w, step) if step else [(True, z, True)]:
+            block = at(zs, 1 - y, 1 - x, c)
+            for piece, lane in zip(parts(block), (last_y, last_x)):
+                if piece is not None:
+                    under(ok, lambda: w.landed(piece, lane + zs))
+            w.send(*core(block, zs, 1 - y, 1 - x), ok)
+        yield
+    for zs in range(n):
+        for ys in range(2):
+            for xs in range(2):
+                w.landed(at(zs, ys, xs, 1 - c), by_core + zs * 4 + ys * 2 + xs)
+    kept.wait()
+
+
+def gather_dp(w, own, at):
+    z, y, n = w.z, w.y, w.levels
+    rise, fall, by_y = (w.take(n) for _ in range(3))
+    here = at(z, y)
+    kept = w.local(own, here)
+    w.send(own, here, rise + z, rise + z, w.up(), z < n - 1)
+    w.send(own, here, fall + z, fall + z, w.down(), z > 0)
+    w.send(own, here, by_y + z, by_y + z, w.over_y())
+    yield
+    yield
+    for step in range(1, n):
+        for rising, zs, ok in sides(w, step):
+            block = at(zs, y)
+            lane = rise if rising else fall
+            under(ok, lambda: w.landed(block, lane + zs))
+            if rising:
+                w.send(block, block, rise + zs, rise + zs, w.up(), jnp.logical_and(ok, z < n - 1))
+            else:
+                w.send(block, block, fall + zs, fall + zs, w.down(), jnp.logical_and(ok, z > 0))
+            w.send(block, block, by_y + zs, by_y + zs, w.over_y(), ok)
+        yield
+        yield
+    for zs in range(n):
+        w.landed(at(zs, 1 - y), by_y + zs)
+    kept.wait()
+
+
+def gather_mp(w, own, at):
+    x, c = w.x, w.c
+    first, second = w.take(), w.take(2)
+    here = at(x, c)
+    kept = w.local(own, here)
+    w.send(own, here, first, first, w.over_x())
+    w.send(own, here, second, second, w.over_core())
+    yield
+    block = at(1 - x, c)
+    w.landed(block, first)
+    w.send(block, block, second + 1, second + 1, w.over_core())
+    yield
+    w.landed(at(x, 1 - c), second)
+    w.landed(at(1 - x, 1 - c), second + 1)
+    kept.wait()
+
+
+def exchange_dp(w, source, target):
+    count = 2 * w.levels
+    first = w.take(count)
+    kept = w.local(source(w.dp), target(w.dp))
+    for step in range(1, count):
+        there = lax.rem(w.dp + step, count)
+        w.send(source(there), target(w.dp), first + step, first + step, (there, w.mp))
+        yield
+    for step in range(1, count):
+        w.landed(target(lax.rem(w.dp + count - step, count)), first + step)
+    kept.wait()
+
+
+PACE = 6
+
+
+def turn(steps, after=()):
+    spare = [one for one in after for _ in range(7)]
+    turn_on(steps, spare)
+    for one in spare:
+        next(one)
+    turn_on(after)
+
+
+def turn_on(steps, spare=()):
+    steps = list(steps)
+    while steps:
+        for _ in range(min(PACE, len(spare))):
+            next(spare.pop(0))
+        left = []
+        for one in steps:
+            try:
+                next(one)
+                left.append(one)
+            except StopIteration:
+                pass
+        steps = left
+
+
+CHUNK = 16
+
+
+def add_up(target, *sources):
+    rows = target.shape[0]
+
+    def one(i, unused):
+        part = pl.ds(pl.multiple_of(i * CHUNK, CHUNK), CHUNK)
+        total = sources[0][part, :].astype(jnp.float32)
+        for source in sources[1:]:
+            total = total + source[part, :].astype(jnp.float32)
+        target[part, :] = total.astype(target.dtype)
+        return unused
+
+    lax.fori_loop(0, rows // CHUNK, one, 0)
+
+
+def chain_z(w, own, below, above, out):
+    z, n = w.z, w.levels
+    rise, fall = w.take(n), w.take(n)
+    for step in range(n - 1, 0, -1):
+        for rising, zt, ok in ((True, z + step, z < n - step), (False, z - step, z >= step)):
+            lane = rise if rising else fall
+            slot = below(zt) if rising else above(zt)
+            inner = jnp.logical_and(ok, (z > 0) if rising else (z < n - 1))
+
+            def take_in():
+                w.landed(slot, lane + zt)
+                add_up(own(zt), own(zt), slot)
+
+            under(inner, take_in)
+            w.send(own(zt), slot, lane + zt, lane + zt, w.up() if rising else w.down(), ok)
+        yield
+    under(z > 0, lambda: w.landed(below(z), rise + z))
+    under(z < n - 1, lambda: w.landed(above(z), fall + z))
+    under(z == 0, lambda: add_up(out, own(z), above(z)))
+    under(z == n - 1, lambda: add_up(out, own(z), below(z)))
+    under(
+        jnp.logical_and(z > 0, z < n - 1), lambda: add_up(out, own(z), below(z), above(z))
+    )
+
+
+def scatter_all(w, part, own, core, half_x, half_y, full_x, full_y, below, above, out):
+    z, y, x, c, n = w.z, w.y, w.x, w.c, w.levels
+    lanes = {name: w.take(n) for name in ("hx", "hy", "fx", "fy")}
+    to_core = w.take(4 * n)
+    rows = own.shape[1]
+    cut = rows // 2 // CHUNK * CHUNK
+    halves = (pl.ds(0, cut), pl.ds(cut, rows - cut))
+
+    def slot(zs, ys, xs):
+        return zs * 4 + ys * 2 + xs
+
+    kinds = ((1 - y, 1 - x), (1 - y, x), (y, 1 - x), (y, x))
+    order = [(True, z, True)] if n == 1 else []
+    for step in range(n - 1, 0, -1):
+        order += [side for side in sides(w, step)]
+    order.append((True, z, True))
+    kept = {}
+    for kind, (ys, xs) in enumerate(kinds):
+        for place, (_, zs, ok) in enumerate(order):
+            here = slot(zs, ys, xs)
+            w.send(
+                part.at[(zs * 2 + ys) * 4 + xs * 2 + (1 - c)],
+                core.at[here],
+                to_core + here,
+                to_core + here,
+                w.over_core(),
+                ok,
+            )
+            made = pltpu.make_async_copy(
+                part.at[(zs * 2 + ys) * 4 + xs * 2 + c], own.at[here], w.locals.at[here]
+            )
+            under(ok, made.start)
+            kept[kind, place] = made
+    yield
+    for kind, (ys, xs) in enumerate(kinds):
+        for place, (_, zs, ok) in enumerate(order):
+            here = slot(zs, ys, xs)
+
+            def act():
+                kept[kind, place].wait()
+                w.landed(core.at[here], to_core + here)
+                add_up(own.at[here], own.at[here], core.at[here])
+                if kind == 1:
+                    w.landed(half_x.at[zs], lanes["hx"] + zs)
+                    add_up(own.at[here, halves[0]], own.at[here, halves[0]], half_x.at[zs])
+                if kind == 2:
+                    w.landed(half_y.at[zs], lanes["hy"] + zs)
+                    add_up(own.at[here, halves[1]], own.at[here, halves[1]], half_y.at[zs])
+                if kind == 3:
+                    w.landed(full_x.at[zs], lanes["fx"] + zs)
+                    w.landed(full_y.at[zs], lanes["fy"] + zs)
+                    add_up(own.at[here], own.at[here], full_x.at[zs], full_y.at[zs])
+
+            under(ok, act)
+            if kind == 0:
+                for name, half, target, device in (
+                    ("hx", halves[0], half_x, w.over_x()),
+                    ("hy", halves[1], half_y, w.over_y()),
+                ):
+                    lane = lanes[name] + zs
+                    w.send(own.at[here, half], target.at[zs], lane, lane, device, ok)
+            if kind == 1:
+                w.send(own.at[here], full_y.at[zs], lanes["fy"] + zs, lanes["fy"] + zs, w.over_y(), ok)
+            if kind == 2:
+                w.send(own.at[here], full_x.at[zs], lanes["fx"] + zs, lanes["fx"] + zs, w.over_x(), ok)
+        yield
+
+    yield from chain_z(
+        w, lambda zt: own.at[slot(zt, y, x)], lambda zt: below.at[zt], lambda zt: above.at[zt], out
+    )
+
+
+def scatter_all_scratch(n, rows, columns):
+    cut = rows // 2 // CHUNK * CHUNK
+    shapes = [(4 * n, rows)] * 2 + [(n, cut), (n, rows - cut)] + [(n, rows)] * 4
+    return [pltpu.VMEM(shape + (columns,), jnp.bfloat16) for shape in shapes]
+
+
+def scatter_dp(w, part, own, over, below, above, out):
+    z, y, n = w.z, w.y, w.levels
+    by_y = w.take(n)
+    kept = []
+    order = []
+    for step in range(n - 1, 0, -1):
+        order += [side for side in sides(w, step)]
+    order.append((True, z, True))
+    for _, zs, ok in order:
+        w.send(part.at[zs * 2 + 1 - y], over.at[zs], by_y + zs, by_y + zs, w.over_y(), ok)
+        made = pltpu.make_async_copy(part.at[zs * 2 + y], own.at[zs], w.locals.at[4 * n + zs])
+        under(ok, made.start)
+        kept.append(made)
+    yield
+    for made, (_, zs, ok) in zip(kept, order):
+
+        def act():
+            made.wait()
+            w.landed(over.at[zs], by_y + zs)
+            add_up(own.at[zs], own.at[zs], over.at[zs])
+
+        under(ok, act)
+    yield
+    yield from chain_z(
+        w, lambda zt: own.at[zt], lambda zt: below.at[zt], lambda zt: above.at[zt], out
+    )
+
+
+def scatter_mp(w, part, own, first, second, out):
+    x, c = w.x, w.c
+    core, cross = w.take(2), w.take()
+    kept = []
+    for i, xs in enumerate((1 - x, x)):
+        w.send(part.at[xs * 2 + 1 - c], first.at[i], core + i, core + i, w.over_core())
+        kept.append(w.local(part.at[xs * 2 + c], own.at[i]))
+    kept[0].wait()
+    w.landed(first.at[0], core)
+    add_up(own.at[0], own.at[0], first.at[0])
+    w.send(own.at[0], second, cross, cross, w.over_x())
+    kept[1].wait()
+    w.landed(first.at[1], core + 1)
+    w.landed(second, cross)
+    add_up(out, own.at[1], first.at[1], second)
+
+
+ANY = pl.BlockSpec(memory_space=pl.ANY)
+WHOLE = pl.BlockSpec(memory_space=pltpu.VMEM)
+
+
+def call(kernel, identity, arrays, outs, scratch, signals, locals_, in_vmem=False, name=None):
+    return pl.pallas_call(
+        kernel,
+        out_shape=[jax.ShapeDtypeStruct(shape, kind) for shape, kind, _ in outs],
+        in_specs=[ANY] * len(arrays),
+        out_specs=[WHOLE if near else ANY for _, _, near in outs],
+        scratch_shapes=list(scratch)
+        + [
+            pltpu.SemaphoreType.DMA((signals,)),
+            pltpu.SemaphoreType.DMA((signals,)),
+            pltpu.SemaphoreType.DMA((max(locals_, 1),)),
+        ],
+        compiler_params=pltpu.CompilerParams(
+            collective_id=identity, has_side_effects=True, vmem_limit_bytes=60 * MIB
+        ),
+        name=name,
+    )(*arrays)
+
+
+def halves(block):
+    rows = block.shape[0]
+    cut = rows // 2 // CHUNK * CHUNK
+    return (block.at[pl.ds(0, cut)], block.at[pl.ds(cut, rows - cut)])
+
+
+def by_x_last(block):
+    return (None, block)
+
+
+def rows_of(ref, index, rows):
+    return ref.at[pl.ds(pl.multiple_of(index * rows, rows), rows)]
+
+
+def columns_of(ref, index, columns):
+    return ref.at[:, pl.ds(pl.multiple_of(index * columns, columns), columns)]
+
+
+def flat(z, y, x, c):
+    return (z * 2 + y) * 4 + x * 2 + c
+
+
+def begin(levels, tensors):
+    names = list(vars(tensors))
+    count = 2 * levels
+    wide = tensors.query_weight.shape[1]
+    unit = tensors.gate_weight.shape[1] // count
+    deep = tensors.gate_weight.shape[0] * count
+    rows = tensors.layer_input.shape[0]
+    packed = tensors.maps.shape
+    low = tensors.gate_expand.shape[0] * count
+    piece = deep // 4
+    shapes = dict(
+        layer_input=(4, rows, deep),
+        maps=(4 * count * packed[0], packed[1]),
+        output_expand=(low, deep),
+        down_expand=(low, deep),
+        query_weight=(deep, wide),
+        output_weight=(wide, deep),
+        expands=(low, tensors.expands.shape[1]),
+        output_shrink=(tensors.output_shrink.shape[0] * count, low),
+        output_grad=(4 * count, rows, deep),
+        gate_weight=(deep, unit),
+        up_weight=(deep, unit),
+        down_weight=(unit, deep),
+        gate_expand=(low, unit),
+        up_expand=(low, unit),
+    )
+
+    def kernel(*refs):
+        given = SimpleNamespace(**dict(zip(names, refs)))
+        got = SimpleNamespace(**dict(zip(shapes, refs[len(names) :])))
+        w = Wires(levels, *refs[len(names) + len(shapes) :])
+        w.greet(far=True)
+
+        def expand_at(into):
+            def at(z, y, x, c):
+                return into.at[
+                    pl.ds(pl.multiple_of((z * 2 + y) * (low // count), low // count), low // count),
+                    pl.ds(pl.multiple_of((x * 2 + c) * piece, piece), piece),
+                ]
+
+            return at
+
+        steps = [
+            gather_mp(w, given.layer_input, lambda x, c: got.layer_input.at[x * 2 + c]),
+            gather_dp(w, given.query_weight, lambda z, y: rows_of(got.query_weight, z * 2 + y, deep // count)),
+            gather_dp(w, given.output_weight, lambda z, y: columns_of(got.output_weight, z * 2 + y, deep // count)),
+            gather_all(w, given.maps, lambda z, y, x, c: rows_of(got.maps, flat(z, y, x, c), packed[0]), halves),
+            gather_dp(w, given.expands, lambda z, y: rows_of(got.expands, z * 2 + y, low // count)),
+            gather_dp(
+                w,
+                given.output_shrink,
+                lambda z, y: rows_of(got.output_shrink, z * 2 + y, given.output_shrink.shape[0]),
+            ),
+        ]
+        for own, into in ((given.output_expand, got.output_expand), (given.down_expand, got.down_expand)):
+            steps.append(gather_all(w, columns_of(own, w.mp, piece), expand_at(into), halves))
+        steps.append(gather_all(w, given.output_grad, lambda z, y, x, c: got.output_grad.at[flat(z, y, x, c)], halves))
+        after = [
+            exchange_dp(w, lambda dp: columns_of(given.gate_weight, dp, unit), lambda dp: rows_of(got.gate_weight, dp, deep // count)),
+            exchange_dp(w, lambda dp: columns_of(given.up_weight, dp, unit), lambda dp: rows_of(got.up_weight, dp, deep // count)),
+            exchange_dp(w, lambda dp: rows_of(given.down_weight, dp, unit), lambda dp: columns_of(got.down_weight, dp, deep // count)),
+            exchange_dp(w, lambda dp: columns_of(given.gate_expand, dp, unit), lambda dp: rows_of(got.gate_expand, dp, low // count)),
+            exchange_dp(w, lambda dp: columns_of(given.up_expand, dp, unit), lambda dp: rows_of(got.up_expand, dp, low // count)),
+        ]
+        turn(steps, after)
+        w.finish()
+
+    kind = jnp.bfloat16
+    given = call(
+        kernel,
+        0,
+        list(vars(tensors).values()),
+        [(shape, kind, False) for shape in shapes.values()],
+        [],
+        64 * levels + 48 * levels * 3,
+        32,
+        name="begin",
+    )
+    return SimpleNamespace(**dict(zip(shapes, given)))
+
+
+def spread(levels, rows):
+    here, wide = rows.shape
+
+    def kernel(own, out, *sems):
+        w = Wires(levels, *sems)
+        w.greet()
+        turn([gather_all(w, own, lambda z, y, x, c: out.at[flat(z, y, x, c)], halves)])
+        w.finish()
+
+    (out,) = call(
+        kernel, 1, [rows], [((8 * levels, here, wide), rows.dtype, False)], [], 40 * levels, 4, name="spread"
+    )
+    return out
+
+
+def collect(levels, part):
+    _, here, wide = part.shape
+
+    def kernel(given, out, *refs):
+        w = Wires(levels, *refs[-3:])
+        w.greet()
+        turn([scatter_all(w, given, *refs[:-3], out)])
+        w.finish()
+
+    (out,) = call(
+        kernel,
+        2,
+        [part],
+        [((here, wide), jnp.float32, True)],
+        scatter_all_scratch(levels, here, wide),
+        40 * levels,
+        4 * levels,
+        name="collect",
+    )
+    return out
+
+
+def share_mp(levels, rows):
+    def kernel(own, out, *sems):
+        w = Wires(levels, *sems)
+        w.greet(flat=True)
+        turn([gather_mp(w, own, lambda x, c: out.at[x * 2 + c])])
+        w.finish()
+
+    (out,) = call(kernel, 3, [rows], [((4,) + rows.shape, rows.dtype, False)], [], 16, 4, name="share_mp")
+    return out
+
+
+def sum_mp(levels, part):
+    _, here, wide = part.shape
+
+    def kernel(given, out, own, first, second, *sems):
+        w = Wires(levels, *sems)
+        w.greet(flat=True)
+        scatter_mp(w, given, own, first, second, out)
+        w.finish()
+
+    (out,) = call(
+        kernel,
+        4,
+        [part],
+        [((here, wide), jnp.float32, True)],
+        [pltpu.VMEM((2, here, wide), part.dtype)] * 2 + [pltpu.VMEM((here, wide), part.dtype)],
+        16,
+        4,
+        name="sum_mp",
+    )
+    return out
+
+
+def end(levels, small, split, units, share):
+    names = list(vars(units))
+    count = 2 * levels
+    deep, unit = units.gate_weight.shape
+    low = units.gate_expand.shape[0]
+    shapes = dict(
+        gate_weight=(deep // count, unit * count),
+        up_weight=(deep // count, unit * count),
+        down_weight=(unit * count, deep // count),
+        gate_expand=(low // count, unit * count),
+        up_expand=(low // count, unit * count),
+    )
+    few, wide = small.shape[1:]
+    many, flatly = split.shape[1:]
+    scratch = scatter_all_scratch(levels, few, wide)
+    scratch += [pltpu.VMEM((levels, many, flatly), jnp.bfloat16)] * 4
+    first = len(names) + 2
+
+    def kernel(*refs):
+        small_ref, split_ref = refs[:2]
+        given = SimpleNamespace(**dict(zip(names, refs[2:])))
+        got = SimpleNamespace(**dict(zip(shapes, refs[first:])))
+        after = first + len(shapes)
+        small_out, split_out, shared = refs[after : after + 3]
+        buffers = refs[after + 3 : -3]
+        w = Wires(levels, *refs[-3:])
+        w.local_count = 5 * levels
+        w.greet(far=True)
+
+        def over_all():
+            yield from scatter_all(w, small_ref, *buffers[:8], small_out)
+            mine = small_out.at[:, pl.ds(wide - share, share)]
+            yield from gather_mp(w, mine, lambda x, c: shared.at[x * 2 + c])
+
+        steps = [
+            scatter_dp(w, split_ref, *buffers[8:], split_out),
+            over_all(),
+        ]
+        after = [
+            exchange_dp(w, lambda dp: rows_of(given.gate_weight, dp, deep // count), lambda dp: columns_of(got.gate_weight, dp, unit)),
+            exchange_dp(w, lambda dp: rows_of(given.up_weight, dp, deep // count), lambda dp: columns_of(got.up_weight, dp, unit)),
+            exchange_dp(w, lambda dp: columns_of(given.down_weight, dp, deep // count), lambda dp: rows_of(got.down_weight, dp, unit)),
+            exchange_dp(w, lambda dp: rows_of(given.gate_expand, dp, low // count), lambda dp: columns_of(got.gate_expand, dp, unit)),
+            exchange_dp(w, lambda dp: rows_of(given.up_expand, dp, low // count), lambda dp: columns_of(got.up_expand, dp, unit)),
+        ]
+        turn(steps, after)
+        w.finish()
+
+    outs = [(shape, jnp.bfloat16, False) for shape in shapes.values()]
+    outs += [((few, wide), jnp.float32, True), ((many, flatly), jnp.float32, True), ((4, few, share), jnp.float32, True)]
+    made = call(
+        kernel,
+        5,
+        [small, split] + list(vars(units).values()),
+        outs,
+        scratch,
+        64 * levels + 40 * levels,
+        5 * levels + 16,
+        name="end",
+    )
+    return SimpleNamespace(**dict(zip(shapes, made))), made[-3], made[-2], made[-1]
+
+
+def low(rows):
+    return rows.astype(jnp.bfloat16)
+
+
+def unit_rows(rows):
+    scale = lax.rsqrt(jnp.mean(rows * rows, axis=-1, keepdims=True) + EPS)
+    return rows * scale, scale
+
+
+def norm_back(grad, normed, scale):
+    return scale * (grad - normed * jnp.mean(grad * normed, axis=-1, keepdims=True))
+
+
+def by_unit(
+    levels,
+    layer_input,
+    output_grad,
+    attention_gain,
+    query_weight,
+    key_weight,
+    value_weight,
+    output_weight,
+    query_shrink,
+    query_expand,
+    key_shrink,
+    key_expand,
+    value_shrink,
+    value_expand,
+    output_shrink,
+    output_expand,
+    feedforward_gain,
+    gate_weight,
+    up_weight,
+    down_weight,
+    gate_shrink,
+    gate_expand,
+    up_shrink,
+    up_expand,
+    down_shrink,
+    down_expand,
+    group_ids,
+    positions,
+    segments,
+):
+    count = 2 * levels
+    rows = layer_input.shape[0]
+    tokens = 4 * rows
+    deep = layer_input.shape[1]
+    head = key_weight.shape[1]
+    heads = query_weight.shape[1] // head
+    rank = query_expand.shape[0] * count
+    mp = lax.axis_index("mp")
+    share = query_shrink.shape[0] // 4
+
+    gains = jnp.stack([attention_gain, feedforward_gain], axis=1)
+    gains = jnp.pad(gains, ((0, 0), (0, 126)))
+    maps = jnp.concatenate(
+        [key_weight, value_weight, query_shrink, key_shrink, value_shrink, gate_shrink, up_shrink, gains],
+        axis=1,
+    )
+    maps = lax.dynamic_slice_in_dim(maps, mp * share, share, 0)
+    expands = jnp.concatenate([query_expand, key_expand, value_expand], axis=1)
+    got = begin(
+        levels,
+        SimpleNamespace(
+            layer_input=layer_input,
+            maps=maps,
+            output_expand=output_expand,
+            down_expand=down_expand,
+            query_weight=query_weight,
+            output_weight=output_weight,
+            expands=expands,
+            output_shrink=output_shrink,
+            output_grad=output_grad,
+            gate_weight=gate_weight,
+            up_weight=up_weight,
+            down_weight=down_weight,
+            gate_expand=gate_expand,
+            up_expand=up_expand,
+        ),
+    )
+    maps = got.maps
+    key_w, value_w = maps[:, :head], maps[:, head : 2 * head]
+    query_a, key_a, value_a, gate_a, up_a = (
+        maps[:, 2 * head + i * rank : 2 * head + (i + 1) * rank] for i in range(5)
+    )
+    gain_one = maps[:, 2 * head + 5 * rank : 2 * head + 5 * rank + 1].astype(jnp.float32)
+    gain_two = maps[:, 2 * head + 5 * rank + 1 : 2 * head + 5 * rank + 2].astype(jnp.float32)
+    query_b = got.expands[:, : heads * head]
+    key_b = got.expands[:, heads * head : (heads + 1) * head]
+    value_b = got.expands[:, (heads + 1) * head :]
+    output_a, output_b = got.output_shrink, got.output_expand
+    query_full = low(gain_one * (got.query_weight.astype(jnp.float32) + matmul(query_a, query_b)))
+    key_full = low(gain_one * (key_w.astype(jnp.float32) + matmul(key_a, key_b)))
+    value_full = low(gain_one * (value_w.astype(jnp.float32) + matmul(value_a, value_b)))
+    inward = jnp.concatenate([query_full, key_full, value_full], axis=1)
+    outward = low(got.output_weight.astype(jnp.float32) + matmul(output_a, output_b))
+
+    allowed = (
+        (group_ids[:, None] == group_ids[None, :])
+        & (positions[None, :] <= positions[:, None])
+        & ((segments[None, :] == 0) | (segments[None, :] == segments[:, None]))
+    )
+    group_rows = got.layer_input.reshape(tokens, deep).astype(jnp.float32)
+    normed = low(unit_rows(group_rows)[0])
+    lin = matmul(normed, inward)
+    wide = heads * head
+    queries = low(rotary(lin[:, :wide].reshape(tokens, heads, head), positions, 1.0) * head ** (-0.5))
+    keys = low(rotary(lin[:, None, wide : wide + head], positions, 1.0)[:, 0, :])
+    values = low(lin[:, wide + head :])
+    scores = jnp.einsum("thd,sd->hts", queries, keys, preferred_element_type=jnp.float32)
+    scores = jnp.where(allowed[None], scores, -1e30)
+    expo = jnp.exp(scores - jnp.max(scores, axis=-1, keepdims=True))
+    probability = expo / jnp.sum(expo, axis=-1, keepdims=True)
+    probability_low = low(probability)
+    mixed = low(
+        jnp.einsum("hts,sd->thd", probability_low, values, preferred_element_type=jnp.float32)
+    ).reshape(tokens, wide)
+    branch = sum_mp(levels, low(matmul(mixed, outward)).reshape(4, rows, deep))
+    own_rows = layer_input.astype(jnp.float32)
+    middle = own_rows + branch
+
+    gate_up = low(
+        gain_two
+        * (
+            jnp.concatenate([got.gate_weight, got.up_weight], axis=1).astype(jnp.float32)
+            + jnp.concatenate([matmul(gate_a, got.gate_expand), matmul(up_a, got.up_expand)], axis=1)
+        )
+    )
+    unit = got.gate_weight.shape[1]
+    down_a, down_b = down_shrink, got.down_expand
+    down_full = low(got.down_weight.astype(jnp.float32) + matmul(down_a, down_b))
+    normed_middle, scale_middle = unit_rows(middle)
+    feed = spread(levels, low(normed_middle)).reshape(4 * count * rows, deep)
+    grads = got.output_grad.reshape(4 * count * rows, deep)
+    pre = matmul(feed, gate_up)
+    hidden_wide, pull = jax.vjp(
+        lambda gate, up: jax.nn.gelu(gate, approximate=True) * up, pre[:, :unit], pre[:, unit:]
+    )
+    hidden = low(hidden_wide)
+    grad_pre = low(jnp.concatenate(pull(against(grads, down_full)), axis=1))
+    blocks = (4 * count, rows, deep)
+    branch = collect(levels, low(matmul(hidden, down_full)).reshape(blocks))
+    grad_normed = collect(levels, low(against(grad_pre, gate_up)).reshape(blocks))
+    result = low(middle + branch)
+    grad_middle = output_grad.astype(jnp.float32) + norm_back(grad_normed, normed_middle, scale_middle)
+
+    down_grad = outer_sum(hidden, grads)
+    gate_up_normed = outer_sum(feed, grad_pre)
+    feed_gain = jnp.sum(gate_up_normed * gate_up.astype(jnp.float32), axis=1, keepdims=True) / gain_two
+    gate_up_grad = low(gate_up_normed * gain_two)
+    down_grad_low = low(down_grad)
+    down_shrink_grad = against(down_grad_low, down_b)
+    down_b_part = outer_sum(down_a, down_grad_low)
+    gate_b_grad = low(outer_sum(gate_a, gate_up_grad[:, :unit]))
+    up_b_grad = low(outer_sum(up_a, gate_up_grad[:, unit:]))
+    gate_a_part = against(gate_up_grad[:, :unit], got.gate_expand)
+    up_a_part = against(gate_up_grad[:, unit:], got.up_expand)
+
+    grad_branch = share_mp(levels, low(grad_middle)).reshape(tokens, deep)
+    output_grad_w = outer_sum(mixed, grad_branch)
+    grad_mixed = low(against(grad_branch, outward)).reshape(tokens, heads, head)
+    grad_values = jnp.einsum("hts,thd->sd", probability_low, grad_mixed, preferred_element_type=jnp.float32)
+    grad_probability = jnp.einsum("thd,sd->hts", grad_mixed, values, preferred_element_type=jnp.float32)
+    grad_scores = low(
+        probability * (grad_probability - jnp.sum(probability * grad_probability, axis=-1, keepdims=True))
+    )
+    grad_queries = jnp.einsum("hts,sd->thd", grad_scores, keys, preferred_element_type=jnp.float32)
+    grad_keys = jnp.einsum("hts,thd->sd", grad_scores, queries, preferred_element_type=jnp.float32)
+    grad_query = rotary(grad_queries * head ** (-0.5), positions, -1.0).reshape(tokens, wide)
+    grad_key = rotary(grad_keys[:, None, :], positions, -1.0)[:, 0, :]
+    grad_lin = low(jnp.concatenate([grad_query, grad_key, grad_values], axis=1))
+    grad_rows = sum_mp(levels, low(against(grad_lin, inward)).reshape(4, rows, deep))
+    normed_own, scale_own = unit_rows(own_rows)
+    input_grad = grad_middle + norm_back(grad_rows, normed_own, scale_own)
+
+    lin_normed = outer_sum(normed, grad_lin)
+    attention_gain_part = jnp.sum(lin_normed * inward.astype(jnp.float32), axis=1, keepdims=True) / gain_one
+    lin_grad = low(lin_normed * gain_one)
+    query_part, key_part, value_part = (
+        lin_grad[:, :wide],
+        lin_grad[:, wide : wide + head],
+        lin_grad[:, wide + head :],
+    )
+    query_b_part = outer_sum(query_a, query_part)
+    key_b_part = outer_sum(key_a, key_part)
+    value_b_part = outer_sum(value_a, value_part)
+    query_a_part = against(query_part, query_b)
+    output_low = low(output_grad_w)
+    output_a_part = against(output_low, output_b)
+    output_b_part = outer_sum(output_a, output_low)
+
+    def by_device(array):
+        return low(array).reshape(4 * count, array.shape[0] // (4 * count), array.shape[1])
+
+    def fold(array):
+        return by_device(array).reshape(4 * count, share, -1)
+
+    def fold_wide(array):
+        cut = low(array).reshape(count, array.shape[0] // count, 4, array.shape[1] // 4)
+        return cut.transpose(0, 2, 1, 3).reshape(4 * count, share, -1)
+
+    gain_part = jnp.pad(jnp.concatenate([attention_gain_part, feed_gain], axis=1), ((0, 0), (0, 62)))
+    small = jnp.concatenate(
+        [
+            by_device(key_part),
+            by_device(value_part),
+            by_device(query_a_part),
+            by_device(gate_a_part),
+            by_device(up_a_part),
+            by_device(gain_part),
+            fold(key_b_part),
+            fold(value_b_part),
+            fold_wide(output_b_part),
+            fold_wide(down_b_part),
+        ],
+        axis=2,
+    )
+    split = jnp.concatenate(
+        [
+            low(query_part).reshape(count, -1, wide),
+            output_low.reshape(wide, count, deep // count).transpose(1, 0, 2).reshape(count, -1, wide),
+            low(query_b_part).reshape(count, -1, wide),
+            low(output_a_part).reshape(count, -1, wide),
+        ],
+        axis=1,
+    )
+    wide_share = 2 * (rank // count) * (deep // 4) // share
+    units, few, many, shared = end(
+        levels,
+        small,
+        split,
+        SimpleNamespace(
+            gate_weight=gate_up_grad[:, :unit],
+            up_weight=gate_up_grad[:, unit:],
+            down_weight=down_grad_low,
+            gate_expand=gate_b_grad,
+            up_expand=up_b_grad,
+        ),
+        wide_share,
+    )
+    key_own, value_own = few[:, :head], few[:, head : 2 * head]
+    query_a_own, gate_a_own, up_a_own = (
+        few[:, 2 * head + i * rank : 2 * head + (i + 1) * rank] for i in range(3)
+    )
+    place = 2 * head + 3 * rank
+    key_b_own = few[:, place + 64 : place + 96].reshape(-1, head)
+    value_b_own = few[:, place + 96 : place + 128].reshape(-1, head)
+    half = wide_share // 2
+
+    def unfold(array):
+        return array.reshape(4, rank // count, deep // 4).transpose(1, 0, 2).reshape(-1, deep)
+
+    key_a_own = against(low(key_own), key_b)
+    value_a_own = against(low(value_own), value_b)
+    first = query_weight.shape[0]
+    second = first + output_weight.size // wide
+    third = second + query_expand.shape[0]
+    wider = jnp.float32
+    return (
+        result,
+        input_grad,
+        few[:, place],
+        many[:first],
+        key_own,
+        value_own,
+        many[first:second].reshape(output_weight.shape),
+        query_a_own,
+        many[second:third],
+        key_a_own,
+        key_b_own,
+        value_a_own,
+        value_b_own,
+        many[third:].reshape(output_shrink.shape),
+        unfold(shared[:, :, :half]),
+        few[:, place + 1],
+        units.gate_weight.astype(wider),
+        units.up_weight.astype(wider),
+        units.down_weight.astype(wider),
+        gate_a_own,
+        units.gate_expand.astype(wider),
+        up_a_own,
+        units.up_expand.astype(wider),
+        down_shrink_grad,
+        unfold(shared[:, :, half:]),
     )
 
 
@@ -474,6 +1443,9 @@
 
 
 def solution(mesh):
+    levels = mesh.shape["dp"] // 2
+    few = mesh.shape["mp"] == 4 and mesh.shape["dp"] % 2 == 0 and levels <= 4
+    step = functools.partial(by_unit, levels) if few else body
     placed = (
         P(("dp", "mp"), None),
         P(("dp", "mp"), None),
@@ -505,7 +1477,7 @@
         P("dp"),
     )
     return jax.shard_map(
-        body,
+        step,
         mesh=mesh,
         in_specs=placed,
         out_specs=(

time: 4390 us -> 1190 us (0.27)
  waiting for transfers between devices: 3730 us -> 0 us
  Pallas kernels: 0 us -> 840 us
  blocking collectives: 257 us -> 0 us
  matrix products: 318 us -> 202 us
  local copies, waits for them, and re-layouts: 14.5 us -> 78.4 us
    reduce_scatter x25 -> x0, waiting for transfers between devices: 2590 us -> none  [the longest x1 282 us: body(): lax.psum_scatter(up_weight_grad.astype(jnp.bfloat16), 'dp', scatter_dimen...]
    all_gather x21 -> x0, waiting for transfers between devices: 1130 us -> none  [the longest x1 222 us: gather_feed(): lax.all_gather(down_weight, 'dp', axis=1, tiled=True)]
    pallas_call x0 -> x8, Pallas kernels: none -> 840 us  [call(): pl.pallas_call(kernel, out_shape=[jax.ShapeDtypeStruct(shape, kind) for s...]
    all_gather x6 -> x0, blocking collectives: 166 us -> none  [the longest x1 33 us: gather_attention(): lax.all_gather(query_expand, 'dp', axis=0, tiled=True)]
    dot_general x24 -> x5, matrix products: 69.1 us -> 6.76 us  [the longest x1 2.51 us: by_unit(): jnp.einsum('thd,sd->hts', grad_mixed, values, preferred_element_type=jnp....]
    psum x2 -> x0, blocking collectives: 49 us -> none  [project_out(): reduced = lax.psum(matmul(mixed, shrink), 'mp').astype(jnp.bfloat16)]
    dot_general x21 -> x11, matrix products: 103 us -> 55.8 us  [matmul(): return jnp.dot(left, right, preferred_element_type=jnp.float32)]
  transfers between devices with their start and end apart: 46 -> 0, of which waited for: 39 -> 0; matrix products, arithmetic and copies ran while one was open for 7% -> 0% of each run, Pallas kernels for 0% -> 0%
where the time goes in v1:
time: 1190 us; the launch traced here: 1180 us
  Pallas kernels  840 us (71%)
  matrix products  202 us (17%)
  local copies, waits for them, and re-layouts  78.4 us (7%)
  other arithmetic  54.6 us (5%)
    pallas_call x8, Pallas kernels, call(): pl.pallas_call(kernel, out_shape=[jax.ShapeDtypeStruct(shape, kind) for s...  840 us
    dot_general x11, matrix products, against(): lax.dot_general(left, right, (((1,), (1,)), ((), ())), preferred_element_...  73.1 us
    dot_general x11, matrix products, outer_sum(): lax.dot_general(left, right, (((0,), (0,)), ((), ())), preferred_element_...  64.1 us
    dot_general x11, matrix products, matmul(): return jnp.dot(left, right, preferred_element_type=jnp.float32)  55.8 us

profile of v1, /device:TPU:0, one launch (start us, length us, event | category | flops | bytes accessed | tf_op | source)
XLA Modules:
  0.0 1176.9 jit_solution(1126888594868987095)
XLA Ops:
  16.1 258.5 %begin.1 = (bf16[4,128,2048]{2,1,0:T(8,128)(2,1)}, bf16[2048,1920]{1,0:T(8,128)(2,1)}, bf16[256,2048]{1,0:T(8,128)(2,1)}, bf16[256,2048]{1,0:T(8,128)(2,1)}, bf1...) custom-call(bf16[128,2048]{1,0:T(8,128)(2,1)} %refs_0_.1, ...), custom_call_target="tpu_custom_call" | custom-call | tf_op jit(solution)/shard_map/begin/pallas_call | solution.py:489
  283.4 2.8 fusion.16
  303.8 2.6 convolution_convert_fusion.4
  306.4 17.9 %sum_mp.2 = f32[128,2048]{1,0:T(8,128)} custom-call(bf16[4,128,2048]{2,1,0:T(8,128)(2,1)} %bitcast.158), custom_call_target="tpu_custom_call" | custom-call | tf_op jit(solution)/shard_map/sum_mp/pallas_call | solution.py:489
  334.6 78.0 %spread.1 = bf16[32,128,2048]{2,1,0:T(8,128)(2,1)} custom-call(bf16[128,2048]{1,0:T(8,128)(2,1)} %multiply_convert_fusion.5.own), custom_call_target="tpu_custom_call" | custom-call | tf_op jit(solution)/shard_map/spread/pallas_call | solution.py:489
  412.6 24.4 %fusion.117 = f32[4096,1024]{0,1:T(8,128)} fusion(bf16[4096,2048]{1,0:T(8,128)(2,1)} %bitcast.144, bf16[2048,1024]{1,0:T(8,128)(2,1)} %fusion.9), kind=kOutput, calls=%fused_computation.207 | convolution fusion | flops 17179869184 | bytes 37748736 | tf_op jit(solution)/shard_map/dot_general | solution.py:18
  437.0 25.9 %fusion.7 = (bf16[4096,512]{0,1:T(8,128)(2,1)}, bf16[4096,512]{0,1:T(8,128)(2,1)}, bf16[4096,512]{0,1:T(8,128)(2,1)}) fusion(f32[4096,1024]{0,1:T(8,128)} %fusion.117, bf16[4096,2048]{1,0:T(8,128)(2,1)} %bitcast.172, bf16[512,2048]{1,0:T(8,128)(2,1)S(1)} %copy-done.22), kind=kOutput, calls=%fused_computation.11 | convolution fusion | flops 8644460544 | bytes 48234496 | tf_op jit(solution)/shard_map/dot_general | solution.py:22
  462.9 13.9 %convolution_convert_fusion.5.refs_4_ = bf16[512,2048]{1,0:T(8,128)(2,1)S(1)} fusion(bf16[4096,512]{0,1:T(8,128)(2,1)} %get-tuple-element.77, bf16[4096,2048]{1,0:T(8,128)(2,1)} %bitcast.173), kind=kOutput, calls=%fused_computation.36 | convolution fusion | flops 8590983168 | bytes 23068672 | tf_op jit(solution)/shard_map/dot_general | solution.py:28
  480.0 28.2 %multiply_reduce_fusion = (f32[2048]{0:T(1024)S(1)}, bf16[2048,1024]{1,0:T(8,128)(2,1)S(1)}) fusion(bf16[2048,1024]{1,0:T(8,128)(2,1)S(1)} %copy-done.10, f32[2048]{0:T(1024)S(1)} %get-tuple-element.69, bf16[4096,2048]{1,0:T(8,128)(2,1)} %bitcast.145, bf16[4096,512]{0,1:T(8,128)(2,1)} %get-tuple-element.76, bf16[4096,512]{0,1:T(8,128)(2,1)} %get-tuple-element.75), kind=kOutput, calls=%fused_computation.16 | convolution fusion | flops 17207130112 | bytes 33570816 | tf_op jit(solution)/shard_map/dot_general | solution.py:28
  508.2 2.7 convolution_convert_fusion.14.refs_5_
  510.8 2.7 convolution_convert_fusion.13.refs_6_
  523.6 25.7 %convolution_convert_fusion = bf16[4096,2048]{1,0:T(8,128)(2,1)} fusion(bf16[2048,1024]{1,0:T(8,128)(2,1)} %fusion.9, bf16[4096,512]{0,1:T(8,128)(2,1)} %get-tuple-element.76, bf16[4096,512]{0,1:T(8,128)(2,1)} %get-tuple-element.75), kind=kOutput, calls=%fused_computation.1 | convolution fusion | flops 17205035008 | bytes 29360128 | tf_op jit(solution)/shard_map/dot_general | solution.py:22
  549.3 119.2 %collect.3 = f32[128,2048]{1,0:T(8,128)} custom-call(bf16[32,128,2048]{2,1,0:T(8,128)(2,1)} %bitcast.146), custom_call_target="tpu_custom_call" | custom-call | tf_op jit(solution)/shard_map/collect/pallas_call | solution.py:489
  672.6 18.8 %share_mp.1 = bf16[4,128,2048]{2,1,0:T(8,128)(2,1)} custom-call(bf16[128,2048]{1,0:T(8,128)(2,1)} %fusion.104.own), custom_call_target="tpu_custom_call" | custom-call | tf_op jit(solution)/shard_map/share_mp/pallas_call | solution.py:489
  691.4 4.4 convolution_convert_fusion.11
  712.7 3.4 convolution_convert_fusion.7
  716.1 2.6 reshape.460
  723.5 6.3 convolution_convert_fusion.2
  729.8 4.7 multiply_reduce_fusion.1
  734.6 17.2 %sum_mp.3 = f32[128,2048]{1,0:T(8,128)} custom-call(bf16[4,128,2048]{2,1,0:T(8,128)(2,1)} %bitcast.157), custom_call_target="tpu_custom_call" | custom-call | tf_op jit(solution)/shard_map/sum_mp/pallas_call | solution.py:489
  757.2 2.7 convolution_convert_fusion.16
  763.3 3.1 fusion.30
  772.1 3.3 convolution_convert_fusion.10
  778.5 12.0 %concatenate.60.refs_0_ = bf16[32,64,1920]{2,1,0:T(8,128)(2,1)} concatenate(bf16[32,64,256]{2,1,0:T(8,128)(2,1)} %bitcast.152, bf16[32,64,256]{2,1,0:T(8,128)(2,1)} %bitcast.151, bf16[32,64,256]{2,1,0:T(8,128)(2,1)} %bitcast.162, bf16[32,64,256]{2,1,0:T(8,128)(2,1)} %bitcast.161, bf16[32,64,256]{2,1,0:T(8,128)(2,1)} %bitcast.160, bf16[32,64,64]{2,1,0:T(8,128)(2,1)} %bitcast.159, ...), dimensions={2} | concatenate | bytes 15728640 | tf_op jit(solution)/shard_map/concatenate | solution.py:946
  790.5 3.1 copy.211
  793.6 4.2 reshape.466
  797.9 4.0 pad_maximum_fusion.3.refs_1_
  801.9 215.2 %end.1 = (bf16[256,4096]{1,0:T(8,128)(2,1)}, bf16[256,4096]{1,0:T(8,128)(2,1)}, bf16[4096,256]{1,0:T(8,128)(2,1)}, bf16[32,4096]{1,0:T(8,128)(2,1)}, bf16[32,409...) custom-call(bf16[32,64,1920]{2,1,0:T(8,128)(2,1)} %concatenate.60.refs_0_, ...), custom_call_target="tpu_custom_call" | custom-call | tf_op jit(solution)/shard_map/end/pallas_call | solution.py:489
  1034.6 4.1 convert_element_type.264
  1045.6 12.5 %convolution_convert_fusion.1 = bf16[4096,2048]{1,0:T(8,128)(2,1)} fusion(bf16[4096,512]{0,1:T(8,128)(2,1)S(1)} %copy-done.73, bf16[512,2048]{1,0:T(8,128)(2,1)S(1)} %copy-done.23), kind=kOutput, calls=%fused_computation.2 | convolution fusion | flops 8598323200 | bytes 23068672 | tf_op jit(solution)/shard_map/dot_general | solution.py:18
  1058.1 115.1 %collect.2 = f32[128,2048]{1,0:T(8,128)} custom-call(bf16[32,128,2048]{2,1,0:T(8,128)(2,1)} %bitcast.147), custom_call_target="tpu_custom_call" | custom-call | tf_op jit(solution)/shard_map/collect/pallas_call | solution.py:489
  1173.2 3.3 fusion.29
  (253 shorter events, 132.2 us)
Async XLA Ops:
  0.7 300.4 %copy-start = (bf16[512,256]{1,0:T(8,128)(2,1)S(1)}, bf16[512,256]{1,0:T(8,128)(2,1)}, u32[]{:S(2)}) copy-start(bf16[512,256]{1,0:T(8,128)(2,1)} %param.51) | copy-start | bytes 786436
  0.7 290.4 %copy-start.58 = (f32[128]{0:T(128)}, f32[128]{0:T(128)S(1)}, u32[]{:S(2)}) copy-start(f32[128]{0:T(128)S(1)} %multiply_power_fusion) | copy-start | bytes 1540
  3.5 287.7 %copy-start.52 = (f32[512]{0:T(512)}, f32[512]{0:T(512)S(1)}, u32[]{:S(2)}) copy-start(f32[512]{0:T(512)S(1)} %convert_element_type.219) | copy-start | bytes 6148
  8.9 285.4 %copy-start.11 = (f32[512,128]{1,0:T(8,128)}, f32[512,128]{1,0:T(8,128)S(1)}, u32[]{:S(2)}) copy-start(f32[512,128]{1,0:T(8,128)S(1)} %get-tuple-element.115) | copy-start | bytes 786436
  274.7 6.8 copy-start.50
  274.7 6.8 copy-start.62
  278.9 9.7 copy-start.27
  283.4 7.6 copy-start.66
  303.8 20.5 %copy-start.3 = (bf16[128,2048]{1,0:T(8,128)(2,1)S(1)}, bf16[128,2048]{1,0:T(8,128)(2,1)}, u32[]{:S(2)}) copy-start(bf16[128,2048]{1,0:T(8,128)(2,1)} %refs_0_.1) | copy-start | bytes 1572868
  306.4 21.6 %copy-start.48 = (bf16[256,512]{1,0:T(8,128)(2,1)S(1)}, bf16[256,512]{1,0:T(8,128)(2,1)}, u32[]{:S(2)}) copy-start(bf16[256,512]{1,0:T(8,128)(2,1)} %get-tuple-element.56) | copy-start | bytes 786436
  412.6 24.4 %copy-start.22 = (bf16[512,2048]{1,0:T(8,128)(2,1)S(1)}, bf16[512,2048]{1,0:T(8,128)(2,1)}, u32[]{:S(2)}) copy-start(bf16[512,2048]{1,0:T(8,128)(2,1)} %fusion.11) | copy-start | bytes 6291460
  462.9 13.9 %copy-start.36 = (bf16[256,2048]{1,0:T(8,128)(2,1)S(1)}, bf16[256,2048]{1,0:T(8,128)(2,1)}, u32[]{:S(2)}) copy-start(bf16[256,2048]{1,0:T(8,128)(2,1)} %get-tuple-element.59) | copy-start | bytes 3145732
  476.8 43.9 %copy-start.13 = (bf16[512,2048]{1,0:T(8,128)(2,1)}, bf16[512,2048]{1,0:T(8,128)(2,1)S(1)}, u32[]{:S(2)}) copy-start(bf16[512,2048]{1,0:T(8,128)(2,1)S(1)} %convolution_convert_fusion.5.refs_4_) | copy-start | bytes 6291460
  549.3 119.3 %copy-start.2 = (f32[128,2048]{1,0:T(8,128)S(1)}, f32[128,2048]{1,0:T(8,128)}, u32[]{:S(2)}) copy-start(f32[128,2048]{1,0:T(8,128)} %sum_mp.2) | copy-start | bytes 3145732
  549.3 119.3 %copy-start.4 = (bf16[128,2048]{1,0:T(8,128)(2,1)S(1)}, bf16[128,2048]{1,0:T(8,128)(2,1)}, u32[]{:S(2)}) copy-start(bf16[128,2048]{1,0:T(8,128)(2,1)} %refs_0_.1) | copy-start | bytes 1572868
  549.3 119.3 %copy-start.57 = (f32[128]{0:T(128)S(1)}, f32[128]{0:T(128)}, u32[]{:S(2)}) copy-start(f32[128]{0:T(128)} %copy-done.56) | copy-start | bytes 1540
  549.3 120.8 %copy-start.7 = (bf16[128,2048]{1,0:T(8,128)(2,1)S(1)}, bf16[128,2048]{1,0:T(8,128)(2,1)}, u32[]{:S(2)}) copy-start(bf16[128,2048]{1,0:T(8,128)(2,1)} %refs_8_.1) | copy-start | bytes 1572868
  712.7 10.7 copy-start.45
  723.4 6.4 copy-start.28
  723.4 6.4 copy-start.39
  723.4 6.4 copy-start.55
  723.4 6.4 copy-start.67
  723.4 6.4 copy-start.69
  790.5 7.4 copy-start.32
  790.5 7.4 copy-start.44
  801.9 222.6 %copy-start.51 = (bf16[256,1024]{1,0:T(8,128)(2,1)S(1)}, bf16[256,1024]{1,0:T(8,128)(2,1)}, u32[]{:S(2)}) copy-start(bf16[256,1024]{1,0:T(8,128)(2,1)} %get-tuple-element.50) | copy-start | bytes 1572868
  1018.2 13.8 %copy-start.43 = (bf16[32,4096]{1,0:T(8,128)(2,1)S(1)}, bf16[32,4096]{1,0:T(8,128)(2,1)}, u32[]{:S(2)}) copy-start(bf16[32,4096]{1,0:T(8,128)(2,1)} %get-tuple-element.67) | copy-start | bytes 786436
  1023.1 15.6 %copy-start.46 = (f32[64,256]{1,0:T(8,128)}, f32[64,256]{1,0:T(8,128)S(1)}, u32[]{:S(2)}) copy-start(f32[64,256]{1,0:T(8,128)S(1)} %get-tuple-element.109) | copy-start | bytes 196612
  1023.1 15.6 %copy-start.47 = (f32[64,256]{1,0:T(8,128)}, f32[64,256]{1,0:T(8,128)S(1)}, u32[]{:S(2)}) copy-start(f32[64,256]{1,0:T(8,128)S(1)} %get-tuple-element.110) | copy-start | bytes 196612
  1031.3 7.4 copy-start.17
  1058.1 115.1 %copy-start.5 = (f32[128,2048]{1,0:T(8,128)S(1)}, f32[128,2048]{1,0:T(8,128)}, u32[]{:S(2)}) copy-start(f32[128,2048]{1,0:T(8,128)} %collect.3) | copy-start | bytes 3145732
  1058.1 118.4 %copy-start.1 = (bf16[512,256]{1,0:T(8,128)(2,1)S(1)}, bf16[512,256]{1,0:T(8,128)(2,1)}, u32[]{:S(2)}) copy-start(bf16[512,256]{1,0:T(8,128)(2,1)} %param.51) | copy-start | bytes 786436
  (42 other events, 139.2 us)

commit v2 on v1

--- a/solution.py
+++ b/solution.py
@@ -125,6 +125,12 @@
         assert self.local_count <= self.locals.shape[0], self.local_count
         made.start()
         return made
+
+    def take_local(self, number):
+        first = self.local_count
+        self.local_count += number
+        assert self.local_count <= self.locals.shape[0], self.local_count
+        return first
 
     def finish(self):
         for when, wait in self.open:
@@ -290,21 +296,21 @@
     kept.wait()
 
 
-PACE = 6
-
-
-def turn(steps, after=()):
+PACE = 4
+
+
+def turn(steps, after=(), pace=PACE):
     spare = [one for one in after for _ in range(7)]
-    turn_on(steps, spare)
+    turn_on(steps, spare, pace)
     for one in spare:
         next(one)
     turn_on(after)
 
 
-def turn_on(steps, spare=()):
+def turn_on(steps, spare=(), pace=0):
     steps = list(steps)
     while steps:
-        for _ in range(min(PACE, len(spare))):
+        for _ in range(min(pace, len(spare))):
             next(spare.pop(0))
         left = []
         for one in steps:
@@ -358,87 +364,120 @@
     )
 
 
-def scatter_all(w, part, own, core, half_x, half_y, full_x, full_y, below, above, out):
+def planes(w):
+    z, n = w.z, w.levels
+    for k in range(n - 1):
+        falling = n - 1 - k
+        low_half = jnp.where(falling > z, falling, falling - 1)
+        high_half = jnp.where(k < z, k, k + 1)
+        yield jnp.where(z < n // 2, low_half, high_half)
+    yield z
+
+
+def scatter_all(w, part, landing, own, core, half_x, half_y, full_x, full_y, below, above, out, make=None):
     z, y, x, c, n = w.z, w.y, w.x, w.c, w.levels
-    lanes = {name: w.take(n) for name in ("hx", "hy", "fx", "fy")}
-    to_core = w.take(4 * n)
+    to_core, to_hx, to_hy, to_fx, to_fy = (w.take(4 * n), w.take(n), w.take(n), w.take(n), w.take(n))
+    rise, fall = w.take(n), w.take(n)
+    from_part, from_landing = w.take_local(4 * n), w.take_local(4 * n)
     rows = own.shape[1]
     cut = rows // 2 // CHUNK * CHUNK
-    halves = (pl.ds(0, cut), pl.ds(cut, rows - cut))
-
-    def slot(zs, ys, xs):
-        return zs * 4 + ys * 2 + xs
-
+    first, second = pl.ds(0, cut), pl.ds(cut, rows - cut)
     kinds = ((1 - y, 1 - x), (1 - y, x), (y, 1 - x), (y, x))
-    order = [(True, z, True)] if n == 1 else []
-    for step in range(n - 1, 0, -1):
-        order += [side for side in sides(w, step)]
-    order.append((True, z, True))
+    order = list(planes(w))
     kept = {}
-    for kind, (ys, xs) in enumerate(kinds):
-        for place, (_, zs, ok) in enumerate(order):
-            here = slot(zs, ys, xs)
-            w.send(
-                part.at[(zs * 2 + ys) * 4 + xs * 2 + (1 - c)],
-                core.at[here],
-                to_core + here,
-                to_core + here,
-                w.over_core(),
-                ok,
+
+    def start(k):
+        zs = order[k]
+        for kind, (ys, xs) in enumerate(kinds):
+            here = k * 4 + kind
+            lane = to_core + here
+            w.send(part.at[flat(zs, ys, xs, 1 - c)], landing.at[here], lane, lane, w.over_core())
+            kept[here] = pltpu.make_async_copy(
+                part.at[flat(zs, ys, xs, c)], own.at[here], w.locals.at[from_part + here]
             )
-            made = pltpu.make_async_copy(
-                part.at[(zs * 2 + ys) * 4 + xs * 2 + c], own.at[here], w.locals.at[here]
-            )
-            under(ok, made.start)
-            kept[kind, place] = made
-    yield
-    for kind, (ys, xs) in enumerate(kinds):
-        for place, (_, zs, ok) in enumerate(order):
-            here = slot(zs, ys, xs)
-
-            def act():
-                kept[kind, place].wait()
-                w.landed(core.at[here], to_core + here)
-                add_up(own.at[here], own.at[here], core.at[here])
-                if kind == 1:
-                    w.landed(half_x.at[zs], lanes["hx"] + zs)
-                    add_up(own.at[here, halves[0]], own.at[here, halves[0]], half_x.at[zs])
-                if kind == 2:
-                    w.landed(half_y.at[zs], lanes["hy"] + zs)
-                    add_up(own.at[here, halves[1]], own.at[here, halves[1]], half_y.at[zs])
-                if kind == 3:
-                    w.landed(full_x.at[zs], lanes["fx"] + zs)
-                    w.landed(full_y.at[zs], lanes["fy"] + zs)
-                    add_up(own.at[here], own.at[here], full_x.at[zs], full_y.at[zs])
-
-            under(ok, act)
+            kept[here].start()
+
+    def join(k):
+        loads = []
+        for kind in range(4):
+            here = k * 4 + kind
+            w.landed(landing.at[here], to_core + here)
+            load = pltpu.make_async_copy(landing.at[here], core.at[kind], w.locals.at[from_landing + here])
+            load.start()
+            loads.append(load)
+        for kind in range(4):
+            here = k * 4 + kind
+            kept[here].wait()
+            loads[kind].wait()
+            add_up(own.at[here], own.at[here], core.at[kind])
             if kind == 0:
-                for name, half, target, device in (
-                    ("hx", halves[0], half_x, w.over_x()),
-                    ("hy", halves[1], half_y, w.over_y()),
-                ):
-                    lane = lanes[name] + zs
-                    w.send(own.at[here, half], target.at[zs], lane, lane, device, ok)
-            if kind == 1:
-                w.send(own.at[here], full_y.at[zs], lanes["fy"] + zs, lanes["fy"] + zs, w.over_y(), ok)
-            if kind == 2:
-                w.send(own.at[here], full_x.at[zs], lanes["fx"] + zs, lanes["fx"] + zs, w.over_x(), ok)
-        yield
-
-    yield from chain_z(
-        w, lambda zt: own.at[slot(zt, y, x)], lambda zt: below.at[zt], lambda zt: above.at[zt], out
-    )
+                w.send(own.at[here, first], half_x.at[k], to_hx + k, to_hx + k, w.over_x())
+                w.send(own.at[here, second], half_y.at[k], to_hy + k, to_hy + k, w.over_y())
+
+    def across(k):
+        here = k * 4 + 1
+        w.landed(half_x.at[k], to_hx + k)
+        add_up(own.at[here, first], own.at[here, first], half_x.at[k])
+        w.send(own.at[here], full_y.at[k], to_fy + k, to_fy + k, w.over_y())
+        here = k * 4 + 2
+        w.landed(half_y.at[k], to_hy + k)
+        add_up(own.at[here, second], own.at[here, second], half_y.at[k])
+        w.send(own.at[here], full_x.at[k], to_fx + k, to_fx + k, w.over_x())
+
+    def along(k):
+        zs, here = order[k], own.at[k * 4 + 3]
+        w.landed(full_x.at[k], to_fx + k)
+        w.landed(full_y.at[k], to_fy + k)
+        if k == n - 1:
+            add_up(here, here, full_x.at[k], full_y.at[k])
+            return
+        rising, falling = zs > z, zs < z
+        more_up, more_down = jnp.logical_and(rising, z > 0), jnp.logical_and(falling, z < n - 1)
+
+        def take_below():
+            w.landed(below.at[zs], rise + zs)
+            add_up(here, here, full_x.at[k], full_y.at[k], below.at[zs])
+
+        def take_above():
+            w.landed(above.at[zs], fall + zs)
+            add_up(here, here, full_x.at[k], full_y.at[k], above.at[zs])
+
+        under(more_up, take_below)
+        under(more_down, take_above)
+        under(
+            jnp.logical_not(jnp.logical_or(more_up, more_down)),
+            lambda: add_up(here, here, full_x.at[k], full_y.at[k]),
+        )
+        w.send(here, below.at[zs], rise + zs, rise + zs, w.up(), rising)
+        w.send(here, above.at[zs], fall + zs, fall + zs, w.down(), falling)
+
+    for k in range(n + 3):
+        if k < n:
+            if make is not None:
+                yield from make(k, order[k])
+            start(k)
+            yield
+        for lag, act in ((1, join), (2, across), (3, along)):
+            if 0 <= k - lag < n:
+                act(k - lag)
+                yield
+    here = own.at[4 * n - 1]
+    under(z > 0, lambda: w.landed(below.at[z], rise + z))
+    under(z < n - 1, lambda: w.landed(above.at[z], fall + z))
+    under(z == 0, lambda: add_up(out, here, above.at[z]))
+    under(z == n - 1, lambda: add_up(out, here, below.at[z]))
+    under(jnp.logical_and(z > 0, z < n - 1), lambda: add_up(out, here, below.at[z], above.at[z]))
 
 
 def scatter_all_scratch(n, rows, columns):
     cut = rows // 2 // CHUNK * CHUNK
-    shapes = [(4 * n, rows)] * 2 + [(n, cut), (n, rows - cut)] + [(n, rows)] * 4
+    shapes = [(4 * n, rows), (4, rows), (n, cut), (n, rows - cut)] + [(n, rows)] * 4
     return [pltpu.VMEM(shape + (columns,), jnp.bfloat16) for shape in shapes]
 
 
 def scatter_dp(w, part, own, over, below, above, out):
     z, y, n = w.z, w.y, w.levels
-    by_y = w.take(n)
+    by_y, spare = w.take(n), w.take_local(n)
     kept = []
     order = []
     for step in range(n - 1, 0, -1):
@@ -446,7 +485,7 @@
     order.append((True, z, True))
     for _, zs, ok in order:
         w.send(part.at[zs * 2 + 1 - y], over.at[zs], by_y + zs, by_y + zs, w.over_y(), ok)
-        made = pltpu.make_async_copy(part.at[zs * 2 + y], own.at[zs], w.locals.at[4 * n + zs])
+        made = pltpu.make_async_copy(part.at[zs * 2 + y], own.at[zs], w.locals.at[spare + zs])
         under(ok, made.start)
         kept.append(made)
     yield
@@ -622,62 +661,8 @@
     return out
 
 
-def collect(levels, part):
-    _, here, wide = part.shape
-
-    def kernel(given, out, *refs):
-        w = Wires(levels, *refs[-3:])
-        w.greet()
-        turn([scatter_all(w, given, *refs[:-3], out)])
-        w.finish()
-
-    (out,) = call(
-        kernel,
-        2,
-        [part],
-        [((here, wide), jnp.float32, True)],
-        scatter_all_scratch(levels, here, wide),
-        40 * levels,
-        4 * levels,
-        name="collect",
-    )
-    return out
-
-
-def share_mp(levels, rows):
-    def kernel(own, out, *sems):
-        w = Wires(levels, *sems)
-        w.greet(flat=True)
-        turn([gather_mp(w, own, lambda x, c: out.at[x * 2 + c])])
-        w.finish()
-
-    (out,) = call(kernel, 3, [rows], [((4,) + rows.shape, rows.dtype, False)], [], 16, 4, name="share_mp")
-    return out
-
-
-def sum_mp(levels, part):
-    _, here, wide = part.shape
-
-    def kernel(given, out, own, first, second, *sems):
-        w = Wires(levels, *sems)
-        w.greet(flat=True)
-        scatter_mp(w, given, own, first, second, out)
-        w.finish()
-
-    (out,) = call(
-        kernel,
-        4,
-        [part],
-        [((here, wide), jnp.float32, True)],
-        [pltpu.VMEM((2, here, wide), part.dtype)] * 2 + [pltpu.VMEM((here, wide), part.dtype)],
-        16,
-        4,
-        name="sum_mp",
-    )
-    return out
-
-
-def end(levels, small, split, units, share):
+def collect(levels, urgent, other, units):
+    _, here, wide = urgent.shape
     names = list(vars(units))
     count = 2 * levels
     deep, unit = units.gate_weight.shape
@@ -689,32 +674,23 @@
         gate_expand=(low // count, unit * count),
         up_expand=(low // count, unit * count),
     )
-    few, wide = small.shape[1:]
-    many, flatly = split.shape[1:]
-    scratch = scatter_all_scratch(levels, few, wide)
-    scratch += [pltpu.VMEM((levels, many, flatly), jnp.bfloat16)] * 4
-    first = len(names) + 2
-
-    def kernel(*refs):
-        small_ref, split_ref = refs[:2]
-        given = SimpleNamespace(**dict(zip(names, refs[2:])))
-        got = SimpleNamespace(**dict(zip(shapes, refs[first:])))
-        after = first + len(shapes)
-        small_out, split_out, shared = refs[after : after + 3]
-        buffers = refs[after + 3 : -3]
-        w = Wires(levels, *refs[-3:])
-        w.local_count = 5 * levels
+    scratch = scatter_all_scratch(levels, here, wide)
+    each = len(scratch)
+
+    def kernel(urgent_ref, other_ref, *refs):
+        given = SimpleNamespace(**dict(zip(names, refs)))
+        refs = refs[len(names) :]
+        got = SimpleNamespace(**dict(zip(shapes, refs)))
+        urgent_out, other_out, urgent_land, other_land = refs[len(names) : len(names) + 4]
+        buffers = refs[len(names) + 4 :]
+        w = Wires(levels, *buffers[-3:])
         w.greet(far=True)
 
-        def over_all():
-            yield from scatter_all(w, small_ref, *buffers[:8], small_out)
-            mine = small_out.at[:, pl.ds(wide - share, share)]
-            yield from gather_mp(w, mine, lambda x, c: shared.at[x * 2 + c])
-
-        steps = [
-            scatter_dp(w, split_ref, *buffers[8:], split_out),
-            over_all(),
-        ]
+        def later():
+            for _ in range(LAG):
+                yield
+            yield from scatter_all(w, other_ref, other_land, *buffers[each : 2 * each], other_out)
+
         after = [
             exchange_dp(w, lambda dp: rows_of(given.gate_weight, dp, deep // count), lambda dp: columns_of(got.gate_weight, dp, unit)),
             exchange_dp(w, lambda dp: rows_of(given.up_weight, dp, deep // count), lambda dp: columns_of(got.up_weight, dp, unit)),
@@ -722,22 +698,94 @@
             exchange_dp(w, lambda dp: rows_of(given.gate_expand, dp, low // count), lambda dp: columns_of(got.gate_expand, dp, unit)),
             exchange_dp(w, lambda dp: rows_of(given.up_expand, dp, low // count), lambda dp: columns_of(got.up_expand, dp, unit)),
         ]
-        turn(steps, after)
+        turn([scatter_all(w, urgent_ref, urgent_land, *buffers[:each], urgent_out), later()], after, BACK)
         w.finish()
 
     outs = [(shape, jnp.bfloat16, False) for shape in shapes.values()]
-    outs += [((few, wide), jnp.float32, True), ((many, flatly), jnp.float32, True), ((4, few, share), jnp.float32, True)]
+    outs += [((here, wide), jnp.float32, True)] * 2 + [((4 * levels, here, wide), jnp.bfloat16, False)] * 2
+    made = call(
+        kernel,
+        2,
+        [urgent, other] + list(vars(units).values()),
+        outs,
+        scratch * 2,
+        2 * 10 * levels + 5 * 2 * levels + 4,
+        16 * levels + 8,
+        name="collect",
+    )
+    return made[5], made[6], SimpleNamespace(**dict(zip(shapes, made)))
+
+
+LAG, BACK = 3, 2
+
+
+def share_mp(levels, rows):
+    def kernel(own, out, *sems):
+        w = Wires(levels, *sems)
+        w.greet(flat=True)
+        turn([gather_mp(w, own, lambda x, c: out.at[x * 2 + c])])
+        w.finish()
+
+    (out,) = call(kernel, 3, [rows], [((4,) + rows.shape, rows.dtype, False)], [], 16, 4, name="share_mp")
+    return out
+
+
+def sum_mp(levels, part):
+    _, here, wide = part.shape
+
+    def kernel(given, out, own, first, second, *sems):
+        w = Wires(levels, *sems)
+        w.greet(flat=True)
+        scatter_mp(w, given, own, first, second, out)
+        w.finish()
+
+    (out,) = call(
+        kernel,
+        4,
+        [part],
+        [((here, wide), jnp.float32, True)],
+        [pltpu.VMEM((2, here, wide), part.dtype)] * 2 + [pltpu.VMEM((here, wide), part.dtype)],
+        16,
+        4,
+        name="sum_mp",
+    )
+    return out
+
+
+def end(levels, small, split, share):
+    few, wide = small.shape[1:]
+    many, flatly = split.shape[1:]
+    scratch = scatter_all_scratch(levels, few, wide)
+    scratch += [pltpu.VMEM((levels, many, flatly), jnp.bfloat16)] * 4
+
+    def kernel(small_ref, split_ref, small_out, split_out, shared, landing, *buffers):
+        w = Wires(levels, *buffers[-3:])
+        w.greet(far=True)
+
+        def over_all():
+            yield from scatter_all(w, small_ref, landing, *buffers[:8], small_out)
+            mine = small_out.at[:, pl.ds(wide - share, share)]
+            yield from gather_mp(w, mine, lambda x, c: shared.at[x * 2 + c])
+
+        turn([scatter_dp(w, split_ref, *buffers[8:-3], split_out), over_all()])
+        w.finish()
+
     made = call(
         kernel,
         5,
-        [small, split] + list(vars(units).values()),
-        outs,
+        [small, split],
+        [
+            ((few, wide), jnp.float32, True),
+            ((many, flatly), jnp.float32, True),
+            ((4, few, share), jnp.float32, True),
+            ((4 * levels, few, wide), jnp.bfloat16, False),
+        ],
         scratch,
-        64 * levels + 40 * levels,
-        5 * levels + 16,
+        16 * levels,
+        9 * levels + 4,
         name="end",
     )
-    return SimpleNamespace(**dict(zip(shapes, made))), made[-3], made[-2], made[-1]
+    return made[:3]
 
 
 def low(rows):
@@ -882,11 +930,6 @@
     hidden = low(hidden_wide)
     grad_pre = low(jnp.concatenate(pull(against(grads, down_full)), axis=1))
     blocks = (4 * count, rows, deep)
-    branch = collect(levels, low(matmul(hidden, down_full)).reshape(blocks))
-    grad_normed = collect(levels, low(against(grad_pre, gate_up)).reshape(blocks))
-    result = low(middle + branch)
-    grad_middle = output_grad.astype(jnp.float32) + norm_back(grad_normed, normed_middle, scale_middle)
-
     down_grad = outer_sum(hidden, grads)
     gate_up_normed = outer_sum(feed, grad_pre)
     feed_gain = jnp.sum(gate_up_normed * gate_up.astype(jnp.float32), axis=1, keepdims=True) / gain_two
@@ -896,6 +939,20 @@
     down_b_part = outer_sum(down_a, down_grad_low)
     gate_b_grad = low(outer_sum(gate_a, gate_up_grad[:, :unit]))
     up_b_grad = low(outer_sum(up_a, gate_up_grad[:, unit:]))
+    grad_normed, branch, units = collect(
+        levels,
+        low(against(grad_pre, gate_up)).reshape(blocks),
+        low(matmul(hidden, down_full)).reshape(blocks),
+        SimpleNamespace(
+            gate_weight=gate_up_grad[:, :unit],
+            up_weight=gate_up_grad[:, unit:],
+            down_weight=down_grad_low,
+            gate_expand=gate_b_grad,
+            up_expand=up_b_grad,
+        ),
+    )
+    result = low(middle + branch)
+    grad_middle = output_grad.astype(jnp.float32) + norm_back(grad_normed, normed_middle, scale_middle)
     gate_a_part = against(gate_up_grad[:, :unit], got.gate_expand)
     up_a_part = against(gate_up_grad[:, unit:], got.up_expand)
 
@@ -968,19 +1025,7 @@
         axis=1,
     )
     wide_share = 2 * (rank // count) * (deep // 4) // share
-    units, few, many, shared = end(
-        levels,
-        small,
-        split,
-        SimpleNamespace(
-            gate_weight=gate_up_grad[:, :unit],
-            up_weight=gate_up_grad[:, unit:],
-            down_weight=down_grad_low,
-            gate_expand=gate_b_grad,
-            up_expand=up_b_grad,
-        ),
-        wide_share,
-    )
+    few, many, shared = end(levels, small, split, wide_share)
     key_own, value_own = few[:, :head], few[:, head : 2 * head]
     query_a_own, gate_a_own, up_a_own = (
         few[:, 2 * head + i * rank : 2 * head + (i + 1) * rank] for i in range(3)

time: 1190 us -> 1080 us (0.908)
  Pallas kernels: 840 us -> 742 us
  local copies, waits for them, and re-layouts: 78.4 us -> 65.5 us
    pallas_call x8 -> x7, Pallas kernels: 840 us -> 742 us  [call(): pl.pallas_call(kernel, out_shape=[jax.ShapeDtypeStruct(shape, kind) for s...]
where the time goes in v2:
time: 1080 us; the launch traced here: 1060 us
  Pallas kernels  742 us (69%)
  matrix products  203 us (19%)
  local copies, waits for them, and re-layouts  65.5 us (6%)
  other arithmetic  51.5 us (5%)
    pallas_call x7, Pallas kernels, call(): pl.pallas_call(kernel, out_shape=[jax.ShapeDtypeStruct(shape, kind) for s...  742 us
    dot_general x11, matrix products, against(): lax.dot_general(left, right, (((1,), (1,)), ((), ())), preferred_element_...  73.3 us
    dot_general x11, matrix products, outer_sum(): lax.dot_general(left, right, (((0,), (0,)), ((), ())), preferred_element_...  63.3 us
    dot_general x11, matrix products, matmul(): return jnp.dot(left, right, preferred_element_type=jnp.float32)  57.7 us

profile of v2, /device:TPU:0, one launch (start us, length us, event | category | flops | bytes accessed | tf_op | source)
XLA Modules:
  0.0 1064.2 jit_solution(17409282611236496199)
XLA Ops:
  16.1 257.9 %begin.1 = (bf16[4,128,2048]{2,1,0:T(8,128)(2,1)}, bf16[2048,1920]{1,0:T(8,128)(2,1)}, bf16[256,2048]{1,0:T(8,128)(2,1)}, bf16[256,2048]{1,0:T(8,128)(2,1)}, bf1...) custom-call(bf16[128,2048]{1,0:T(8,128)(2,1)} %refs_0_.1, ...), custom_call_target="tpu_custom_call" | custom-call | tf_op jit(solution)/shard_map/begin/pallas_call | solution.py:528
  278.3 2.5 convert_reduce_fusion.1
  282.8 2.8 fusion.16
  303.4 2.6 convolution_convert_fusion.4
  306.0 18.2 %sum_mp.2 = f32[128,2048]{1,0:T(8,128)} custom-call(bf16[4,128,2048]{2,1,0:T(8,128)(2,1)} %bitcast.158), custom_call_target="tpu_custom_call" | custom-call | tf_op jit(solution)/shard_map/sum_mp/pallas_call | solution.py:528
  331.9 2.6 fusion.9
  334.5 78.8 %spread.1 = bf16[32,128,2048]{2,1,0:T(8,128)(2,1)} custom-call(bf16[128,2048]{1,0:T(8,128)(2,1)} %multiply_convert_fusion.5.own), custom_call_target="tpu_custom_call" | custom-call | tf_op jit(solution)/shard_map/spread/pallas_call | solution.py:528
  413.3 24.1 %fusion.117 = f32[4096,1024]{0,1:T(8,128)} fusion(bf16[4096,2048]{1,0:T(8,128)(2,1)} %bitcast.146, bf16[2048,1024]{1,0:T(8,128)(2,1)} %fusion.9), kind=kOutput, calls=%fused_computation.207 | convolution fusion | flops 17179869184 | bytes 37748736 | tf_op jit(solution)/shard_map/dot_general | solution.py:18
  437.4 25.9 %fusion.7 = (bf16[4096,512]{0,1:T(8,128)(2,1)}, bf16[4096,512]{0,1:T(8,128)(2,1)}, bf16[4096,512]{0,1:T(8,128)(2,1)}) fusion(f32[4096,1024]{0,1:T(8,128)} %fusion.117, bf16[4096,2048]{1,0:T(8,128)(2,1)} %bitcast.172, bf16[512,2048]{1,0:T(8,128)(2,1)S(1)} %copy-done.27), kind=kOutput, calls=%fused_computation.11 | convolution fusion | flops 8644460544 | bytes 48234496 | tf_op jit(solution)/shard_map/dot_general | solution.py:22
  463.3 13.9 %convolution_convert_fusion.5.refs_2_ = bf16[512,2048]{1,0:T(8,128)(2,1)S(1)} fusion(bf16[4096,512]{0,1:T(8,128)(2,1)} %get-tuple-element.81, bf16[4096,2048]{1,0:T(8,128)(2,1)} %bitcast.173), kind=kOutput, calls=%fused_computation.36 | convolution fusion | flops 8590983168 | bytes 23068672 | tf_op jit(solution)/shard_map/dot_general | solution.py:28
  480.3 28.6 %multiply_reduce_fusion = (f32[2048]{0:T(1024)S(1)}, bf16[2048,1024]{1,0:T(8,128)(2,1)S(1)}) fusion(bf16[2048,1024]{1,0:T(8,128)(2,1)S(1)} %copy-done.14, f32[2048]{0:T(1024)S(1)} %get-tuple-element.74, bf16[4096,2048]{1,0:T(8,128)(2,1)} %bitcast.147, bf16[4096,512]{0,1:T(8,128)(2,1)} %get-tuple-element.80, bf16[4096,512]{0,1:T(8,128)(2,1)} %get-tuple-element.79), kind=kOutput, calls=%fused_computation.16 | convolution fusion | flops 17207130112 | bytes 33570816 | tf_op jit(solution)/shard_map/dot_general | solution.py:28
  509.0 2.7 convolution_convert_fusion.15.refs_4_
  511.6 2.7 convolution_convert_fusion.16.refs_3_
  525.1 25.4 %convolution_convert_fusion.1 = bf16[4096,2048]{1,0:T(8,128)(2,1)} fusion(bf16[2048,1024]{1,0:T(8,128)(2,1)} %fusion.9, bf16[4096,512]{0,1:T(8,128)(2,1)} %get-tuple-element.80, bf16[4096,512]{0,1:T(8,128)(2,1)} %get-tuple-element.79), kind=kOutput, calls=%fused_computation.2 | convolution fusion | flops 17205035008 | bytes 29360128 | tf_op jit(solution)/shard_map/dot_general | solution.py:22
  550.5 14.8 %convolution_convert_fusion = bf16[4096,2048]{1,0:T(8,128)(2,1)} fusion(bf16[4096,512]{0,1:T(8,128)(2,1)} %get-tuple-element.81, bf16[512,2048]{1,0:T(8,128)(2,1)S(1)} %copy-done.28), kind=kOutput, calls=%fused_computation.1 | convolution fusion | flops 8598323200 | bytes 23068672 | tf_op jit(solution)/shard_map/dot_general | solution.py:18
  565.3 217.9 %collect.1 = (bf16[256,4096]{1,0:T(8,128)(2,1)}, bf16[256,4096]{1,0:T(8,128)(2,1)}, bf16[4096,256]{1,0:T(8,128)(2,1)}, bf16[32,4096]{1,0:T(8,128)(2,1)}, bf16[32...) custom-call(bf16[32,128,2048]{2,1,0:T(8,128)(2,1)} %bitcast.144, ...), custom_call_target="tpu_custom_call" | custom-call | tf_op jit(solution)/shard_map/collect/pallas_call | solution.py:528
  789.0 17.9 %share_mp.1 = bf16[4,128,2048]{2,1,0:T(8,128)(2,1)} custom-call(bf16[128,2048]{1,0:T(8,128)(2,1)} %fusion.104.own), custom_call_target="tpu_custom_call" | custom-call | tf_op jit(solution)/shard_map/share_mp/pallas_call | solution.py:528
  806.8 4.5 convolution_convert_fusion.11
  815.4 2.5 fusion.18
  826.6 2.5 convolution_convert_fusion.7
  833.4 6.3 convolution_convert_fusion.2
  839.7 4.8 multiply_reduce_fusion.1
  844.5 18.2 %sum_mp.3 = f32[128,2048]{1,0:T(8,128)} custom-call(bf16[4,128,2048]{2,1,0:T(8,128)(2,1)} %bitcast.157), custom_call_target="tpu_custom_call" | custom-call | tf_op jit(solution)/shard_map/sum_mp/pallas_call | solution.py:528
  864.4 3.3 fusion.29
  871.2 2.7 convolution_convert_fusion.14
  879.7 3.8 convolution_convert_fusion.10
  886.6 12.1 %concatenate.60.small_ref = bf16[32,64,1920]{2,1,0:T(8,128)(2,1)} concatenate(bf16[32,64,256]{2,1,0:T(8,128)(2,1)} %bitcast.152, bf16[32,64,256]{2,1,0:T(8,128)(2,1)} %bitcast.151, bf16[32,64,256]{2,1,0:T(8,128)(2,1)} %bitcast.162, bf16[32,64,256]{2,1,0:T(8,128)(2,1)} %bitcast.160, bf16[32,64,256]{2,1,0:T(8,128)(2,1)} %bitcast.161, bf16[32,64,64]{2,1,0:T(8,128)(2,1)} %bitcast.159, ...), dimensions={2} | concatenate | bytes 15728640 | tf_op jit(solution)/shard_map/concatenate | solution.py:1003
  900.2 4.2 reshape.466
  904.4 3.6 pad_maximum_fusion.3.split_ref
  908.1 132.9 %end.1 = (f32[64,1920]{1,0:T(8,128)}, f32[576,512]{1,0:T(8,128)}, f32[4,64,512]{2,1,0:T(8,128)}, bf16[16,64,1920]{2,1,0:T(8,128)(2,1)}) custom-call(bf16[32,64,1920]{2,1,0:T(8,128)(2,1)} %concatenate.60.small_ref, bf16[8,576,512]{2,1,0:T(8,128)(2,1)} %pad_maximum_fusion.3.split_ref), custom_call_target="tpu_custom_call" | custom-call | tf_op jit(solution)/shard_map/end/pallas_call | solution.py:528
  1054.8 4.1 convert_element_type.264
  1058.9 2.5 convert_element_type.265
  (262 shorter events, 115.0 us)
Async XLA Ops:
  0.7 300.1 %copy-start = (bf16[512,256]{1,0:T(8,128)(2,1)S(1)}, bf16[512,256]{1,0:T(8,128)(2,1)}, u32[]{:S(2)}) copy-start(bf16[512,256]{1,0:T(8,128)(2,1)} %param.51) | copy-start | bytes 786436
  0.7 289.8 %copy-start.64 = (f32[128]{0:T(128)}, f32[128]{0:T(128)S(1)}, u32[]{:S(2)}) copy-start(f32[128]{0:T(128)S(1)} %multiply_power_fusion) | copy-start | bytes 1540
  3.5 287.0 %copy-start.58 = (f32[512]{0:T(512)}, f32[512]{0:T(512)S(1)}, u32[]{:S(2)}) copy-start(f32[512]{0:T(512)S(1)} %convert_element_type.219) | copy-start | bytes 6148
  8.9 285.1 %copy-start.15 = (f32[512,128]{1,0:T(8,128)}, f32[512,128]{1,0:T(8,128)S(1)}, u32[]{:S(2)}) copy-start(f32[512,128]{1,0:T(8,128)S(1)} %get-tuple-element.119) | copy-start | bytes 786436
  274.0 6.8 copy-start.56
  274.0 6.8 copy-start.68
  278.3 9.8 copy-start.31
  282.8 7.6 copy-start.72
  303.4 20.8 %copy-start.3 = (bf16[128,2048]{1,0:T(8,128)(2,1)S(1)}, bf16[128,2048]{1,0:T(8,128)(2,1)}, u32[]{:S(2)}) copy-start(bf16[128,2048]{1,0:T(8,128)(2,1)} %refs_0_.1) | copy-start | bytes 1572868
  306.0 21.9 %copy-start.55 = (bf16[256,512]{1,0:T(8,128)(2,1)S(1)}, bf16[256,512]{1,0:T(8,128)(2,1)}, u32[]{:S(2)}) copy-start(bf16[256,512]{1,0:T(8,128)(2,1)} %get-tuple-element.61) | copy-start | bytes 786436
  413.3 24.1 %copy-start.27 = (bf16[512,2048]{1,0:T(8,128)(2,1)S(1)}, bf16[512,2048]{1,0:T(8,128)(2,1)}, u32[]{:S(2)}) copy-start(bf16[512,2048]{1,0:T(8,128)(2,1)} %fusion.11) | copy-start | bytes 6291460
  463.3 13.9 %copy-start.41 = (bf16[256,2048]{1,0:T(8,128)(2,1)S(1)}, bf16[256,2048]{1,0:T(8,128)(2,1)}, u32[]{:S(2)}) copy-start(bf16[256,2048]{1,0:T(8,128)(2,1)} %get-tuple-element.58) | copy-start | bytes 3145732
  477.2 44.2 %copy-start.21 = (bf16[512,2048]{1,0:T(8,128)(2,1)}, bf16[512,2048]{1,0:T(8,128)(2,1)S(1)}, u32[]{:S(2)}) copy-start(bf16[512,2048]{1,0:T(8,128)(2,1)S(1)} %convolution_convert_fusion.5.refs_2_) | copy-start | bytes 6291460
  525.1 25.4 %copy-start.28 = (bf16[512,2048]{1,0:T(8,128)(2,1)S(1)}, bf16[512,2048]{1,0:T(8,128)(2,1)}, u32[]{:S(2)}) copy-start(bf16[512,2048]{1,0:T(8,128)(2,1)} %fusion.11) | copy-start | bytes 6291460
  565.3 217.9 %copy-start.2 = (f32[128,2048]{1,0:T(8,128)S(1)}, f32[128,2048]{1,0:T(8,128)}, u32[]{:S(2)}) copy-start(f32[128,2048]{1,0:T(8,128)} %sum_mp.2) | copy-start | bytes 3145732
  565.3 217.9 %copy-start.4 = (bf16[128,2048]{1,0:T(8,128)(2,1)S(1)}, bf16[128,2048]{1,0:T(8,128)(2,1)}, u32[]{:S(2)}) copy-start(bf16[128,2048]{1,0:T(8,128)(2,1)} %refs_0_.1) | copy-start | bytes 1572868
  565.3 218.0 %copy-start.63 = (f32[128]{0:T(128)S(1)}, f32[128]{0:T(128)}, u32[]{:S(2)}) copy-start(f32[128]{0:T(128)} %copy-done.62) | copy-start | bytes 1540
  565.3 219.6 %copy-start.9 = (bf16[128,2048]{1,0:T(8,128)(2,1)S(1)}, bf16[128,2048]{1,0:T(8,128)(2,1)}, u32[]{:S(2)}) copy-start(bf16[128,2048]{1,0:T(8,128)(2,1)} %refs_8_.1) | copy-start | bytes 1572868
  826.6 6.7 copy-start.51
  833.3 6.4 copy-start.32
  833.3 6.4 copy-start.44
  833.3 6.4 copy-start.61
  833.3 6.4 copy-start.73
  833.3 6.4 copy-start.75
  844.5 19.9 %copy-start.5 = (f32[128,2048]{1,0:T(8,128)S(1)}, f32[128,2048]{1,0:T(8,128)}, u32[]{:S(2)}) copy-start(f32[128,2048]{1,0:T(8,128)} %get-tuple-element.64) | copy-start | bytes 3145732
  869.4 6.9 copy-start.13
  886.6 12.1 %copy-start.7 = (bf16[512,2048]{1,0:T(8,128)(2,1)S(1)}, bf16[512,2048]{1,0:T(8,128)(2,1)}, u32[]{:S(2)}) copy-start(bf16[512,2048]{1,0:T(8,128)(2,1)} %copy-done.6) | copy-start | bytes 6291460
  908.0 140.4 %copy-start.57 = (bf16[256,1024]{1,0:T(8,128)(2,1)S(1)}, bf16[256,1024]{1,0:T(8,128)(2,1)}, u32[]{:S(2)}) copy-start(bf16[256,1024]{1,0:T(8,128)(2,1)} %get-tuple-element.52) | copy-start | bytes 1572868
  1040.9 10.7 %copy-start.35 = (f32[576,512]{1,0:T(8,128)S(1)}, f32[576,512]{1,0:T(8,128)}, u32[]{:S(2)}) copy-start(f32[576,512]{1,0:T(8,128)} %get-tuple-element.66) | copy-start | bytes 3538948
  1047.1 11.8 %copy-start.52 = (f32[64,256]{1,0:T(8,128)}, f32[64,256]{1,0:T(8,128)S(1)}, u32[]{:S(2)}) copy-start(f32[64,256]{1,0:T(8,128)S(1)} %get-tuple-element.113) | copy-start | bytes 196612
  1047.1 11.8 %copy-start.53 = (f32[64,256]{1,0:T(8,128)}, f32[64,256]{1,0:T(8,128)S(1)}, u32[]{:S(2)}) copy-start(f32[64,256]{1,0:T(8,128)S(1)} %get-tuple-element.114) | copy-start | bytes 196612
  1052.5 6.4 copy-start.18
  (47 other events, 166.7 us)

commit v3 on v2

--- a/solution.py
+++ b/solution.py
@@ -1,4 +1,5 @@
 import functools
+import math
 from types import SimpleNamespace
 
 import jax
@@ -435,8 +436,8 @@
         more_up, more_down = jnp.logical_and(rising, z > 0), jnp.logical_and(falling, z < n - 1)
 
         def take_below():
-            w.landed(below.at[zs], rise + zs)
-            add_up(here, here, full_x.at[k], full_y.at[k], below.at[zs])
+            w.landed(below.at[zs - 1], rise + zs)
+            add_up(here, here, full_x.at[k], full_y.at[k], below.at[zs - 1])
 
         def take_above():
             w.landed(above.at[zs], fall + zs)
@@ -448,13 +449,13 @@
             jnp.logical_not(jnp.logical_or(more_up, more_down)),
             lambda: add_up(here, here, full_x.at[k], full_y.at[k]),
         )
-        w.send(here, below.at[zs], rise + zs, rise + zs, w.up(), rising)
+        w.send(here, below.at[zs - 1], rise + zs, rise + zs, w.up(), rising)
         w.send(here, above.at[zs], fall + zs, fall + zs, w.down(), falling)
 
     for k in range(n + 3):
+        if make is not None:
+            yield from make(k)
         if k < n:
-            if make is not None:
-                yield from make(k, order[k])
             start(k)
             yield
         for lag, act in ((1, join), (2, across), (3, along)):
@@ -462,16 +463,16 @@
                 act(k - lag)
                 yield
     here = own.at[4 * n - 1]
-    under(z > 0, lambda: w.landed(below.at[z], rise + z))
+    under(z > 0, lambda: w.landed(below.at[z - 1], rise + z))
     under(z < n - 1, lambda: w.landed(above.at[z], fall + z))
     under(z == 0, lambda: add_up(out, here, above.at[z]))
-    under(z == n - 1, lambda: add_up(out, here, below.at[z]))
-    under(jnp.logical_and(z > 0, z < n - 1), lambda: add_up(out, here, below.at[z], above.at[z]))
+    under(z == n - 1, lambda: add_up(out, here, below.at[z - 1]))
+    under(jnp.logical_and(z > 0, z < n - 1), lambda: add_up(out, here, below.at[z - 1], above.at[z]))
 
 
 def scatter_all_scratch(n, rows, columns):
     cut = rows // 2 // CHUNK * CHUNK
-    shapes = [(4 * n, rows), (4, rows), (n, cut), (n, rows - cut)] + [(n, rows)] * 4
+    shapes = [(4 * n, rows), (4, rows), (n, cut), (n, rows - cut)] + [(n, rows)] * 2 + [(n - 1, rows)] * 2
     return [pltpu.VMEM(shape + (columns,), jnp.bfloat16) for shape in shapes]
 
 
@@ -520,6 +521,7 @@
     add_up(out, own.at[1], first.at[1], second)
 
 
+VMEM = 62 * MIB
 ANY = pl.BlockSpec(memory_space=pl.ANY)
 WHOLE = pl.BlockSpec(memory_space=pltpu.VMEM)
 
@@ -537,7 +539,7 @@
             pltpu.SemaphoreType.DMA((max(locals_, 1),)),
         ],
         compiler_params=pltpu.CompilerParams(
-            collective_id=identity, has_side_effects=True, vmem_limit_bytes=60 * MIB
+            collective_id=identity, has_side_effects=True, vmem_limit_bytes=VMEM
         ),
         name=name,
     )(*arrays)
@@ -661,62 +663,272 @@
     return out
 
 
-def collect(levels, urgent, other, units):
-    _, here, wide = urgent.shape
-    names = list(vars(units))
+def gelu_pair(gate):
+    inner = GELU * (gate + 0.044715 * gate * gate * gate)
+    bend = jnp.tanh(inner)
+    slope = GELU * (1.0 + 3.0 * 0.044715 * gate * gate)
+    return 0.5 * gate * (1.0 + bend), 0.5 * (1.0 + bend) + 0.5 * gate * (1.0 - bend * bend) * slope
+
+
+GELU = (2.0 / math.pi) ** 0.5
+TALL = 256
+
+
+def feed(levels, rows, tokens, grads, gate_up, down):
+    deep, both = gate_up.shape
+    unit = both // 2
+    total = tokens.shape[0]
+    level = total // levels
     count = 2 * levels
-    deep, unit = units.gate_weight.shape
-    low = units.gate_expand.shape[0]
-    shapes = dict(
-        gate_weight=(deep // count, unit * count),
-        up_weight=(deep // count, unit * count),
-        down_weight=(unit * count, deep // count),
-        gate_expand=(low // count, unit * count),
-        up_expand=(low // count, unit * count),
-    )
-    scratch = scatter_all_scratch(levels, here, wide)
+    strip = deep // count
+    half = total // 2
+    steps = level // TALL
+    kind = jnp.bfloat16
+    scratch = scatter_all_scratch(levels, rows, deep)
     each = len(scratch)
 
-    def kernel(urgent_ref, other_ref, *refs):
-        given = SimpleNamespace(**dict(zip(names, refs)))
-        refs = refs[len(names) :]
-        got = SimpleNamespace(**dict(zip(shapes, refs)))
-        urgent_out, other_out, urgent_land, other_land = refs[len(names) : len(names) + 4]
-        buffers = refs[len(names) + 4 :]
+    def kernel(tokens_ref, grads_ref, gate_up_hbm, down_hbm, *refs):
+        grad_out, branch_out, pair_hbm, single_hbm, gate_own, up_own, down_own = refs[:7]
+        hidden_hbm, pre_hbm, grad_part, branch_part, grad_land, branch_land = refs[7:13]
+        buffers = refs[13:]
+        one, two = buffers[:each], buffers[each : 2 * each - 1]
+        two = two[:1] + (one[1],) + two[1:]
+        gate_up_ref, down_ref, arena, hidden_stage, pre_stage, columns, down_stage, loads, stores = buffers[
+            2 * each - 1 : -3
+        ]
+
+        def space(number, slot):
+            return arena.at[pl.ds(pl.multiple_of((2 * number + slot) * TALL, TALL), TALL)]
+
         w = Wires(levels, *buffers[-3:])
+        weights = [w.local(gate_up_hbm, gate_up_ref), w.local(down_hbm, down_ref)]
+        order = list(planes(w))
+
+        def load(k, j, slot):
+            start = pl.ds(pl.multiple_of(order[k] * level + j * TALL, TALL), TALL)
+            return (
+                pltpu.make_async_copy(tokens_ref.at[start], space(0, slot), loads.at[0, slot]),
+                pltpu.make_async_copy(grads_ref.at[start], space(1, slot), loads.at[1, slot]),
+            )
+
+        def store(k, j, slot):
+            start = pl.multiple_of(order[k] * level + j * TALL, TALL)
+            block = order[k] * (level // rows) + j * (TALL // rows)
+            made = [
+                pltpu.make_async_copy(hidden_stage.at[slot], hidden_hbm.at[pl.ds(start, TALL)], stores.at[0, slot]),
+                pltpu.make_async_copy(pre_stage.at[slot], pre_hbm.at[pl.ds(start, TALL)], stores.at[1, slot]),
+            ]
+            for i in range(TALL // rows):
+                piece = pl.ds(i * rows, rows)
+                made += [
+                    pltpu.make_async_copy(space(2, slot).at[piece], grad_part.at[block + i], stores.at[2 + 2 * i, slot]),
+                    pltpu.make_async_copy(space(3, slot).at[piece], branch_part.at[block + i], stores.at[3 + 2 * i, slot]),
+                ]
+            return made
+
+        for copy in load(0, 0, 0):
+            copy.start()
         w.greet(far=True)
-
-        def later():
-            for _ in range(LAG):
+        for copy in weights:
+            copy.wait()
+
+        lanes = w.take(3 * count)
+
+        def there(i):
+            return lax.rem(w.dp + 1 + i, count)
+
+        def strip_of(ref, i):
+            return columns_of(ref, there(i), strip)
+
+        def strip_load(ref, i):
+            slot = lax.rem(i, 2)
+            return pltpu.make_async_copy(strip_of(ref, i), columns.at[slot], loads.at[0, slot])
+
+        def pair_store(i):
+            slot = lax.rem(i, 2)
+            return pltpu.make_async_copy(pre_stage.at[slot], rows_of(pair_hbm, there(i), strip), stores.at[0, slot])
+
+        def single_store(i):
+            slot = lax.rem(i, 2)
+            return pltpu.make_async_copy(down_stage.at[slot], strip_of(single_hbm, i), stores.at[1, slot])
+
+        def pair_pieces(i):
+            both_rows = rows_of(pair_hbm, there(i), strip)
+            yield both_rows.at[:, pl.ds(0, unit)], columns_of(gate_own, w.dp, unit), lanes + i
+            yield both_rows.at[:, pl.ds(unit, unit)], columns_of(up_own, w.dp, unit), lanes + count + i
+
+        def single_pieces(i):
+            yield strip_of(single_hbm, i), rows_of(down_own, w.dp, unit), lanes + 2 * count + i
+
+        def give(pieces, i):
+            for source, target, lane in pieces(i):
+                w.copy(source, target, lane, lane, (there(i), w.mp)).start()
+
+        def keep(pieces):
+            for source, target, _ in pieces(count - 1):
+                w.local(source, target).wait()
+
+        def product(left, right, left_wide, right_wide):
+            return sum(
+                lax.dot_general(
+                    left[pl.ds(0, half), pl.ds(i * left_wide[0], left_wide[1])] if left_wide[0] else left[pl.ds(i * half, half), :],
+                    right[pl.ds(0, half), pl.ds(i * right_wide[0], right_wide[1])] if right_wide[0] else right[pl.ds(i * half, half), :],
+                    (((0,), (0,)), ((), ())),
+                    preferred_element_type=jnp.float32,
+                )
+                for i in range(2)
+            )
+
+        def pair_strip(i, carry):
+            slot = lax.rem(i, 2)
+            strip_load(tokens_ref, i).wait()
+
+            @pl.when(i < count - 1)
+            def _():
+                strip_load(tokens_ref, i + 1).start()
+
+            @pl.when(i == count - 1)
+            def _():
+                strip_load(grads_ref, count - 1 - i).start()
+
+            pre_stage[slot] = product(columns.at[slot], arena, (0, 0), (both, both)).astype(kind)
+            pair_store(i).start()
+
+            @pl.when(i > 0)
+            def _():
+                pair_store(i - 1).wait()
+                give(pair_pieces, i - 1)
+
+            return carry
+
+        def single_strip(i, carry):
+            slot = lax.rem(i, 2)
+            strip_load(grads_ref, i).wait()
+
+            @pl.when(i < count - 1)
+            def _():
+                strip_load(grads_ref, i + 1).start()
+
+            down_stage[slot] = product(gate_up_ref, columns.at[slot], (unit, unit), (0, 0)).astype(kind)
+            single_store(i).start()
+
+            @pl.when(i > 0)
+            def _():
+                single_store(i - 1).wait()
+                give(single_pieces, i - 1)
+
+            return carry
+
+        def gradients(k):
+            if k == levels:
+                held = []
+                for i in range(2):
+                    piece = pl.ds(i * half, half)
+                    held.append(w.local(pre_hbm.at[piece], arena.at[:, pl.ds(i * both, both)]))
+                    held.append(w.local(hidden_hbm.at[piece], gate_up_ref.at[:, pl.ds(i * unit, unit)]))
+                strip_load(tokens_ref, 0).start()
+                for copy in held:
+                    copy.wait()
+                lax.fori_loop(0, count // 2, pair_strip, 0)
+            if k == levels + 1:
+                lax.fori_loop(count // 2, count, pair_strip, 0)
+                pair_store(count - 1).wait()
+                keep(pair_pieces)
+            if k == levels + 2:
+                lax.fori_loop(0, count, single_strip, 0)
+                single_store(count - 1).wait()
+                keep(single_pieces)
+
+        def make(k):
+            if k >= levels:
+                gradients(k)
                 yield
-            yield from scatter_all(w, other_ref, other_land, *buffers[each : 2 * each], other_out)
-
-        after = [
-            exchange_dp(w, lambda dp: rows_of(given.gate_weight, dp, deep // count), lambda dp: columns_of(got.gate_weight, dp, unit)),
-            exchange_dp(w, lambda dp: rows_of(given.up_weight, dp, deep // count), lambda dp: columns_of(got.up_weight, dp, unit)),
-            exchange_dp(w, lambda dp: columns_of(given.down_weight, dp, deep // count), lambda dp: rows_of(got.down_weight, dp, unit)),
-            exchange_dp(w, lambda dp: rows_of(given.gate_expand, dp, low // count), lambda dp: columns_of(got.gate_expand, dp, unit)),
-            exchange_dp(w, lambda dp: rows_of(given.up_expand, dp, low // count), lambda dp: columns_of(got.up_expand, dp, unit)),
-        ]
-        turn([scatter_all(w, urgent_ref, urgent_land, *buffers[:each], urgent_out), later()], after, BACK)
+                return
+
+            def chunk(j, carry):
+                slot = lax.rem(j, 2)
+                for copy in load(k, j, slot):
+                    copy.wait()
+
+                @pl.when(j < steps - 1)
+                def _():
+                    for copy in load(k, j + 1, 1 - slot):
+                        copy.start()
+
+                if k < levels - 1:
+
+                    @pl.when(j == steps - 1)
+                    def _():
+                        for copy in load(k + 1, 0, 0):
+                            copy.start()
+
+                @pl.when(j >= 2)
+                def _():
+                    for copy in store(k, j - 2, slot):
+                        copy.wait()
+
+                pre = jnp.dot(space(0, slot)[...], gate_up_ref[...], preferred_element_type=jnp.float32)
+                back = against(space(1, slot)[...], down_ref[...])
+                gate, up = pre[:, :unit], pre[:, unit:]
+                bent, slope = gelu_pair(gate)
+                hidden = (bent * up).astype(kind)
+                grad_pre = jnp.concatenate([back * up * slope, back * bent], axis=1).astype(kind)
+                hidden_stage[slot] = hidden
+                pre_stage[slot] = grad_pre
+                space(2, slot)[...] = against(grad_pre, gate_up_ref[...]).astype(kind)
+                space(3, slot)[...] = jnp.dot(hidden, down_ref[...], preferred_element_type=jnp.float32).astype(kind)
+                for copy in store(k, j, slot):
+                    copy.start()
+                return carry
+
+            lax.fori_loop(0, steps, chunk, 0)
+            for j in range(max(steps - 2, 0), steps):
+                for copy in store(k, j, j % 2):
+                    copy.wait()
+            yield
+
+        def idle(k):
+            yield
+
+        turn(
+            [
+                scatter_all(w, grad_part, grad_land, *one, grad_out, make=make),
+                scatter_all(w, branch_part, branch_land, *two, branch_out, make=idle),
+            ]
+        )
+        for i in range(count - 1):
+            source = lax.rem(w.dp + count - 1 - i, count)
+            for sent, (_, _, lane) in zip(
+                (columns_of(gate_own, source, unit), columns_of(up_own, source, unit), rows_of(down_own, source, unit)),
+                (*pair_pieces(i), *single_pieces(i)),
+            ):
+                w.landed(sent, lane)
+                w.copy(sent, sent, lane, lane, w.over_x()).wait_send()
         w.finish()
 
-    outs = [(shape, jnp.bfloat16, False) for shape in shapes.values()]
-    outs += [((here, wide), jnp.float32, True)] * 2 + [((4 * levels, here, wide), jnp.bfloat16, False)] * 2
+    assert total == 2 * deep and 2 * both == deep and 8 * TALL == deep and strip == TALL
+    tall = [(deep, deep), (2, TALL, unit), (2, TALL, both), (2, total, strip), (2, unit, strip)]
+    outs = [((rows, deep), jnp.float32, True)] * 2
+    outs += [((deep, both), kind, False), ((unit, deep), kind, False)]
+    outs += [((strip, unit * count), kind, False)] * 2 + [((unit * count, strip), kind, False)]
+    outs += [((total, unit), kind, False), ((total, both), kind, False)]
+    outs += [((total // rows, rows, deep), kind, False)] * 2 + [((4 * levels, rows, deep), kind, False)] * 2
     made = call(
         kernel,
         2,
-        [urgent, other] + list(vars(units).values()),
+        [tokens, grads, gate_up, down],
         outs,
-        scratch * 2,
-        2 * 10 * levels + 5 * 2 * levels + 4,
-        16 * levels + 8,
-        name="collect",
-    )
-    return made[5], made[6], SimpleNamespace(**dict(zip(shapes, made)))
-
-
-LAG, BACK = 3, 2
+        scratch
+        + scratch[:1]
+        + scratch[2:]
+        + [pltpu.VMEM(gate_up.shape, kind), pltpu.VMEM(down.shape, kind)]
+        + [pltpu.VMEM(shape, kind) for shape in tall]
+        + [pltpu.SemaphoreType.DMA((2, 2)), pltpu.SemaphoreType.DMA((2 + 2 * (TALL // rows), 2))],
+        2 * 10 * levels + 6 * levels + 4,
+        16 * levels + 12,
+        name="feed",
+    )
+    return made[:7]
 
 
 def share_mp(levels, rows):
@@ -752,14 +964,31 @@
     return out
 
 
-def end(levels, small, split, share):
+BACK = 4
+
+
+def end(levels, small, split, units, share):
+    names = list(vars(units))
+    count = 2 * levels
+    low, unit = units.gate_expand.shape
+    shapes = dict(
+        gate_expand=(low // count, unit * count),
+        up_expand=(low // count, unit * count),
+    )
     few, wide = small.shape[1:]
     many, flatly = split.shape[1:]
     scratch = scatter_all_scratch(levels, few, wide)
     scratch += [pltpu.VMEM((levels, many, flatly), jnp.bfloat16)] * 4
-
-    def kernel(small_ref, split_ref, small_out, split_out, shared, landing, *buffers):
-        w = Wires(levels, *buffers[-3:])
+    first = len(names) + 2
+
+    def kernel(*refs):
+        small_ref, split_ref = refs[:2]
+        given = SimpleNamespace(**dict(zip(names, refs[2:])))
+        got = SimpleNamespace(**dict(zip(shapes, refs[first:])))
+        after = first + len(shapes)
+        small_out, split_out, shared, landing = refs[after : after + 4]
+        buffers = refs[after + 4 : -3]
+        w = Wires(levels, *refs[-3:])
         w.greet(far=True)
 
         def over_all():
@@ -767,25 +996,30 @@
             mine = small_out.at[:, pl.ds(wide - share, share)]
             yield from gather_mp(w, mine, lambda x, c: shared.at[x * 2 + c])
 
-        turn([scatter_dp(w, split_ref, *buffers[8:-3], split_out), over_all()])
+        steps = [
+            scatter_dp(w, split_ref, *buffers[8:], split_out),
+            over_all(),
+        ]
+        after = [
+            exchange_dp(w, lambda dp: rows_of(given.gate_expand, dp, low // count), lambda dp: columns_of(got.gate_expand, dp, unit)),
+            exchange_dp(w, lambda dp: rows_of(given.up_expand, dp, low // count), lambda dp: columns_of(got.up_expand, dp, unit)),
+        ]
+        turn(steps, after, BACK)
         w.finish()
 
+    outs = [(shape, jnp.bfloat16, False) for shape in shapes.values()]
+    outs += [((few, wide), jnp.float32, True), ((many, flatly), jnp.float32, True), ((4, few, share), jnp.float32, True), ((4 * levels, few, wide), jnp.bfloat16, False)]
     made = call(
         kernel,
         5,
-        [small, split],
-        [
-            ((few, wide), jnp.float32, True),
-            ((many, flatly), jnp.float32, True),
-            ((4, few, share), jnp.float32, True),
-            ((4 * levels, few, wide), jnp.bfloat16, False),
-        ],
+        [small, split] + list(vars(units).values()),
+        outs,
         scratch,
-        16 * levels,
-        9 * levels + 4,
+        32 * levels,
+        9 * levels + 16,
         name="end",
     )
-    return made[:3]
+    return SimpleNamespace(**dict(zip(shapes, made))), made[-4], made[-3], made[-2]
 
 
 def low(rows):
@@ -921,40 +1155,21 @@
     down_a, down_b = down_shrink, got.down_expand
     down_full = low(got.down_weight.astype(jnp.float32) + matmul(down_a, down_b))
     normed_middle, scale_middle = unit_rows(middle)
-    feed = spread(levels, low(normed_middle)).reshape(4 * count * rows, deep)
+    normed_all = spread(levels, low(normed_middle)).reshape(4 * count * rows, deep)
     grads = got.output_grad.reshape(4 * count * rows, deep)
-    pre = matmul(feed, gate_up)
-    hidden_wide, pull = jax.vjp(
-        lambda gate, up: jax.nn.gelu(gate, approximate=True) * up, pre[:, :unit], pre[:, unit:]
-    )
-    hidden = low(hidden_wide)
-    grad_pre = low(jnp.concatenate(pull(against(grads, down_full)), axis=1))
-    blocks = (4 * count, rows, deep)
-    down_grad = outer_sum(hidden, grads)
-    gate_up_normed = outer_sum(feed, grad_pre)
-    feed_gain = jnp.sum(gate_up_normed * gate_up.astype(jnp.float32), axis=1, keepdims=True) / gain_two
-    gate_up_grad = low(gate_up_normed * gain_two)
-    down_grad_low = low(down_grad)
+    grad_normed, branch, pair_grad, down_grad_low, gate_own, up_own, down_own = feed(levels, rows, normed_all, grads, gate_up, down_full)
+    result = low(middle + branch)
+    grad_middle = output_grad.astype(jnp.float32) + norm_back(grad_normed, normed_middle, scale_middle)
+
+    feed_gain = (
+        jnp.sum(pair_grad.astype(jnp.float32) * gate_up.astype(jnp.float32), axis=1, keepdims=True) / gain_two
+    )
     down_shrink_grad = against(down_grad_low, down_b)
     down_b_part = outer_sum(down_a, down_grad_low)
-    gate_b_grad = low(outer_sum(gate_a, gate_up_grad[:, :unit]))
-    up_b_grad = low(outer_sum(up_a, gate_up_grad[:, unit:]))
-    grad_normed, branch, units = collect(
-        levels,
-        low(against(grad_pre, gate_up)).reshape(blocks),
-        low(matmul(hidden, down_full)).reshape(blocks),
-        SimpleNamespace(
-            gate_weight=gate_up_grad[:, :unit],
-            up_weight=gate_up_grad[:, unit:],
-            down_weight=down_grad_low,
-            gate_expand=gate_b_grad,
-            up_expand=up_b_grad,
-        ),
-    )
-    result = low(middle + branch)
-    grad_middle = output_grad.astype(jnp.float32) + norm_back(grad_normed, normed_middle, scale_middle)
-    gate_a_part = against(gate_up_grad[:, :unit], got.gate_expand)
-    up_a_part = against(gate_up_grad[:, unit:], got.up_expand)
+    gate_b_grad = low(outer_sum(low(gain_two * gate_a.astype(jnp.float32)), pair_grad[:, :unit]))
+    up_b_grad = low(outer_sum(low(gain_two * up_a.astype(jnp.float32)), pair_grad[:, unit:]))
+    gate_a_part = gain_two * against(pair_grad[:, :unit], got.gate_expand)
+    up_a_part = gain_two * against(pair_grad[:, unit:], got.up_expand)
 
     grad_branch = share_mp(levels, low(grad_middle)).reshape(tokens, deep)
     output_grad_w = outer_sum(mixed, grad_branch)
@@ -1025,7 +1240,16 @@
         axis=1,
     )
     wide_share = 2 * (rank // count) * (deep // 4) // share
-    few, many, shared = end(levels, small, split, wide_share)
+    units, few, many, shared = end(
+        levels,
+        small,
+        split,
+        SimpleNamespace(
+            gate_expand=gate_b_grad,
+            up_expand=up_b_grad,
+        ),
+        wide_share,
+    )
     key_own, value_own = few[:, :head], few[:, head : 2 * head]
     query_a_own, gate_a_own, up_a_own = (
         few[:, 2 * head + i * rank : 2 * head + (i + 1) * rank] for i in range(3)
@@ -1044,6 +1268,7 @@
     second = first + output_weight.size // wide
     third = second + query_expand.shape[0]
     wider = jnp.float32
+    own_gain = feedforward_gain.astype(wider)[:, None]
     return (
         result,
         input_grad,
@@ -1061,9 +1286,9 @@
         many[third:].reshape(output_shrink.shape),
         unfold(shared[:, :, :half]),
         few[:, place + 1],
-        units.gate_weight.astype(wider),
-        units.up_weight.astype(wider),
-        units.down_weight.astype(wider),
+        own_gain * gate_own.astype(wider),
+        own_gain * up_own.astype(wider),
+        down_own.astype(wider),
         gate_a_own,
         units.gate_expand.astype(wider),
         up_a_own,

time: 1080 us -> 1030 us (0.954)
  matrix products: 203 us -> 73.2 us
  Pallas kernels: 742 us -> 815 us
  local copies, waits for them, and re-layouts: 65.5 us -> 82.3 us
    pallas_call x7, Pallas kernels: 742 us -> 815 us  [call(): pl.pallas_call(kernel, out_shape=[jax.ShapeDtypeStruct(shape, kind) for s...]
    dot_general x11 -> x9, matrix products: 73.3 us -> 21.7 us  [against(): lax.dot_general(left, right, (((1,), (1,)), ((), ())), preferred_element_...]
    dot_general x11 -> x9, matrix products: 63.3 us -> 21.1 us  [outer_sum(): lax.dot_general(left, right, (((0,), (0,)), ((), ())), preferred_element_...]
    dot_general x11 -> x9, matrix products: 57.7 us -> 19.8 us  [matmul(): return jnp.dot(left, right, preferred_element_type=jnp.float32)]
where the time goes in v3:
time: 1030 us; the launch traced here: 1020 us
  Pallas kernels  815 us (79%)
  local copies, waits for them, and re-layouts  82.3 us (8%)
  matrix products  73.2 us (7%)
  other arithmetic  45.7 us (4%)
    pallas_call x7, Pallas kernels, call(): pl.pallas_call(kernel, out_shape=[jax.ShapeDtypeStruct(shape, kind) for s...  815 us
    dot_general x9, matrix products, against(): lax.dot_general(left, right, (((1,), (1,)), ((), ())), preferred_element_...  21.7 us
    dot_general x9, matrix products, outer_sum(): lax.dot_general(left, right, (((0,), (0,)), ((), ())), preferred_element_...  21.1 us

profile of v3, /device:TPU:0, one launch (start us, length us, event | category | flops | bytes accessed | tf_op | source)
XLA Modules:
  0.0 1018.0 jit_solution(1897232135068510771)
XLA Ops:
  10.1 257.9 %begin.1 = (bf16[4,128,2048]{2,1,0:T(8,128)(2,1)}, bf16[2048,1920]{1,0:T(8,128)(2,1)}, bf16[256,2048]{1,0:T(8,128)(2,1)}, bf16[256,2048]{1,0:T(8,128)(2,1)}, bf1...) custom-call(bf16[128,2048]{1,0:T(8,128)(2,1)} %refs_0_.1, ...), custom_call_target="tpu_custom_call" | custom-call | tf_op jit(solution)/shard_map/begin/pallas_call | solution.py:530
  269.7 2.8 multiply_convert_fusion.1
  272.5 2.8 fusion.7
  275.3 2.4 fusion.8
  291.4 2.4 convolution_convert_fusion.7
  294.9 2.6 convolution_convert_fusion.2
  297.5 18.2 %sum_mp.2 = f32[128,2048]{1,0:T(8,128)} custom-call(bf16[4,128,2048]{2,1,0:T(8,128)(2,1)} %bitcast.144), custom_call_target="tpu_custom_call" | custom-call | tf_op jit(solution)/shard_map/sum_mp/pallas_call | solution.py:530
  318.2 78.8 %spread.1 = bf16[32,128,2048]{2,1,0:T(8,128)(2,1)} custom-call(bf16[128,2048]{1,0:T(8,128)(2,1)} %multiply_convert_fusion.6.own), custom_call_target="tpu_custom_call" | custom-call | tf_op jit(solution)/shard_map/spread/pallas_call | solution.py:530
  401.5 2.8 fusion.2.gate_up_hbm
  406.3 265.7 %feed.1 = (f32[128,2048]{1,0:T(8,128)}, f32[128,2048]{1,0:T(8,128)}, bf16[2048,1024]{1,0:T(8,128)(2,1)}, bf16[512,2048]{1,0:T(8,128)(2,1)}, bf16[256,4096]{1,0:T...) custom-call(bf16[4096,2048]{1,0:T(8,128)(2,1)} %bitcast.132, ...), custom_call_target="tpu_custom_call" | custom-call | tf_op jit(solution)/shard_map/feed/pallas_call | solution.py:530
  672.1 7.0 convert_multiply_fusion
  679.1 3.3 fusion.28.refs_3_
  682.4 3.5 fusion.25.refs_2_
  688.1 17.6 %share_mp.1 = bf16[4,128,2048]{2,1,0:T(8,128)(2,1)} custom-call(bf16[128,2048]{1,0:T(8,128)(2,1)} %fusion.106.own), custom_call_target="tpu_custom_call" | custom-call | tf_op jit(solution)/shard_map/share_mp/pallas_call | solution.py:530
  705.8 3.6 convolution_convert_fusion.6
  723.1 3.5 multiply_reduce_fusion.1
  726.6 3.0 convolution_convert_fusion.9
  733.6 3.0 copy.202
  736.6 4.1 reshape.459
  742.9 2.4 pad_maximum_fusion.refs_1_
  748.2 2.5 copy.203
  757.7 4.6 multiply_reduce_fusion
  765.0 3.1 fusion.36
  773.7 3.5 fusion.10
  788.0 2.6 reshape.455
  790.6 2.5 copy.167
  795.3 11.9 %concatenate.55.refs_0_ = bf16[32,64,1920]{2,1,0:T(8,128)(2,1)} concatenate(bf16[32,64,256]{2,1,0:T(8,128)(2,1)} %bitcast.138, bf16[32,64,256]{2,1,0:T(8,128)(2,1)} %bitcast.137, bf16[32,64,256]{2,1,0:T(8,128)(2,1)} %bitcast.148, bf16[32,64,256]{2,1,0:T(8,128)(2,1)} %bitcast.147, bf16[32,64,256]{2,1,0:T(8,128)(2,1)} %bitcast.146, bf16[32,64,64]{2,1,0:T(8,128)(2,1)} %bitcast.145, ...), dimensions={2} | concatenate | bytes 15728640 | tf_op jit(solution)/shard_map/concatenate | solution.py:1218
  807.2 158.5 %end.1 = (bf16[32,4096]{1,0:T(8,128)(2,1)}, bf16[32,4096]{1,0:T(8,128)(2,1)}, f32[64,1920]{1,0:T(8,128)}, f32[576,512]{1,0:T(8,128)}, f32[4,64,512]{2,1,0:T(8,128)}, /*index=5*/bf16[16,64,1920]{2,1,0:T(8,128)(2,1)}) custom-call(bf16[32,64,1920]{2,1,0:T(8,128)(2,1)} %concatenate.55.refs_0_, bf16[8,576,512]{2,1,0:T(8,128)(2,1)} %pad_maximum_fusion.refs_1_, ...), custom_call_target="tpu_custom_call" | custom-call | tf_op jit(solution)/shard_map/end/pallas_call | solution.py:530
  985.0 3.3 fusion.118
  988.4 3.6 convolution_convert_fusion
  992.0 17.9 %sum_mp.3 = f32[128,2048]{1,0:T(8,128)} custom-call(bf16[4,128,2048]{2,1,0:T(8,128)(2,1)} %bitcast.143), custom_call_target="tpu_custom_call" | custom-call | tf_op jit(solution)/shard_map/sum_mp/pallas_call | solution.py:530
  1011.5 3.6 fusion.35
  (252 shorter events, 111.0 us)
Async XLA Ops:
  0.7 403.6 %copy-start = (bf16[512,256]{1,0:T(8,128)(2,1)S(1)}, bf16[512,256]{1,0:T(8,128)(2,1)}, u32[]{:S(2)}) copy-start(bf16[512,256]{1,0:T(8,128)(2,1)} %param.51) | copy-start | bytes 786436
  0.7 8.7 copy-start.50
  0.7 8.7 copy-start.54
  0.7 8.7 copy-start.53
  272.5 6.4 copy-start.66
  275.3 3.6 copy-start.69
  285.8 5.6 copy-start.18
  285.8 5.6 copy-start.20
  297.5 18.2 %copy-start.2 = (bf16[128,2048]{1,0:T(8,128)(2,1)S(1)}, bf16[128,2048]{1,0:T(8,128)(2,1)}, u32[]{:S(2)}) copy-start(bf16[128,2048]{1,0:T(8,128)(2,1)} %refs_0_.1) | copy-start | bytes 1572868
  317.2 369.6 %copy-start.56 = (f32[128]{0:T(128)}, f32[128]{0:T(128)S(1)}, u32[]{:S(2)}) copy-start(f32[128]{0:T(128)S(1)} %add_rsqrt_fusion.1) | copy-start | bytes 1540
  406.3 265.7 %copy-start.62 = (bf16[256]{0:T(256)(128)(2,1)S(1)}, bf16[256]{0:T(256)(128)(2,1)}, u32[]{:S(2)}) copy-start(bf16[256]{0:T(256)(128)(2,1)} %param.43) | copy-start | bytes 1540
  672.1 7.0 copy-start.10
  682.4 3.5 copy-start.4
  686.8 19.0 %copy-start.59 = (f32[128]{0:T(128)}, f32[128]{0:T(128)S(1)}, u32[]{:S(2)}) copy-start(f32[128]{0:T(128)S(1)} %get-tuple-element.124) | copy-start | bytes 1540
  705.8 3.7 copy-start.17
  719.3 3.5 copy-start.70
  719.3 3.8 copy-start.73
  723.1 3.5 copy-start.75
  726.6 4.8 copy-start.12
  726.6 3.4 copy-start.21
  726.6 3.5 copy-start.64
  773.7 3.5 copy-start.11
  773.7 3.5 copy-start.46
  965.7 8.1 copy-start.39
  967.4 6.5 copy-start.44
  967.4 6.5 copy-start.45
  974.0 11.0 %copy-start.31 = (bf16[256,2048]{1,0:T(8,128)(2,1)S(1)}, bf16[256,2048]{1,0:T(8,128)(2,1)}, u32[]{:S(2)}) copy-start(bf16[256,2048]{1,0:T(8,128)(2,1)} %get-tuple-element.64) | copy-start | bytes 3145732
  985.0 3.3 copy-start.71
  992.0 17.9 %copy-start.58 = (f32[128]{0:T(128)S(1)}, f32[128]{0:T(128)}, u32[]{:S(2)}) copy-start(f32[128]{0:T(128)} %get-tuple-element.123) | copy-start | bytes 1540
  992.0 19.5 %copy-start.57 = (f32[128]{0:T(128)S(1)}, f32[128]{0:T(128)}, u32[]{:S(2)}) copy-start(f32[128]{0:T(128)} %copy-done.56) | copy-start | bytes 1540
  992.0 19.5 %copy-start.60 = (f32[128]{0:T(128)S(1)}, f32[128]{0:T(128)}, u32[]{:S(2)}) copy-start(f32[128]{0:T(128)} %copy-done.59) | copy-start | bytes 1540
  1011.5 3.6 copy-start.16
  (45 other events, 104.8 us)

commit v4 on v3

--- a/solution.py
+++ b/solution.py
@@ -340,31 +340,6 @@
     lax.fori_loop(0, rows // CHUNK, one, 0)
 
 
-def chain_z(w, own, below, above, out):
-    z, n = w.z, w.levels
-    rise, fall = w.take(n), w.take(n)
-    for step in range(n - 1, 0, -1):
-        for rising, zt, ok in ((True, z + step, z < n - step), (False, z - step, z >= step)):
-            lane = rise if rising else fall
-            slot = below(zt) if rising else above(zt)
-            inner = jnp.logical_and(ok, (z > 0) if rising else (z < n - 1))
-
-            def take_in():
-                w.landed(slot, lane + zt)
-                add_up(own(zt), own(zt), slot)
-
-            under(inner, take_in)
-            w.send(own(zt), slot, lane + zt, lane + zt, w.up() if rising else w.down(), ok)
-        yield
-    under(z > 0, lambda: w.landed(below(z), rise + z))
-    under(z < n - 1, lambda: w.landed(above(z), fall + z))
-    under(z == 0, lambda: add_up(out, own(z), above(z)))
-    under(z == n - 1, lambda: add_up(out, own(z), below(z)))
-    under(
-        jnp.logical_and(z > 0, z < n - 1), lambda: add_up(out, own(z), below(z), above(z))
-    )
-
-
 def planes(w):
     z, n = w.z, w.levels
     for k in range(n - 1):
@@ -392,11 +367,12 @@
         for kind, (ys, xs) in enumerate(kinds):
             here = k * 4 + kind
             lane = to_core + here
-            w.send(part.at[flat(zs, ys, xs, 1 - c)], landing.at[here], lane, lane, w.over_core())
-            kept[here] = pltpu.make_async_copy(
-                part.at[flat(zs, ys, xs, c)], own.at[here], w.locals.at[from_part + here]
-            )
-            kept[here].start()
+            for source, into in part(zs, ys, xs, 1 - c):
+                w.copy(source, into(landing.at[here]), lane, lane, w.over_core()).start()
+            w.open.append((True, w.copy(landing.at[here], landing.at[here], lane, lane, w.over_core()).wait_send))
+            for source, into in part(zs, ys, xs, c):
+                pltpu.make_async_copy(source, into(own.at[here]), w.locals.at[from_part + here]).start()
+            kept[here] = pltpu.make_async_copy(landing.at[here], own.at[here], w.locals.at[from_part + here])
 
     def join(k):
         loads = []
@@ -432,25 +408,7 @@
         if k == n - 1:
             add_up(here, here, full_x.at[k], full_y.at[k])
             return
-        rising, falling = zs > z, zs < z
-        more_up, more_down = jnp.logical_and(rising, z > 0), jnp.logical_and(falling, z < n - 1)
-
-        def take_below():
-            w.landed(below.at[zs - 1], rise + zs)
-            add_up(here, here, full_x.at[k], full_y.at[k], below.at[zs - 1])
-
-        def take_above():
-            w.landed(above.at[zs], fall + zs)
-            add_up(here, here, full_x.at[k], full_y.at[k], above.at[zs])
-
-        under(more_up, take_below)
-        under(more_down, take_above)
-        under(
-            jnp.logical_not(jnp.logical_or(more_up, more_down)),
-            lambda: add_up(here, here, full_x.at[k], full_y.at[k]),
-        )
-        w.send(here, below.at[zs - 1], rise + zs, rise + zs, w.up(), rising)
-        w.send(here, above.at[zs], fall + zs, fall + zs, w.down(), falling)
+        pass_on(w, zs, here, (full_x.at[k], full_y.at[k]), below, above, rise, fall)
 
     for k in range(n + 3):
         if make is not None:
@@ -462,12 +420,41 @@
             if 0 <= k - lag < n:
                 act(k - lag)
                 yield
-    here = own.at[4 * n - 1]
+    last_sum(w, own.at[4 * n - 1], (), below, above, rise, fall, out)
+
+
+def pass_on(w, zs, here, sources, below, above, rise, fall):
+    z, n = w.z, w.levels
+    rising, falling = zs > z, zs < z
+    more_up, more_down = jnp.logical_and(rising, z > 0), jnp.logical_and(falling, z < n - 1)
+
+    def take_below():
+        w.landed(below.at[zs - 1], rise + zs)
+        add_up(here, here, *sources, below.at[zs - 1])
+
+    def take_above():
+        w.landed(above.at[zs], fall + zs)
+        add_up(here, here, *sources, above.at[zs])
+
+    under(more_up, take_below)
+    under(more_down, take_above)
+    under(
+        jnp.logical_not(jnp.logical_or(more_up, more_down)), lambda: add_up(here, here, *sources)
+    )
+    w.send(here, below.at[zs - 1], rise + zs, rise + zs, w.up(), rising)
+    w.send(here, above.at[zs], fall + zs, fall + zs, w.down(), falling)
+
+
+def last_sum(w, here, sources, below, above, rise, fall, out):
+    z, n = w.z, w.levels
     under(z > 0, lambda: w.landed(below.at[z - 1], rise + z))
     under(z < n - 1, lambda: w.landed(above.at[z], fall + z))
-    under(z == 0, lambda: add_up(out, here, above.at[z]))
-    under(z == n - 1, lambda: add_up(out, here, below.at[z - 1]))
-    under(jnp.logical_and(z > 0, z < n - 1), lambda: add_up(out, here, below.at[z - 1], above.at[z]))
+    under(z == 0, lambda: add_up(out, here, *sources, above.at[z]))
+    under(z == n - 1, lambda: add_up(out, here, *sources, below.at[z - 1]))
+    under(
+        jnp.logical_and(z > 0, z < n - 1),
+        lambda: add_up(out, here, *sources, below.at[z - 1], above.at[z]),
+    )
 
 
 def scatter_all_scratch(n, rows, columns):
@@ -477,31 +464,23 @@
 
 
 def scatter_dp(w, part, own, over, below, above, out):
-    z, y, n = w.z, w.y, w.levels
-    by_y, spare = w.take(n), w.take_local(n)
-    kept = []
-    order = []
-    for step in range(n - 1, 0, -1):
-        order += [side for side in sides(w, step)]
-    order.append((True, z, True))
-    for _, zs, ok in order:
-        w.send(part.at[zs * 2 + 1 - y], over.at[zs], by_y + zs, by_y + zs, w.over_y(), ok)
-        made = pltpu.make_async_copy(part.at[zs * 2 + y], own.at[zs], w.locals.at[spare + zs])
-        under(ok, made.start)
-        kept.append(made)
-    yield
-    for made, (_, zs, ok) in zip(kept, order):
-
-        def act():
-            made.wait()
-            w.landed(over.at[zs], by_y + zs)
-            add_up(own.at[zs], own.at[zs], over.at[zs])
-
-        under(ok, act)
-    yield
-    yield from chain_z(
-        w, lambda zt: own.at[zt], lambda zt: below.at[zt], lambda zt: above.at[zt], out
-    )
+    y, n = w.y, w.levels
+    by_y, rise, fall, spare = w.take(n), w.take(n), w.take(n), w.take_local(n)
+    order = list(planes(w))
+    for k, zs in enumerate(order):
+        for source, into in part(zs, 1 - y):
+            w.copy(source, into(over.at[k]), by_y + k, by_y + k, w.over_y()).start()
+        w.open.append((True, w.copy(over.at[k], over.at[k], by_y + k, by_y + k, w.over_y()).wait_send))
+        for source, into in part(zs, y):
+            pltpu.make_async_copy(source, into(own.at[k]), w.locals.at[spare + k]).start()
+        yield
+    for k, zs in enumerate(order):
+        pltpu.make_async_copy(over.at[k], own.at[k], w.locals.at[spare + k]).wait()
+        w.landed(over.at[k], by_y + k)
+        if k < n - 1:
+            pass_on(w, zs, own.at[k], (over.at[k],), below, above, rise, fall)
+            yield
+    last_sum(w, own.at[n - 1], (over.at[n - 1],), below, above, rise, fall, out)
 
 
 def scatter_mp(w, part, own, first, second, out):
@@ -565,6 +544,14 @@
 
 def flat(z, y, x, c):
     return (z * 2 + y) * 4 + x * 2 + c
+
+
+def one_block(array):
+    return lambda z, y, x, c: [(array.at[flat(z, y, x, c)], lambda ref: ref)]
+
+
+def corner(first, rows, column, columns):
+    return lambda ref: ref.at[pl.ds(first, rows), pl.ds(column, columns)]
 
 
 def begin(levels, tensors):
@@ -688,9 +675,9 @@
     each = len(scratch)
 
     def kernel(tokens_ref, grads_ref, gate_up_hbm, down_hbm, *refs):
-        grad_out, branch_out, pair_hbm, single_hbm, gate_own, up_own, down_own = refs[:7]
-        hidden_hbm, pre_hbm, grad_part, branch_part, grad_land, branch_land = refs[7:13]
-        buffers = refs[13:]
+        grad_out, branch_out, pair_hbm, single_hbm, gate_own, up_own = refs[:6]
+        hidden_hbm, pre_hbm, grad_part, branch_part, grad_land, branch_land = refs[6:12]
+        buffers = refs[12:]
         one, two = buffers[:each], buffers[each : 2 * each - 1]
         two = two[:1] + (one[1],) + two[1:]
         gate_up_ref, down_ref, arena, hidden_stage, pre_stage, columns, down_stage, loads, stores = buffers[
@@ -732,7 +719,7 @@
         for copy in weights:
             copy.wait()
 
-        lanes = w.take(3 * count)
+        lanes = w.take(2 * count)
 
         def there(i):
             return lax.rem(w.dp + 1 + i, count)
@@ -756,9 +743,6 @@
             both_rows = rows_of(pair_hbm, there(i), strip)
             yield both_rows.at[:, pl.ds(0, unit)], columns_of(gate_own, w.dp, unit), lanes + i
             yield both_rows.at[:, pl.ds(unit, unit)], columns_of(up_own, w.dp, unit), lanes + count + i
-
-        def single_pieces(i):
-            yield strip_of(single_hbm, i), rows_of(down_own, w.dp, unit), lanes + 2 * count + i
 
         def give(pieces, i):
             for source, target, lane in pieces(i):
@@ -815,7 +799,6 @@
             @pl.when(i > 0)
             def _():
                 single_store(i - 1).wait()
-                give(single_pieces, i - 1)
 
             return carry
 
@@ -837,7 +820,6 @@
             if k == levels + 2:
                 lax.fori_loop(0, count, single_strip, 0)
                 single_store(count - 1).wait()
-                keep(single_pieces)
 
         def make(k):
             if k >= levels:
@@ -892,15 +874,15 @@
 
         turn(
             [
-                scatter_all(w, grad_part, grad_land, *one, grad_out, make=make),
-                scatter_all(w, branch_part, branch_land, *two, branch_out, make=idle),
+                scatter_all(w, one_block(grad_part), grad_land, *one, grad_out, make=make),
+                scatter_all(w, one_block(branch_part), branch_land, *two, branch_out, make=idle),
             ]
         )
         for i in range(count - 1):
             source = lax.rem(w.dp + count - 1 - i, count)
             for sent, (_, _, lane) in zip(
-                (columns_of(gate_own, source, unit), columns_of(up_own, source, unit), rows_of(down_own, source, unit)),
-                (*pair_pieces(i), *single_pieces(i)),
+                (columns_of(gate_own, source, unit), columns_of(up_own, source, unit)),
+                pair_pieces(i),
             ):
                 w.landed(sent, lane)
                 w.copy(sent, sent, lane, lane, w.over_x()).wait_send()
@@ -910,7 +892,7 @@
     tall = [(deep, deep), (2, TALL, unit), (2, TALL, both), (2, total, strip), (2, unit, strip)]
     outs = [((rows, deep), jnp.float32, True)] * 2
     outs += [((deep, both), kind, False), ((unit, deep), kind, False)]
-    outs += [((strip, unit * count), kind, False)] * 2 + [((unit * count, strip), kind, False)]
+    outs += [((strip, unit * count), kind, False)] * 2
     outs += [((total, unit), kind, False), ((total, both), kind, False)]
     outs += [((total // rows, rows, deep), kind, False)] * 2 + [((4 * levels, rows, deep), kind, False)] * 2
     made = call(
@@ -928,7 +910,7 @@
         16 * levels + 12,
         name="feed",
     )
-    return made[:7]
+    return made[:6]
 
 
 def share_mp(levels, rows):
@@ -964,62 +946,87 @@
     return out
 
 
-BACK = 4
-
-
-def end(levels, small, split, units, share):
+BACK = 2
+
+
+def end(levels, rank, small, wides, query, output, units):
+    count = 2 * levels
+    deep, narrow = small.shape
+    few, piece = deep // (4 * count), deep // 4
+    wide = narrow + piece
+    high = rank // count
+    strip = deep // count
+    unit = units.down_weight.shape[0]
     names = list(vars(units))
-    count = 2 * levels
-    low, unit = units.gate_expand.shape
     shapes = dict(
-        gate_expand=(low // count, unit * count),
-        up_expand=(low // count, unit * count),
-    )
-    few, wide = small.shape[1:]
-    many, flatly = split.shape[1:]
+        down_weight=(unit * count, strip),
+        gate_expand=(high, unit * count),
+        up_expand=(high, unit * count),
+    )
+    heads = query[0].shape[1]
+    query_shape = (strip + high, heads)
+    output_shape = (heads + heads // count, strip)
     scratch = scatter_all_scratch(levels, few, wide)
-    scratch += [pltpu.VMEM((levels, many, flatly), jnp.bfloat16)] * 4
-    first = len(names) + 2
+    each = len(scratch)
+    scratch += [pltpu.VMEM((levels,) + query_shape, jnp.bfloat16)] * 4
+    scratch += [pltpu.VMEM((levels,) + output_shape, jnp.bfloat16)] * 4
 
     def kernel(*refs):
-        small_ref, split_ref = refs[:2]
-        given = SimpleNamespace(**dict(zip(names, refs[2:])))
-        got = SimpleNamespace(**dict(zip(shapes, refs[first:])))
-        after = first + len(shapes)
-        small_out, split_out, shared, landing = refs[after : after + 4]
-        buffers = refs[after + 4 : -3]
-        w = Wires(levels, *refs[-3:])
+        small_ref, wide_one, wide_two, query_w, query_b, output_w, output_a = refs[:7]
+        given = SimpleNamespace(**dict(zip(names, refs[7:])))
+        refs = refs[7 + len(names) :]
+        got = SimpleNamespace(**dict(zip(shapes, refs)))
+        small_out, query_out, output_out, shared, landing = refs[len(names) : len(names) + 5]
+        buffers = refs[len(names) + 5 :]
+        w = Wires(levels, *buffers[-3:])
         w.greet(far=True)
 
+        def blocks(z, y, x, c):
+            place = (pl.ds(pl.multiple_of((z * 2 + y) * high, high), high), pl.ds(pl.multiple_of((x * 2 + c) * piece, piece), piece))
+            yield rows_of(small_ref, flat(z, y, x, c), few), corner(0, few, 0, narrow)
+            yield wide_one.at[place], corner(0, high, narrow, piece)
+            yield wide_two.at[place], corner(high, high, narrow, piece)
+
+        def query_blocks(z, y):
+            yield rows_of(query_w, z * 2 + y, strip), corner(0, strip, 0, heads)
+            yield rows_of(query_b, z * 2 + y, high), corner(strip, high, 0, heads)
+
+        def output_blocks(z, y):
+            yield columns_of(output_w, z * 2 + y, strip), corner(0, heads, 0, strip)
+            yield rows_of(output_a, z * 2 + y, heads // count), corner(heads, heads // count, 0, strip)
+
         def over_all():
-            yield from scatter_all(w, small_ref, landing, *buffers[:8], small_out)
-            mine = small_out.at[:, pl.ds(wide - share, share)]
+            yield from scatter_all(w, blocks, landing, *buffers[:each], small_out)
+            mine = small_out.at[:, pl.ds(narrow, piece)]
             yield from gather_mp(w, mine, lambda x, c: shared.at[x * 2 + c])
 
+        after = [
+            exchange_dp(w, lambda dp: columns_of(given.down_weight, dp, strip), lambda dp: rows_of(got.down_weight, dp, unit)),
+            exchange_dp(w, lambda dp: rows_of(given.gate_expand, dp, high), lambda dp: columns_of(got.gate_expand, dp, unit)),
+            exchange_dp(w, lambda dp: rows_of(given.up_expand, dp, high), lambda dp: columns_of(got.up_expand, dp, unit)),
+        ]
         steps = [
-            scatter_dp(w, split_ref, *buffers[8:], split_out),
             over_all(),
-        ]
-        after = [
-            exchange_dp(w, lambda dp: rows_of(given.gate_expand, dp, low // count), lambda dp: columns_of(got.gate_expand, dp, unit)),
-            exchange_dp(w, lambda dp: rows_of(given.up_expand, dp, low // count), lambda dp: columns_of(got.up_expand, dp, unit)),
+            scatter_dp(w, query_blocks, *buffers[each : each + 4], query_out),
+            scatter_dp(w, output_blocks, *buffers[each + 4 : each + 8], output_out),
         ]
         turn(steps, after, BACK)
         w.finish()
 
     outs = [(shape, jnp.bfloat16, False) for shape in shapes.values()]
-    outs += [((few, wide), jnp.float32, True), ((many, flatly), jnp.float32, True), ((4, few, share), jnp.float32, True), ((4 * levels, few, wide), jnp.bfloat16, False)]
+    outs += [((few, wide), jnp.float32, True), (query_shape, jnp.float32, True), (output_shape, jnp.float32, True)]
+    outs += [((4, few, piece), jnp.float32, True), ((4 * levels, few, wide), jnp.bfloat16, False)]
     made = call(
         kernel,
         5,
-        [small, split] + list(vars(units).values()),
+        [small, *wides, *query, *output, *vars(units).values()],
         outs,
         scratch,
         32 * levels,
-        9 * levels + 16,
+        10 * levels + 16,
         name="end",
     )
-    return SimpleNamespace(**dict(zip(shapes, made))), made[-4], made[-3], made[-2]
+    return SimpleNamespace(**dict(zip(shapes, made))), *made[3:7]
 
 
 def low(rows):
@@ -1033,6 +1040,11 @@
 
 def norm_back(grad, normed, scale):
     return scale * (grad - normed * jnp.mean(grad * normed, axis=-1, keepdims=True))
+
+
+def ones_in(rows, column):
+    columns = jnp.arange(128)[None, :]
+    return jnp.broadcast_to((columns >= column) & (columns < column + 32), (rows, 128)).astype(jnp.bfloat16)
 
 
 def by_unit(
@@ -1157,15 +1169,11 @@
     normed_middle, scale_middle = unit_rows(middle)
     normed_all = spread(levels, low(normed_middle)).reshape(4 * count * rows, deep)
     grads = got.output_grad.reshape(4 * count * rows, deep)
-    grad_normed, branch, pair_grad, down_grad_low, gate_own, up_own, down_own = feed(levels, rows, normed_all, grads, gate_up, down_full)
+    grad_normed, branch, pair_grad, down_grad_low, gate_own, up_own = feed(levels, rows, normed_all, grads, gate_up, down_full)
     result = low(middle + branch)
     grad_middle = output_grad.astype(jnp.float32) + norm_back(grad_normed, normed_middle, scale_middle)
 
-    feed_gain = (
-        jnp.sum(pair_grad.astype(jnp.float32) * gate_up.astype(jnp.float32), axis=1, keepdims=True) / gain_two
-    )
     down_shrink_grad = against(down_grad_low, down_b)
-    down_b_part = outer_sum(down_a, down_grad_low)
     gate_b_grad = low(outer_sum(low(gain_two * gate_a.astype(jnp.float32)), pair_grad[:, :unit]))
     up_b_grad = low(outer_sum(low(gain_two * up_a.astype(jnp.float32)), pair_grad[:, unit:]))
     gate_a_part = gain_two * against(pair_grad[:, :unit], got.gate_expand)
@@ -1189,66 +1197,42 @@
     input_grad = grad_middle + norm_back(grad_rows, normed_own, scale_own)
 
     lin_normed = outer_sum(normed, grad_lin)
-    attention_gain_part = jnp.sum(lin_normed * inward.astype(jnp.float32), axis=1, keepdims=True) / gain_one
     lin_grad = low(lin_normed * gain_one)
     query_part, key_part, value_part = (
         lin_grad[:, :wide],
         lin_grad[:, wide : wide + head],
         lin_grad[:, wide + head :],
     )
-    query_b_part = outer_sum(query_a, query_part)
-    key_b_part = outer_sum(key_a, key_part)
-    value_b_part = outer_sum(value_a, value_part)
-    query_a_part = against(query_part, query_b)
     output_low = low(output_grad_w)
-    output_a_part = against(output_low, output_b)
-    output_b_part = outer_sum(output_a, output_low)
-
-    def by_device(array):
-        return low(array).reshape(4 * count, array.shape[0] // (4 * count), array.shape[1])
+    gain_parts = matmul(low(lin_normed) * inward, ones_in(inward.shape[1], 0)) + matmul(
+        pair_grad * gate_up, ones_in(2 * unit, 32)
+    )
 
     def fold(array):
-        return by_device(array).reshape(4 * count, share, -1)
-
-    def fold_wide(array):
-        cut = low(array).reshape(count, array.shape[0] // count, 4, array.shape[1] // 4)
-        return cut.transpose(0, 2, 1, 3).reshape(4 * count, share, -1)
-
-    gain_part = jnp.pad(jnp.concatenate([attention_gain_part, feed_gain], axis=1), ((0, 0), (0, 62)))
+        return low(array).reshape(4 * count, array.shape[0] // (4 * count), head).reshape(deep, -1)
+
+    folded = jnp.concatenate(
+        [fold(outer_sum(key_a, key_part)), fold(outer_sum(value_a, value_part))], axis=1
+    )
     small = jnp.concatenate(
         [
-            by_device(key_part),
-            by_device(value_part),
-            by_device(query_a_part),
-            by_device(gate_a_part),
-            by_device(up_a_part),
-            by_device(gain_part),
-            fold(key_b_part),
-            fold(value_b_part),
-            fold_wide(output_b_part),
-            fold_wide(down_b_part),
-        ],
-        axis=2,
-    )
-    split = jnp.concatenate(
-        [
-            low(query_part).reshape(count, -1, wide),
-            output_low.reshape(wide, count, deep // count).transpose(1, 0, 2).reshape(count, -1, wide),
-            low(query_b_part).reshape(count, -1, wide),
-            low(output_a_part).reshape(count, -1, wide),
+            lin_grad[:, wide:],
+            low(against(query_part, query_b)),
+            low(gate_a_part),
+            low(up_a_part),
+            low(gain_parts[:, :64]),
+            folded,
         ],
         axis=1,
     )
-    wide_share = 2 * (rank // count) * (deep // 4) // share
-    units, few, many, shared = end(
+    units, few, query_sum, output_sum, shared = end(
         levels,
+        rank,
         small,
-        split,
-        SimpleNamespace(
-            gate_expand=gate_b_grad,
-            up_expand=up_b_grad,
-        ),
-        wide_share,
+        (low(outer_sum(output_a, output_low)), low(outer_sum(down_a, down_grad_low))),
+        (query_part, low(outer_sum(query_a, query_part))),
+        (output_low, low(against(output_low, output_b))),
+        SimpleNamespace(down_weight=down_grad_low, gate_expand=gate_b_grad, up_expand=up_b_grad),
     )
     key_own, value_own = few[:, :head], few[:, head : 2 * head]
     query_a_own, gate_a_own, up_a_own = (
@@ -1257,44 +1241,44 @@
     place = 2 * head + 3 * rank
     key_b_own = few[:, place + 64 : place + 96].reshape(-1, head)
     value_b_own = few[:, place + 96 : place + 128].reshape(-1, head)
-    half = wide_share // 2
+    high = rank // count
 
     def unfold(array):
-        return array.reshape(4, rank // count, deep // 4).transpose(1, 0, 2).reshape(-1, deep)
+        return jnp.concatenate([array[i] for i in range(4)], axis=1)
+
+    def own_part(gain):
+        return lax.dynamic_slice_in_dim(gain.astype(jnp.float32), mp * share, share, 0)
 
     key_a_own = against(low(key_own), key_b)
     value_a_own = against(low(value_own), value_b)
-    first = query_weight.shape[0]
-    second = first + output_weight.size // wide
-    third = second + query_expand.shape[0]
     wider = jnp.float32
     own_gain = feedforward_gain.astype(wider)[:, None]
     return (
         result,
         input_grad,
-        few[:, place],
-        many[:first],
+        few[:, place] / own_part(attention_gain),
+        query_sum[: deep // count],
         key_own,
         value_own,
-        many[first:second].reshape(output_weight.shape),
+        output_sum[:wide],
         query_a_own,
-        many[second:third],
+        query_sum[deep // count :],
         key_a_own,
         key_b_own,
         value_a_own,
         value_b_own,
-        many[third:].reshape(output_shrink.shape),
-        unfold(shared[:, :, :half]),
-        few[:, place + 1],
+        output_sum[wide:],
+        unfold(shared[:, :high]),
+        few[:, place + 32] / own_part(feedforward_gain),
         own_gain * gate_own.astype(wider),
         own_gain * up_own.astype(wider),
-        down_own.astype(wider),
+        units.down_weight.astype(wider),
         gate_a_own,
         units.gate_expand.astype(wider),
         up_a_own,
         units.up_expand.astype(wider),
         down_shrink_grad,
-        unfold(shared[:, :, half:]),
+        unfold(shared[:, high:]),
     )
 
 

time: 1030 us -> 935 us (0.908)
  Pallas kernels: 815 us -> 764 us
  local copies, waits for them, and re-layouts: 82.3 us -> 42 us
    pallas_call x7, Pallas kernels: 815 us -> 764 us  [call(): pl.pallas_call(kernel, out_shape=[jax.ShapeDtypeStruct(shape, kind) for s...]
    reshape x14 -> x0, local copies, waits for them, and re-layouts: 20.9 us -> none  [the longest x2 7.08 us: by_unit(): output_low.reshape(wide, count, deep // count).transpose(1, 0, 2)]
    dot_general x9 -> x11, matrix products: 19.8 us -> 25.4 us  [matmul(): return jnp.dot(left, right, preferred_element_type=jnp.float32)]
where the time goes in v4:
time: 935 us; the launch traced here: 924 us
  Pallas kernels  764 us (82%)
  matrix products  79 us (8%)
  local copies, waits for them, and re-layouts  42 us (4%)
  other arithmetic  37 us (4%)
    pallas_call x7, Pallas kernels, call(): pl.pallas_call(kernel, out_shape=[jax.ShapeDtypeStruct(shape, kind) for s...  764 us
    dot_general x9, matrix products, outer_sum(): lax.dot_general(left, right, (((0,), (0,)), ((), ())), preferred_element_...  26.7 us
    dot_general x11, matrix products, matmul(): return jnp.dot(left, right, preferred_element_type=jnp.float32)  25.4 us

profile of v4, /device:TPU:0, one launch (start us, length us, event | category | flops | bytes accessed | tf_op | source)
XLA Modules:
  0.0 924.4 jit_solution(2228494607588079017)
XLA Ops:
  10.1 257.9 %begin.1 = (bf16[4,128,2048]{2,1,0:T(8,128)(2,1)}, bf16[2048,1920]{1,0:T(8,128)(2,1)}, bf16[256,2048]{1,0:T(8,128)(2,1)}, bf16[256,2048]{1,0:T(8,128)(2,1)}, bf1...) custom-call(bf16[128,2048]{1,0:T(8,128)(2,1)} %refs_0_.1, ...), custom_call_target="tpu_custom_call" | custom-call | tf_op jit(solution)/shard_map/begin/pallas_call | solution.py:509
  269.7 2.8 multiply_convert_fusion.1
  272.5 2.8 fusion.12
  275.4 2.4 fusion.13
  278.9 2.3 fusion.113
  289.2 2.2 fusion.118
  291.5 2.4 convolution_convert_fusion.7
  294.9 2.6 convolution_convert_fusion.2
  297.5 18.1 %sum_mp.2 = f32[128,2048]{1,0:T(8,128)} custom-call(bf16[4,128,2048]{2,1,0:T(8,128)(2,1)} %bitcast.122), custom_call_target="tpu_custom_call" | custom-call | tf_op jit(solution)/shard_map/sum_mp/pallas_call | solution.py:509
  318.2 78.8 %spread.1 = bf16[32,128,2048]{2,1,0:T(8,128)(2,1)} custom-call(bf16[128,2048]{1,0:T(8,128)(2,1)} %multiply_convert_fusion.6.own), custom_call_target="tpu_custom_call" | custom-call | tf_op jit(solution)/shard_map/spread/pallas_call | solution.py:509
  399.0 2.1 fusion.51
  401.6 2.8 fusion.2.gate_up_hbm
  404.3 2.0 fusion.3.down_hbm
  406.4 233.4 %feed.1 = (f32[128,2048]{1,0:T(8,128)}, f32[128,2048]{1,0:T(8,128)}, bf16[2048,1024]{1,0:T(8,128)(2,1)}, bf16[512,2048]{1,0:T(8,128)(2,1)}, bf16[256,4096]{1,0:T...) custom-call(bf16[4096,2048]{1,0:T(8,128)(2,1)} %bitcast.117, ...), custom_call_target="tpu_custom_call" | custom-call | tf_op jit(solution)/shard_map/feed/pallas_call | solution.py:509
  639.8 7.0 convert_multiply_fusion
  646.7 3.4 fusion.33.refs_9_
  650.1 3.4 fusion.30.refs_8_
  655.8 19.0 %share_mp.1 = bf16[4,128,2048]{2,1,0:T(8,128)(2,1)} custom-call(bf16[128,2048]{1,0:T(8,128)(2,1)} %fusion.112.own), custom_call_target="tpu_custom_call" | custom-call | tf_op jit(solution)/shard_map/share_mp/pallas_call | solution.py:509
  674.8 3.2 convolution_convert_fusion.1.refs_5_
  691.7 2.3 fusion.36
  694.2 4.3 multiply_convert_fusion
  698.5 3.7 convolution_convert_fusion.9.refs_4_
  708.2 4.3 fusion.7
  722.5 2.3 fusion.114
  724.8 10.0 %concatenate.53.refs_0_ = bf16[2048,1408]{1,0:T(8,128)(2,1)} concatenate(bf16[2048,512]{1,0:T(8,128)(2,1)} %get-tuple-element.86, bf16[2048,256]{1,0:T(8,128)(2,1)} %convolution_convert_fusion.5, bf16[2048,256]{1,0:T(8,128)(2,1)} %fusion.14, bf16[2048,256]{1,0:T(8,128)(2,1)} %fusion.15, bf16[2048,64]{1,0:T(8,128)(2,1)S(1)} %fusion.44, bf16[2048,32]{1,0:T(8,128)(2,1)S(1)} %reshape_reshape.6, ...), dimensions={1} | concatenate | bytes 11534336 | tf_op jit(solution)/shard_map/concatenate | solution.py:1217
  734.8 3.3 fusion.16.refs_2_
  738.1 139.2 %end.1 = (bf16[4096,256]{1,0:T(8,128)(2,1)}, bf16[32,4096]{1,0:T(8,128)(2,1)}, bf16[32,4096]{1,0:T(8,128)(2,1)}, f32[64,1920]{1,0:T(8,128)}, f32[288,512]{1,0:T(...) custom-call(bf16[2048,1408]{1,0:T(8,128)(2,1)} %concatenate.53.refs_0_, ...), custom_call_target="tpu_custom_call" | custom-call | tf_op jit(solution)/shard_map/end/pallas_call | solution.py:509
  877.4 4.0 convert_element_type.259
  894.0 3.3 fusion.121
  897.3 3.6 convolution_convert_fusion
  900.9 17.9 %sum_mp.3 = f32[128,2048]{1,0:T(8,128)} custom-call(bf16[4,128,2048]{2,1,0:T(8,128)(2,1)} %bitcast.121), custom_call_target="tpu_custom_call" | custom-call | tf_op jit(solution)/shard_map/sum_mp/pallas_call | solution.py:509
  920.5 3.5 fusion.40
  (230 shorter events, 72.1 us)
Async XLA Ops:
  0.7 403.7 %copy-start = (bf16[512,256]{1,0:T(8,128)(2,1)S(1)}, bf16[512,256]{1,0:T(8,128)(2,1)}, u32[]{:S(2)}) copy-start(bf16[512,256]{1,0:T(8,128)(2,1)} %param.51) | copy-start | bytes 786436
  0.7 8.7 copy-start.57
  0.7 8.7 copy-start.61
  0.7 8.7 copy-start.60
  272.5 6.4 copy-start.66
  275.3 3.6 copy-start.68
  285.8 5.6 copy-start.17
  285.8 5.6 copy-start.19
  297.5 18.2 %copy-start.3 = (bf16[128,2048]{1,0:T(8,128)(2,1)S(1)}, bf16[128,2048]{1,0:T(8,128)(2,1)}, u32[]{:S(2)}) copy-start(bf16[128,2048]{1,0:T(8,128)(2,1)} %refs_0_.1) | copy-start | bytes 1572868
  406.4 233.4 %copy-start.63 = (bf16[256]{0:T(256)(128)(2,1)S(1)}, bf16[256]{0:T(256)(128)(2,1)}, u32[]{:S(2)}) copy-start(bf16[256]{0:T(256)(128)(2,1)} %param.43) | copy-start | bytes 1540
  639.8 7.0 copy-start.4
  650.1 3.4 copy-start.7
  674.8 4.7 copy-start.24
  678.0 3.7 copy-start.9
  694.2 4.3 copy-start.72
  698.5 5.4 copy-start.12
  698.5 3.7 copy-start.10
  698.5 3.7 copy-start.36
  708.1 4.7 copy-start.1
  708.2 5.9 copy-start.5
  877.4 4.0 copy-start.41
  881.4 3.4 copy-start.46
  881.4 4.2 copy-start.45
  881.5 5.0 copy-start.38
  882.3 5.0 copy-start.37
  883.1 5.0 copy-start.49
  884.8 9.2 copy-start.31
  893.9 3.3 copy-start.40
  893.9 3.3 copy-start.48
  893.9 3.3 copy-start.67
  893.9 3.3 copy-start.69
  893.9 3.3 copy-start.71
  (42 other events, 90.2 us)

commit v5 on v4

--- a/solution.py
+++ b/solution.py
@@ -184,7 +184,8 @@
         return (block, block, place, place, w.over_core())
 
     here = at(z, y, x, c)
-    kept = w.local(own, here)
+    kept = w.local(own, here) if own is not None else None
+    own = here if own is None else own
     w.send(own, here, rise + z, rise + z, w.up(), z < n - 1)
     w.send(own, here, fall + z, fall + z, w.down(), z > 0)
     w.send(own, here, by_x + z, by_x + z, w.over_x())
@@ -237,7 +238,8 @@
         for ys in range(2):
             for xs in range(2):
                 w.landed(at(zs, ys, xs, 1 - c), by_core + zs * 4 + ys * 2 + xs)
-    kept.wait()
+    if kept is not None:
+        kept.wait()
 
 
 def gather_dp(w, own, at):
@@ -490,10 +492,14 @@
     for i, xs in enumerate((1 - x, x)):
         w.send(part.at[xs * 2 + 1 - c], first.at[i], core + i, core + i, w.over_core())
         kept.append(w.local(part.at[xs * 2 + c], own.at[i]))
+    yield
     kept[0].wait()
     w.landed(first.at[0], core)
     add_up(own.at[0], own.at[0], first.at[0])
     w.send(own.at[0], second, cross, cross, w.over_x())
+    yield
+    yield
+    yield
     kept[1].wait()
     w.landed(first.at[1], core + 1)
     w.landed(second, cross)
@@ -554,6 +560,9 @@
     return lambda ref: ref.at[pl.ds(first, rows), pl.ds(column, columns)]
 
 
+LAST = by_x_last
+
+
 def begin(levels, tensors):
     names = list(vars(tensors))
     count = 2 * levels
@@ -561,7 +570,11 @@
     unit = tensors.gate_weight.shape[1] // count
     deep = tensors.gate_weight.shape[0] * count
     rows = tensors.layer_input.shape[0]
-    packed = tensors.maps.shape
+    maps = list(tensors.maps)
+    share = maps[0].shape[0] // 4
+    packed = (share, sum(piece.shape[1] for piece in maps))
+    del tensors.maps
+    names = list(vars(tensors))
     low = tensors.gate_expand.shape[0] * count
     piece = deep // 4
     shapes = dict(
@@ -583,9 +596,19 @@
 
     def kernel(*refs):
         given = SimpleNamespace(**dict(zip(names, refs)))
-        got = SimpleNamespace(**dict(zip(shapes, refs[len(names) :])))
-        w = Wires(levels, *refs[len(names) + len(shapes) :])
+        pieces = refs[len(names) : len(names) + len(maps)]
+        refs = refs[len(names) + len(maps) :]
+        got = SimpleNamespace(**dict(zip(shapes, refs)))
+        w = Wires(levels, *refs[len(shapes) :])
+        block = rows_of(got.maps, w.dp * 4 + w.mp, share)
+        placed, column = [], 0
+        for ref in pieces:
+            target = block.at[:, pl.ds(column, ref.shape[1])]
+            placed.append(w.local(rows_of(ref, w.mp, share), target))
+            column += ref.shape[1]
         w.greet(far=True)
+        for copy in placed:
+            copy.wait()
 
         def expand_at(into):
             def at(z, y, x, c):
@@ -600,7 +623,7 @@
             gather_mp(w, given.layer_input, lambda x, c: got.layer_input.at[x * 2 + c]),
             gather_dp(w, given.query_weight, lambda z, y: rows_of(got.query_weight, z * 2 + y, deep // count)),
             gather_dp(w, given.output_weight, lambda z, y: columns_of(got.output_weight, z * 2 + y, deep // count)),
-            gather_all(w, given.maps, lambda z, y, x, c: rows_of(got.maps, flat(z, y, x, c), packed[0]), halves),
+            gather_all(w, None, lambda z, y, x, c: rows_of(got.maps, flat(z, y, x, c), packed[0]), LAST),
             gather_dp(w, given.expands, lambda z, y: rows_of(got.expands, z * 2 + y, low // count)),
             gather_dp(
                 w,
@@ -609,8 +632,8 @@
             ),
         ]
         for own, into in ((given.output_expand, got.output_expand), (given.down_expand, got.down_expand)):
-            steps.append(gather_all(w, columns_of(own, w.mp, piece), expand_at(into), halves))
-        steps.append(gather_all(w, given.output_grad, lambda z, y, x, c: got.output_grad.at[flat(z, y, x, c)], halves))
+            steps.append(gather_all(w, columns_of(own, w.mp, piece), expand_at(into), LAST))
+        steps.append(gather_all(w, given.output_grad, lambda z, y, x, c: got.output_grad.at[flat(z, y, x, c)], LAST))
         after = [
             exchange_dp(w, lambda dp: columns_of(given.gate_weight, dp, unit), lambda dp: rows_of(got.gate_weight, dp, deep // count)),
             exchange_dp(w, lambda dp: columns_of(given.up_weight, dp, unit), lambda dp: rows_of(got.up_weight, dp, deep // count)),
@@ -625,7 +648,7 @@
     given = call(
         kernel,
         0,
-        list(vars(tensors).values()),
+        list(vars(tensors).values()) + maps,
         [(shape, kind, False) for shape in shapes.values()],
         [],
         64 * levels + 48 * levels * 3,
@@ -659,6 +682,7 @@
 
 GELU = (2.0 / math.pi) ** 0.5
 TALL = 256
+GRIP = 4
 
 
 def feed(levels, rows, tokens, grads, gate_up, down):
@@ -802,29 +826,32 @@
 
             return carry
 
-        def gradients(k):
-            if k == levels:
-                held = []
-                for i in range(2):
-                    piece = pl.ds(i * half, half)
-                    held.append(w.local(pre_hbm.at[piece], arena.at[:, pl.ds(i * both, both)]))
-                    held.append(w.local(hidden_hbm.at[piece], gate_up_ref.at[:, pl.ds(i * unit, unit)]))
-                strip_load(tokens_ref, 0).start()
-                for copy in held:
-                    copy.wait()
-                lax.fori_loop(0, count // 2, pair_strip, 0)
-            if k == levels + 1:
-                lax.fori_loop(count // 2, count, pair_strip, 0)
-                pair_store(count - 1).wait()
-                keep(pair_pieces)
-            if k == levels + 2:
-                lax.fori_loop(0, count, single_strip, 0)
-                single_store(count - 1).wait()
+        made = []
+
+        def gradients():
+            while len(made) < levels:
+                yield
+            held = []
+            for i in range(2):
+                piece = pl.ds(i * half, half)
+                held.append(w.local(pre_hbm.at[piece], arena.at[:, pl.ds(i * both, both)]))
+                held.append(w.local(hidden_hbm.at[piece], gate_up_ref.at[:, pl.ds(i * unit, unit)]))
+            strip_load(tokens_ref, 0).start()
+            for copy in held:
+                copy.wait()
+            for i in range(0, count, GRIP):
+                lax.fori_loop(i, i + GRIP, pair_strip, 0)
+                if i + GRIP == count:
+                    pair_store(count - 1).wait()
+                    keep(pair_pieces)
+                yield
+            for i in range(0, count, count):
+                lax.fori_loop(i, i + count, single_strip, 0)
+                yield
+            single_store(count - 1).wait()
 
         def make(k):
             if k >= levels:
-                gradients(k)
-                yield
                 return
 
             def chunk(j, carry):
@@ -867,15 +894,18 @@
             for j in range(max(steps - 2, 0), steps):
                 for copy in store(k, j, j % 2):
                     copy.wait()
+            made.append(k)
             yield
 
         def idle(k):
-            yield
+            if k < levels:
+                yield
 
         turn(
             [
                 scatter_all(w, one_block(grad_part), grad_land, *one, grad_out, make=make),
                 scatter_all(w, one_block(branch_part), branch_land, *two, branch_out, make=idle),
+                gradients(),
             ]
         )
         for i in range(count - 1):
@@ -930,7 +960,7 @@
     def kernel(given, out, own, first, second, *sems):
         w = Wires(levels, *sems)
         w.greet(flat=True)
-        scatter_mp(w, given, own, first, second, out)
+        turn([scatter_mp(w, given, own, first, second, out)])
         w.finish()
 
     (out,) = call(
@@ -949,8 +979,9 @@
 BACK = 2
 
 
-def end(levels, rank, small, wides, query, output, units):
+def end(levels, rank, small, wides, query, output, rows, units):
     count = 2 * levels
+    here = rows.shape[1]
     deep, narrow = small.shape
     few, piece = deep // (4 * count), deep // 4
     wide = narrow + piece
@@ -970,14 +1001,15 @@
     each = len(scratch)
     scratch += [pltpu.VMEM((levels,) + query_shape, jnp.bfloat16)] * 4
     scratch += [pltpu.VMEM((levels,) + output_shape, jnp.bfloat16)] * 4
+    scratch += [pltpu.VMEM((2, here, deep), jnp.bfloat16)] * 2 + [pltpu.VMEM((here, deep), jnp.bfloat16)]
 
     def kernel(*refs):
-        small_ref, wide_one, wide_two, query_w, query_b, output_w, output_a = refs[:7]
-        given = SimpleNamespace(**dict(zip(names, refs[7:])))
-        refs = refs[7 + len(names) :]
+        small_ref, wide_one, wide_two, query_w, query_b, output_w, output_a, rows_ref = refs[:8]
+        given = SimpleNamespace(**dict(zip(names, refs[8:])))
+        refs = refs[8 + len(names) :]
         got = SimpleNamespace(**dict(zip(shapes, refs)))
-        small_out, query_out, output_out, shared, landing = refs[len(names) : len(names) + 5]
-        buffers = refs[len(names) + 5 :]
+        small_out, query_out, output_out, shared, rows_out, landing = refs[len(names) : len(names) + 6]
+        buffers = refs[len(names) + 6 :]
         w = Wires(levels, *buffers[-3:])
         w.greet(far=True)
 
@@ -1006,6 +1038,7 @@
             exchange_dp(w, lambda dp: rows_of(given.up_expand, dp, high), lambda dp: columns_of(got.up_expand, dp, unit)),
         ]
         steps = [
+            scatter_mp(w, rows_ref, *buffers[each + 8 : each + 11], rows_out),
             over_all(),
             scatter_dp(w, query_blocks, *buffers[each : each + 4], query_out),
             scatter_dp(w, output_blocks, *buffers[each + 4 : each + 8], output_out),
@@ -1015,18 +1048,19 @@
 
     outs = [(shape, jnp.bfloat16, False) for shape in shapes.values()]
     outs += [((few, wide), jnp.float32, True), (query_shape, jnp.float32, True), (output_shape, jnp.float32, True)]
-    outs += [((4, few, piece), jnp.float32, True), ((4 * levels, few, wide), jnp.bfloat16, False)]
+    outs += [((4, few, piece), jnp.float32, True), ((here, deep), jnp.float32, True)]
+    outs += [((4 * levels, few, wide), jnp.bfloat16, False)]
     made = call(
         kernel,
         5,
-        [small, *wides, *query, *output, *vars(units).values()],
+        [small, *wides, *query, *output, rows, *vars(units).values()],
         outs,
         scratch,
-        32 * levels,
-        10 * levels + 16,
+        32 * levels + 3,
+        10 * levels + 18,
         name="end",
     )
-    return SimpleNamespace(**dict(zip(shapes, made))), *made[3:7]
+    return SimpleNamespace(**dict(zip(shapes, made))), *made[3:8]
 
 
 def low(rows):
@@ -1090,11 +1124,7 @@
 
     gains = jnp.stack([attention_gain, feedforward_gain], axis=1)
     gains = jnp.pad(gains, ((0, 0), (0, 126)))
-    maps = jnp.concatenate(
-        [key_weight, value_weight, query_shrink, key_shrink, value_shrink, gate_shrink, up_shrink, gains],
-        axis=1,
-    )
-    maps = lax.dynamic_slice_in_dim(maps, mp * share, share, 0)
+    maps = [key_weight, value_weight, query_shrink, key_shrink, value_shrink, gate_shrink, up_shrink, gains]
     expands = jnp.concatenate([query_expand, key_expand, value_expand], axis=1)
     got = begin(
         levels,
@@ -1192,10 +1222,6 @@
     grad_query = rotary(grad_queries * head ** (-0.5), positions, -1.0).reshape(tokens, wide)
     grad_key = rotary(grad_keys[:, None, :], positions, -1.0)[:, 0, :]
     grad_lin = low(jnp.concatenate([grad_query, grad_key, grad_values], axis=1))
-    grad_rows = sum_mp(levels, low(against(grad_lin, inward)).reshape(4, rows, deep))
-    normed_own, scale_own = unit_rows(own_rows)
-    input_grad = grad_middle + norm_back(grad_rows, normed_own, scale_own)
-
     lin_normed = outer_sum(normed, grad_lin)
     lin_grad = low(lin_normed * gain_one)
     query_part, key_part, value_part = (
@@ -1225,15 +1251,18 @@
         ],
         axis=1,
     )
-    units, few, query_sum, output_sum, shared = end(
+    units, few, query_sum, output_sum, shared, grad_rows = end(
         levels,
         rank,
         small,
         (low(outer_sum(output_a, output_low)), low(outer_sum(down_a, down_grad_low))),
         (query_part, low(outer_sum(query_a, query_part))),
         (output_low, low(against(output_low, output_b))),
+        low(against(grad_lin, inward)).reshape(4, rows, deep),
         SimpleNamespace(down_weight=down_grad_low, gate_expand=gate_b_grad, up_expand=up_b_grad),
     )
+    normed_own, scale_own = unit_rows(own_rows)
+    input_grad = grad_middle + norm_back(grad_rows, normed_own, scale_own)
     key_own, value_own = few[:, :head], few[:, head : 2 * head]
     query_a_own, gate_a_own, up_a_own = (
         few[:, 2 * head + i * rank : 2 * head + (i + 1) * rank] for i in range(3)

time: 935 us -> 909 us (0.972)
  Pallas kernels: 764 us -> 745 us
    pallas_call x7 -> x6, Pallas kernels: 764 us -> 745 us  [call(): pl.pallas_call(kernel, out_shape=[jax.ShapeDtypeStruct(shape, kind) for s...]
where the time goes in v5:
time: 909 us; the launch traced here: 898 us
  Pallas kernels  745 us (82%)
  matrix products  78.4 us (9%)
  local copies, waits for them, and re-layouts  36.9 us (4%)
  other arithmetic  35.7 us (4%)
    pallas_call x6, Pallas kernels, call(): pl.pallas_call(kernel, out_shape=[jax.ShapeDtypeStruct(shape, kind) for s...  745 us
    dot_general x11, matrix products, matmul(): return jnp.dot(left, right, preferred_element_type=jnp.float32)  25.6 us
    dot_general x9, matrix products, outer_sum(): lax.dot_general(left, right, (((0,), (0,)), ((), ())), preferred_element_...  25.5 us

profile of v5, /device:TPU:0, one launch (start us, length us, event | category | flops | bytes accessed | tf_op | source)
XLA Modules:
  0.0 898.1 jit_solution(6149074377397852798)
XLA Ops:
  4.3 258.0 %begin.1 = (bf16[4,128,2048]{2,1,0:T(8,128)(2,1)}, bf16[2048,1920]{1,0:T(8,128)(2,1)}, bf16[256,2048]{1,0:T(8,128)(2,1)}, bf16[256,2048]{1,0:T(8,128)(2,1)}, bf1...) custom-call(bf16[128,2048]{1,0:T(8,128)(2,1)} %refs_0_.1, ...), custom_call_target="tpu_custom_call" | custom-call | tf_op jit(solution)/shard_map/begin/pallas_call | solution.py:515
  264.0 2.8 multiply_convert_fusion.1
  266.8 2.8 fusion.12
  269.7 2.4 fusion.13
  273.2 2.3 fusion.113
  284.8 2.0 fusion.118
  286.8 2.1 convolution_convert_fusion.7
  290.3 2.6 convolution_convert_fusion.2
  292.9 17.9 %sum_mp.1 = f32[128,2048]{1,0:T(8,128)} custom-call(bf16[4,128,2048]{2,1,0:T(8,128)(2,1)} %bitcast.122), custom_call_target="tpu_custom_call" | custom-call | tf_op jit(solution)/shard_map/sum_mp/pallas_call | solution.py:515
  313.3 80.1 %spread.1 = bf16[32,128,2048]{2,1,0:T(8,128)(2,1)} custom-call(bf16[128,2048]{1,0:T(8,128)(2,1)} %multiply_convert_fusion.6.own), custom_call_target="tpu_custom_call" | custom-call | tf_op jit(solution)/shard_map/spread/pallas_call | solution.py:515
  393.5 2.0 fusion.54
  395.6 2.1 fusion.51
  398.1 2.8 fusion.2.gate_up_hbm
  400.9 2.0 fusion.3.down_hbm
  402.9 238.8 %feed.1 = (f32[128,2048]{1,0:T(8,128)}, f32[128,2048]{1,0:T(8,128)}, bf16[2048,1024]{1,0:T(8,128)(2,1)}, bf16[512,2048]{1,0:T(8,128)(2,1)}, bf16[256,4096]{1,0:T...) custom-call(bf16[4096,2048]{1,0:T(8,128)(2,1)} %bitcast.117, ...), custom_call_target="tpu_custom_call" | custom-call | tf_op jit(solution)/shard_map/feed/pallas_call | solution.py:515
  641.7 4.2 fusion.33.refs_10_
  645.9 3.5 fusion.30.refs_9_
  651.6 19.4 %share_mp.1 = bf16[4,128,2048]{2,1,0:T(8,128)(2,1)} custom-call(bf16[128,2048]{1,0:T(8,128)(2,1)} %fusion.112.own), custom_call_target="tpu_custom_call" | custom-call | tf_op jit(solution)/shard_map/share_mp/pallas_call | solution.py:515
  671.0 3.6 convolution_convert_fusion.6
  679.3 2.1 copy.125
  684.6 2.3 fusion.36
  687.7 3.6 convolution_convert_fusion
  695.1 4.2 multiply_convert_fusion
  699.3 3.6 convolution_convert_fusion.9.refs_4_
  706.6 2.0 convolution_convert_fusion.11
  708.9 4.5 fusion.7
  723.2 2.3 fusion.114
  725.5 10.0 %concatenate.49.refs_0_ = bf16[2048,1408]{1,0:T(8,128)(2,1)} concatenate(bf16[2048,512]{1,0:T(8,128)(2,1)} %get-tuple-element.88, bf16[2048,256]{1,0:T(8,128)(2,1)} %convolution_convert_fusion.5, bf16[2048,256]{1,0:T(8,128)(2,1)} %fusion.14, bf16[2048,256]{1,0:T(8,128)(2,1)} %fusion.15, bf16[2048,64]{1,0:T(8,128)(2,1)} %fusion.44, bf16[2048,32]{1,0:T(8,128)(2,1)S(1)} %reshape_reshape.6, ...), dimensions={1} | concatenate | bytes 11534336 | tf_op jit(solution)/shard_map/concatenate | solution.py:1243
  735.5 3.3 fusion.16.refs_2_
  738.8 131.2 %end.1 = (bf16[4096,256]{1,0:T(8,128)(2,1)}, bf16[32,4096]{1,0:T(8,128)(2,1)}, bf16[32,4096]{1,0:T(8,128)(2,1)}, f32[64,1920]{1,0:T(8,128)}, f32[288,512]{1,0:T(...) custom-call(bf16[2048,1408]{1,0:T(8,128)(2,1)} %concatenate.49.refs_0_, ...), custom_call_target="tpu_custom_call" | custom-call | tf_op jit(solution)/shard_map/end/pallas_call | solution.py:515
  871.8 7.0 convert_multiply_fusion
  878.8 2.3 convert_element_type.259
  (220 shorter events, 66.6 us)
Async XLA Ops:
  0.7 400.2 %copy-start = (bf16[512,256]{1,0:T(8,128)(2,1)S(1)}, bf16[512,256]{1,0:T(8,128)(2,1)}, u32[]{:S(2)}) copy-start(bf16[512,256]{1,0:T(8,128)(2,1)} %param.51) | copy-start | bytes 786436
  264.0 5.6 copy-start.57
  266.8 6.4 copy-start.67
  269.6 3.6 copy-start.69
  278.1 3.6 copy-start.60
  280.1 3.4 copy-start.15
  280.1 3.4 copy-start.55
  280.1 3.4 copy-start.59
  280.2 6.5 copy-start.21
  280.2 6.5 copy-start.22
  292.9 17.9 %copy-start.3 = (bf16[128,2048]{1,0:T(8,128)(2,1)S(1)}, bf16[128,2048]{1,0:T(8,128)(2,1)}, u32[]{:S(2)}) copy-start(bf16[128,2048]{1,0:T(8,128)(2,1)} %refs_0_.1) | copy-start | bytes 1572868
  641.7 4.2 copy-start.4
  645.9 3.5 copy-start.6
  671.0 3.7 copy-start.19
  679.3 3.7 copy-start.61
  687.7 3.6 copy-start.23
  687.7 3.6 copy-start.65
  692.7 10.2 %copy-start.8 = (bf16[512,2048]{1,0:T(8,128)(2,1)}, bf16[512,2048]{1,0:T(8,128)(2,1)S(1)}, u32[]{:S(2)}) copy-start(bf16[512,2048]{1,0:T(8,128)(2,1)S(1)} %convolution_convert_fusion.1.refs_5_) | copy-start | bytes 6291460
  699.3 5.3 copy-start.13
  699.3 3.6 copy-start.39
  708.9 4.7 copy-start.1
  708.9 5.9 copy-start.5
  738.8 133.1 %copy-start.62 = (bf16[256]{0:T(256)(128)(2,1)S(1)}, bf16[256]{0:T(256)(128)(2,1)}, u32[]{:S(2)}) copy-start(bf16[256]{0:T(256)(128)(2,1)} %param.43) | copy-start | bytes 1540
  871.8 7.0 copy-start.20
  878.8 3.8 copy-start.54
  878.8 5.4 copy-start.12
  882.6 3.8 copy-start.47
  882.6 3.8 copy-start.48
  884.6 3.6 copy-start.41
  886.4 9.4 %copy-start.63 = (bf16[256]{0:T(256)(128)(2,1)S(1)}, bf16[256]{0:T(256)(128)(2,1)}, u32[]{:S(2)}) copy-start(bf16[256]{0:T(256)(128)(2,1)} %param.30) | copy-start | bytes 1540
  886.4 9.9 %copy-start.17 = (bf16[512,2048]{1,0:T(8,128)(2,1)S(1)}, bf16[512,2048]{1,0:T(8,128)(2,1)}, u32[]{:S(2)}) copy-start(bf16[512,2048]{1,0:T(8,128)(2,1)} %get-tuple-element.70.refs_8_) | copy-start | bytes 6291460
  886.4 9.9 %copy-start.34 = (bf16[256,2048]{1,0:T(8,128)(2,1)S(1)}, bf16[256,2048]{1,0:T(8,128)(2,1)}, u32[]{:S(2)}) copy-start(bf16[256,2048]{1,0:T(8,128)(2,1)} %get-tuple-element.66) | copy-start | bytes 3145732
  (41 other events, 90.1 us)
